TPU v7x, 32 devices: a whole 2x2x4 slice. The times are simulated.
32 devices in a mesh: section: 2 (over y), expert: 16 (over z, x, core).
Axes of the slice: x: 2, y: 2, z: 4, core: 2. Of those that a mesh axis runs over, the one named last changes fastest.
Arguments:
- tokens: bfloat16 [2048, 3584], P('expert'), may hold values from -6 to 6
- norm_gain: bfloat16 [3584], replicated, may hold values from 0.25 to 1.75
- router: bfloat16 [3584, 16], replicated, may hold values from -0.09375 to 0.09375
- w_gate: bfloat16 [16, 3584, 1024], P('expert', None, 'section'), may hold values from -0.09375 to 0.09375
- w_up: bfloat16 [16, 3584, 1024], P('expert', None, 'section'), may hold values from -0.09375 to 0.09375
- w_down: bfloat16 [16, 1024, 3584], P('expert', 'section'), may hold values from -0.1875 to 0.1875
- expert_ids: int32 [2048, 3], P('expert'), may hold values from 0 to 15, all different within a row; in each aligned block of 128 rows (0 to 127, 128 to 255, ...) at most 36 rows name the same one
Outputs:
- layer_out: bfloat16 [2048, 3584], P('expert', 'section')
Inputs may be any that keep to these rules, and one draw needn't show every extreme that they name: `expert_ids`: each row names 3 different experts. Within each aligned block of 128 rows (the rows of one index of the expert axis) no expert is named by more than 36 rows, and in every draw some expert is named by exactly 36 rows of some block.
All inputs are finite; a program needn't handle non-finite values.
Results may differ from a plain program's by a relative error of at most 0.013.
Values may be sent and summed in bfloat16 or wider, within the bound.
No kernel may reach another device: no remote copies, remote signals or barrier semaphores. Data moves between devices by JAX's collectives and lax.ppermute only.
A program may use at most 64 MiB of HBM per device.

v0:
```python
import jax
import jax.numpy as jnp
from jax import lax
from jax.sharding import PartitionSpec as P

EPSILON = 1e-06


def per_device(tokens, norm_gain, router, w_gate, w_up, w_down, expert_ids):
    tok_count, model_width = tokens.shape
    top_count = expert_ids.shape[1]
    expert_count = router.shape[1]
    cap_slots = tok_count * top_count * 3 // (2 * expert_count)
    pair_count = tok_count * top_count
    tokens_f = tokens.astype(jnp.float32)
    mean_sq = jnp.mean(tokens_f * tokens_f, axis=-1, keepdims=True)
    normed = (tokens_f * lax.rsqrt(mean_sq + EPSILON) * norm_gain.astype(jnp.float32)).astype(
        jnp.bfloat16
    )
    logits = jnp.dot(normed, router, preferred_element_type=jnp.float32)
    scores = jax.nn.sigmoid(logits)
    picked = jnp.take_along_axis(scores, expert_ids, axis=1)
    route_weight = 2.5 * picked / jnp.sum(picked, axis=1, keepdims=True)
    flat_ids = expert_ids.reshape(-1)
    onehot = (flat_ids[:, None] == jnp.arange(expert_count, dtype=jnp.int32)[None, :]).astype(
        jnp.float32
    )
    pair_rows = jnp.arange(pair_count, dtype=jnp.int32)
    earlier = (pair_rows[None, :] < pair_rows[:, None]).astype(jnp.float32)
    before = jnp.dot(
        earlier, onehot, precision=lax.Precision.HIGHEST, preferred_element_type=jnp.float32
    )
    slot_rank = jnp.sum(onehot * before, axis=1).astype(jnp.int32)
    slot_index = flat_ids * cap_slots + slot_rank
    copies = normed[pair_rows // top_count]
    buffer = (
        jnp.zeros((expert_count * cap_slots, model_width), jnp.bfloat16).at[slot_index].set(copies)
    )
    buffer = buffer.reshape(expert_count, cap_slots, model_width)
    received = lax.all_to_all(buffer, "expert", split_axis=0, concat_axis=0, tiled=True)
    gate_act = jnp.einsum("ecd,dh->ech", received, w_gate[0], preferred_element_type=jnp.float32)
    up_act = jnp.einsum("ecd,dh->ech", received, w_up[0], preferred_element_type=jnp.float32)
    hidden = (jax.nn.silu(gate_act) * up_act).astype(jnp.bfloat16)
    partial_value = jnp.einsum(
        "ech,hd->ecd", hidden, w_down[0], preferred_element_type=jnp.float32
    ).astype(jnp.bfloat16)
    summed = lax.psum_scatter(
        partial_value.astype(jnp.float32).astype(jnp.bfloat16),
        "section",
        scatter_dimension=2,
        tiled=True,
    ).astype(jnp.float32)
    returned = lax.all_to_all(
        summed.astype(jnp.bfloat16), "expert", split_axis=0, concat_axis=0, tiled=True
    ).astype(summed.dtype)
    ret_width = returned.shape[2]
    picked_rows = returned.reshape(expert_count * cap_slots, ret_width)[slot_index]
    picked_rows = picked_rows.reshape(tok_count, top_count, ret_width)
    mixed_sum = jnp.einsum("tkd,tk->td", picked_rows, route_weight)
    out_width = mixed_sum.shape[1]
    residual = lax.dynamic_slice_in_dim(tokens, lax.axis_index("section") * out_width, out_width, 1)
    return (residual.astype(jnp.float32) + mixed_sum).astype(jnp.bfloat16)


def solution(mesh):
    placed = (
        P("expert", None),
        P(),
        P(),
        P("expert", None, "section"),
        P("expert", None, "section"),
        P("expert", "section", None),
        P("expert", None),
    )
    return jax.shard_map(
        per_device, mesh=mesh, in_specs=placed, out_specs=P("expert", "section"), check_vma=False
    )
```

profile of v0, /device:TPU:11, one launch (start us, length us, event | category | flops | bytes accessed | tf_op | source)
XLA Modules:
  0.0 292.7 jit_solution(1083474531214730788)
XLA Ops:
  6.6 0.7 broadcast_multiply_fusion
  7.3 0.8 copy.16
  8.1 1.4 fusion.8
  9.5 0.7 convert_element_type.45
  10.8 0.2 fusion.17
  11.0 1.5 fusion.10
  12.5 15.1 %scatter_custom_fusion = bf16[576,3584]{1,0:T(8,128)(2,1)} fusion(s32[384]{0:T(512)S(1)} %fusion.25, bf16[128,3584]{1,0:T(8,128)(2,1)S(1)} %fusion.10, s32[1024]{0:T(1024)S(1)} %pad_clamp_fusion.1, bf16[]{:T(256)} %constant.18.clone.1), kind=kCustom, calls=%fused_computation.10 | custom fusion | bytes 4128770 | tf_op jit(solution)/shard_map/scatter | solution.py:37
  27.6 6.9 %reshape.105 = bf16[16,36,3584]{2,1,0:T(8,128)(2,1)} reshape(bf16[576,3584]{1,0:T(8,128)(2,1)} %scatter_custom_fusion) | data formatting | bytes 8257536 | tf_op jit(solution)/shard_map/reshape | solution.py:39
  34.5 107.5 %all_to_all.10 = bf16[16,36,3584]{2,1,0:T(8,128)(2,1)S(1)} all-to-all(bf16[16,36,3584]{2,1,0:T(8,128)(2,1)} %reshape.105), channel_id=1, replica_groups=mesh['section'=2,'expert'=16] {'expert'}, dimensions={0} | all-to-all | bytes 8257536 | tf_op jit(solution)/shard_map/all_to_all | solution.py:40
  142.0 2.1 copy-done.2
  144.1 2.6 fusion.3
  146.7 11.6 %convolution_convert_fusion = bf16[16,36,3584]{2,1,0:T(8,128)(2,1)} fusion(bf16[1,512,3584]{2,1,0:T(8,128)(2,1)} %param.12, bf16[16,36,3584]{2,1,0:T(8,128)(2,1)} %copy-done.2, bf16[1,3584,512]{2,1,0:T(8,128)(2,1)} %param.11, f32[16,36,512]{2,1,0:T(8,128)S(1)} %fusion.3), kind=kOutput, calls=%fused_computation.4 | convolution fusion | flops 4231692288 | bytes 16777216 | tf_op jit(solution)/shard_map/ech,hd->ecd/dot_general | solution.py:44
  158.4 58.6 %reduce-scatter.2.cloned.1.call-done = bf16[16,36,1792]{2,1,0:T(8,128)(2,1)} async-done(((bf16[16,36,3584]{2,1,0:T(8,128)(2,1)}), bf16[16,36,1792]{2,1,0:T(8,128)(2,1)}) %reduce-scatter.2.cloned.1.call-update) | async-done | bytes 2064400 | tf_op jit(solution)/shard_map/reduce_scatter | solution.py:47
  217.0 6.4 %all-to-all-start.1 = ((bf16[16,36,1792]{2,1,0:T(8,128)(2,1)}), bf16[16,36,1792]{2,1,0:T(8,128)(2,1)}, u32[]{:S(2)}, u32[]{:S(2)}) async-start(bf16[16,36,1792]{2,1,0:T(8,128)(2,1)} %reduce-scatter.2.cloned.1.call-done), calls=%async_computation.2 | async-start | bytes 4587520 | tf_op jit(solution)/shard_map/all_to_all | solution.py:53
  223.8 0.3 fusion.20
  224.1 2.9 gather_fusion.1
  227.3 0.8 copy.19
  228.1 0.6 pad_clamp_fusion
  228.7 46.5 %all-to-all-done.1 = bf16[16,36,1792]{2,1,0:T(8,128)(2,1)} async-done(((bf16[16,36,1792]{2,1,0:T(8,128)(2,1)}), bf16[16,36,1792]{2,1,0:T(8,128)(2,1)}, u32[]{:S(2)}, u32[]{:S(2)}) %all-to-all-start.1) | async-done | bytes 2064416 | tf_op jit(solution)/shard_map/all_to_all | solution.py:53
  275.2 2.5 reshape.106
  277.7 2.5 gather_fusion
  280.3 2.1 reshape.107
  282.4 2.6 fusion.29
  285.0 0.9 fusion.21
  (28 shorter events, 1.3 us)
Async XLA Ops:
  6.5 217.2 %copy-start = (bf16[3584,16]{0,1:T(8,128)(2,1)S(1)}, bf16[3584,16]{0,1:T(8,128)(2,1)}, u32[]{:S(2)}) copy-start(bf16[3584,16]{0,1:T(8,128)(2,1)} %param.9) | copy-start | bytes 344068
  6.5 210.5 %reduce-scatter.2.cloned.1.call-start = ((), (), s32[]{:S(2)}) async-start(), calls=%async_computation.3 | async-start | bytes 6881280 | tf_op jit(solution)/shard_map/reduce_scatter | solution.py:47
  34.5 109.6 %copy-start.5 = (bf16[1,3584,512]{2,1,0:T(8,128)(2,1)S(1)}, bf16[1,3584,512]{2,1,0:T(8,128)(2,1)}, u32[]{:S(2)}) copy-start(bf16[1,3584,512]{2,1,0:T(8,128)(2,1)} %param.10) | copy-start | bytes 11010052
  142.0 2.1 copy-start.2
  158.4 65.0 %copy-start.4 = (s32[128,3]{0,1:T(4,128)S(1)}, s32[128,3]{0,1:T(4,128)}, u32[]{:S(2)}) copy-start(s32[128,3]{0,1:T(4,128)} %param.13) | copy-start | bytes 4612
  217.0 58.1 %all-to-all-start.1 = ((bf16[16,36,1792]{2,1,0:T(8,128)(2,1)}), bf16[16,36,1792]{2,1,0:T(8,128)(2,1)}, u32[]{:S(2)}, u32[]{:S(2)}) async-start(bf16[16,36,1792]{2,1,0:T(8,128)(2,1)} %reduce-scatter.2.cloned.1.call-done), calls=%async_computation.2 | async-start | bytes 4587520 | tf_op jit(solution)/shard_map/all_to_all | solution.py:53
  280.2 2.1 copy-start.3
  280.2 4.7 %copy-start.1 = (bf16[128,3584]{1,0:T(8,128)(2,1)S(1)}, bf16[128,3584]{1,0:T(8,128)(2,1)}, u32[]{:S(2)}) copy-start(bf16[128,3584]{1,0:T(8,128)(2,1)} %param.7) | copy-start | bytes 2752516
Sparse Core Ops, SparseCore 0:
  158.5 58.4 reduce-scatter.1
where the time goes:
time: 293 us
  blocking collectives  107 us (37%)
  waiting for transfers between devices  105 us (36%)
  local copies, waits for them, and re-layouts  36.9 us (13%)
  matrix products  17.3 us (6%)
  between operations  13.5 us (5%)
  starting transfers between devices  6.39 us (2%)
  other arithmetic  5.89 us (2%)
    all_to_all x1, blocking collectives, per_device(): lax.all_to_all(buffer, 'expert', split_axis=0, concat_axis=0, tiled=True)  107 us
    reduce_scatter x1, waiting for transfers between devices, per_device(): lax.psum_scatter(partial_value.astype(jnp.float32).astype(jnp.bfloat16),...  58.6 us
    all_to_all x1, waiting for transfers between devices, per_device(): lax.all_to_all(summed.astype(jnp.bfloat16), 'expert', split_axis=0, conca...  46.5 us
    scatter x1, local copies, waits for them, and re-layouts, per_device(): jnp.zeros((expert_count * cap_slots, model_width), jnp.bfloat16)  15.1 us
    dot_general x1, matrix products, per_device(): jnp.einsum('ech,hd->ecd', hidden, w_down[0], preferred_element_type=jnp.f...  11.6 us
    reshape x1, local copies, waits for them, and re-layouts, per_device(): buffer = buffer.reshape(expert_count, cap_slots, model_width)  6.88 us
    all_to_all x1, starting transfers between devices, per_device(): lax.all_to_all(summed.astype(jnp.bfloat16), 'expert', split_axis=0, conca...  6.39 us
  transfers between devices with their start and end apart: 2, of which 2 were waited for; matrix products, arithmetic and copies ran while one was open for 2% of the time, Pallas kernels for 0%

commit v1 on v0

v1 whole, which is shorter than its diff:
```python
import jax
import jax.numpy as jnp
from jax import lax
from jax.sharding import PartitionSpec as P

EPSILON = 1e-06
F32, BF16 = jnp.float32, jnp.bfloat16


def per_device(sections, experts, tokens, norm_gain, router, w_gate, w_up, w_down, expert_ids):
    tok_count, model_width = tokens.shape
    top_count = expert_ids.shape[1]
    cap = tok_count * top_count * 3 // (2 * experts)
    width = model_width // sections
    half = experts // 2
    chips = experts // 4
    me = lax.axis_index("expert")
    section = lax.axis_index("section")

    def swap(value, mask):
        return lax.ppermute(value, "expert", [(i, i ^ mask) for i in range(experts)])

    tokens_f = tokens.astype(F32)
    mean_sq = jnp.mean(tokens_f * tokens_f, axis=-1, keepdims=True)
    normed = (tokens_f * lax.rsqrt(mean_sq + EPSILON) * norm_gain.astype(F32)).astype(BF16)
    mine = lax.dynamic_slice_in_dim(normed, section * width, width, 1)

    def table(ids):
        named = jnp.any(ids[:, :, None] == jnp.arange(experts, dtype=jnp.int32), axis=1)
        rows = lax.broadcasted_iota(jnp.int32, (tok_count, tok_count), 0)
        cols = lax.broadcasted_iota(jnp.int32, (tok_count, tok_count), 1)
        before = jnp.dot(
            (cols < rows).astype(BF16), named.astype(BF16), preferred_element_type=F32
        )
        return named, jnp.where(named, before, -1.0)

    ids_core = swap(expert_ids, 1)
    ids_far = swap(expert_ids, half)
    ids_far_core = swap(expert_ids, half + 1)
    named, table_own = table(expert_ids)
    logits = jnp.dot(normed, router, preferred_element_type=F32)
    scores = jnp.where(named, jax.nn.sigmoid(logits), 0.0)
    weight = 2.5 * scores / jnp.sum(scores, axis=1, keepdims=True)
    weight_core = swap(weight, 1)
    weight_far = swap(weight, half)
    weight_far_core = swap(weight, half + 1)

    near = (((me // 2) ^ jnp.arange(chips, dtype=jnp.int32)) * 2 + me % 2)[:, None]
    near = (near == jnp.arange(experts, dtype=jnp.int32)[None, :]).astype(F32)

    def columns(first, second):
        both = jnp.concatenate([first, second], axis=0)
        return lax.dot_general(
            near, both, (((1,), (1,)), ((), ())), precision=lax.Precision.HIGHEST,
            preferred_element_type=F32,
        )

    row = lax.broadcasted_iota(jnp.int32, (1, 2 * cap, 2 * tok_count), 1)
    col = lax.broadcasted_iota(jnp.int32, (1, 2 * cap, 2 * tok_count), 2)
    wanted = jnp.where(row // cap == col // tok_count, row % cap, -2).astype(F32)

    def choose(first, second):
        return columns(first, second)[:, None, :] == wanted

    def pick(chosen, toks):
        flat = chosen.astype(BF16).reshape(chips * 2 * cap, 2 * tok_count)
        return jnp.dot(flat, toks, preferred_element_type=F32).astype(BF16).reshape(
            chips, 2 * cap, toks.shape[1]
        )

    def spread(rows):
        return jnp.concatenate(
            [rows[:1]] + [swap(rows[q : q + 1], 2 * q) for q in range(1, chips)], axis=0
        )

    def feature_exchange(rows):
        rows = rows.reshape(chips * 2 * cap, rows.shape[2])
        if sections == 2:
            other = lax.ppermute(rows, "section", [(0, 1), (1, 0)])
            low = jnp.where(section == 0, rows, other)
            high = jnp.where(section == 0, other, rows)
            return jnp.concatenate([low, high], axis=1)
        return lax.all_gather(rows, "section", axis=1, tiled=True)

    def experts_of(full):
        gate_act = jnp.dot(full, w_gate[0], preferred_element_type=F32)
        up_act = jnp.dot(full, w_up[0], preferred_element_type=F32)
        hidden = (jax.nn.silu(gate_act) * up_act).astype(BF16)
        part = jnp.dot(hidden, w_down[0], preferred_element_type=F32).astype(BF16)
        if sections == 2:
            keep = lax.dynamic_slice_in_dim(part, section * width, width, 1)
            give = lax.dynamic_slice_in_dim(part, (1 - section) * width, width, 1)
            got = lax.ppermute(give, "section", [(0, 1), (1, 0)])
            done = (keep.astype(F32) + got.astype(F32)).astype(BF16)
        else:
            done = lax.psum_scatter(part, "section", scatter_dimension=1, tiled=True)
        return done.reshape(chips, 2 * cap, width)

    def mix(chosen, first, second, rows):
        factors = jnp.where(chosen, columns(first, second)[:, None, :], 0.0).astype(BF16)
        factors = factors.reshape(chips * 2 * cap, 2 * tok_count)
        both = lax.dot_general(
            factors, rows.reshape(chips * 2 * cap, width), (((0,), (0,)), ((), ())),
            preferred_element_type=F32,
        )
        got = swap(both[tok_count:].astype(BF16), 1)
        return both[:tok_count] + got.astype(F32)

    chosen_near = choose(table_own, table(ids_core)[1])
    toks_near = jnp.concatenate([mine, swap(mine, 1)], axis=0)
    full_near = feature_exchange(spread(pick(chosen_near, toks_near)))
    far = swap(mine, half)
    chosen_far = choose(table(ids_far)[1], table(ids_far_core)[1])
    toks_far = jnp.concatenate([far, swap(far, 1)], axis=0)
    full_far = feature_exchange(spread(pick(chosen_far, toks_far)))

    back_near = spread(experts_of(full_near))
    back_far = spread(experts_of(full_far))
    sum_far = swap(mix(chosen_far, weight_far, weight_far_core, back_far).astype(BF16), half)
    sum_near = mix(chosen_near, weight, weight_core, back_near)
    residual = lax.dynamic_slice_in_dim(tokens, section * width, width, 1)
    return (residual.astype(F32) + sum_near + sum_far.astype(F32)).astype(BF16)


def solution(mesh):
    placed = (
        P("expert", None),
        P(),
        P(),
        P("expert", None, "section"),
        P("expert", None, "section"),
        P("expert", "section", None),
        P("expert", None),
    )

    def body(*args):
        return per_device(mesh.shape["section"], mesh.shape["expert"], *args)

    return jax.shard_map(
        body, mesh=mesh, in_specs=placed, out_specs=P("expert", "section"), check_vma=False
    )
```

time: 293 us -> 177 us (0.60)
  the two profiles are of different devices: /device:TPU:11 before, /device:TPU:0 now
where the time goes in v1:
time: 177 us
  waiting for transfers between devices  108 us (61%)
  starting transfers between devices  30 us (17%)
  matrix products  21.1 us (12%)
  other arithmetic  11 us (6%)
  local copies, waits for them, and re-layouts  6.1 us (3%)
    ppermute x24, waiting for transfers between devices, swap(): lax.ppermute(value, 'expert', [(i, i ^ mask) for i in range(experts)])  71.4 us
    ppermute x24, starting transfers between devices, swap(): lax.ppermute(value, 'expert', [(i, i ^ mask) for i in range(experts)])  24.7 us
    ppermute x2, waiting for transfers between devices, experts_of(): got = lax.ppermute(give, 'section', [(0, 1), (1, 0)])  22.6 us
    ppermute x2, waiting for transfers between devices, feature_exchange(): other = lax.ppermute(rows, 'section', [(0, 1), (1, 0)])  14.4 us
    dot_general x2, matrix products, experts_of(): part = jnp.dot(hidden, w_down[0], preferred_element_type=F32).astype(BF16)  13.9 us
  transfers between devices with their start and end apart: 28, of which 18 were waited for; matrix products, arithmetic and copies ran while one was open for 20% of the time, Pallas kernels for 0%

profile of v1, /device:TPU:0, one launch (start us, length us, event | category | flops | bytes accessed | tf_op | source)
XLA Modules:
  0.0 176.9 jit_solution(3978944684580524599)
XLA Ops:
  0.5 3.7 %collective-permute-start.13 = (s32[128,3]{0,1:T(4,128)}, s32[128,3]{0,1:T(4,128)S(1)}, u32[]{:S(2)}, u32[]{:S(2)}) collective-permute-start(s32[128,3]{0,1:T(4,128)} %param.13), channel_id=1, source_target_pairs={{0,9},{1,8},{2,11},{3,10},{4,13},{5,12},{6,15},{7,14},{8,1},{9,0},... | collective-permute-start | bytes 4616 | tf_op jit(solution)/shard_map/ppermute | solution.py:21
  7.9 2.9 %collective-permute-start.16 = (bf16[128,1792]{1,0:T(8,128)(2,1)S(1)}, bf16[128,1792]{1,0:T(8,128)(2,1)S(1)}, u32[]{:S(2)}, u32[]{:S(2)}) collective-permute-start(bf16[128,1792]{1,0:T(8,128)(2,1)S(1)} %constant_dynamic-slice_fusion.2), channel_id=1, source_target_pairs={{0,8},{1,9},{2,10},{3,11},{4,12},{5,13},{6,14},{7,15},{8,0},{9,1},... | collective-permute-start | bytes 1376264 | tf_op jit(solution)/shard_map/ppermute | solution.py:21
  16.7 14.6 %collective-permute-done.16 = bf16[128,1792]{1,0:T(8,128)(2,1)S(1)} collective-permute-done((bf16[128,1792]{1,0:T(8,128)(2,1)S(1)}, bf16[128,1792]{1,0:T(8,128)(2,1)S(1)}, u32[]{:S(2)}, u32[]{:S(2)}) %collective-permute-start.16) | collective-permute-done | bytes 458784 | tf_op jit(solution)/shard_map/ppermute | solution.py:21
  32.5 4.4 %collective-permute-done.5 = bf16[1,72,1792]{2,1,0:T(8,128)(2,1)S(1)} collective-permute-done((bf16[1,72,1792]{2,1,0:T(8,128)(2,1)S(1)}, bf16[1,72,1792]{2,1,0:T(8,128)(2,1)S(1)}, u32[]{:S(2)}, u32[]{:S(2)}) %collective-permute-start.5) | collective-permute-done | bytes 258080 | tf_op jit(solution)/shard_map/ppermute | solution.py:21
  37.0 1.6 collective-permute-start.6
  41.3 2.0 %collective-permute-start.20 = (bf16[1,72,1792]{2,1,0:T(8,128)(2,1)S(1)}, bf16[1,72,1792]{2,1,0:T(8,128)(2,1)}, u32[]{:S(2)}, u32[]{:S(2)}) collective-permute-start(bf16[1,72,1792]{2,1,0:T(8,128)(2,1)S(1)} %get-tuple-element.14), channel_id=1, source_target_pairs={{0,6},{1,7},{2,4},{3,5},{4,2},{5,3},{6,0},{7,1},{8,14},{9,15},{10,... | collective-permute-start | bytes 774152 | tf_op jit(solution)/shard_map/ppermute | solution.py:21
  43.3 5.2 %collective-permute-done.18 = bf16[1,72,1792]{2,1,0:T(8,128)(2,1)S(1)} collective-permute-done((bf16[1,72,1792]{2,1,0:T(8,128)(2,1)}, bf16[1,72,1792]{2,1,0:T(8,128)(2,1)S(1)}, u32[]{:S(2)}, u32[]{:S(2)}) %collective-permute-start.18) | collective-permute-done | bytes 258080 | tf_op jit(solution)/shard_map/ppermute | solution.py:21
  48.5 2.0 %collective-permute-done.19 = bf16[1,72,1792]{2,1,0:T(8,128)(2,1)S(1)} collective-permute-done((bf16[1,72,1792]{2,1,0:T(8,128)(2,1)S(1)}, bf16[1,72,1792]{2,1,0:T(8,128)(2,1)S(1)}, u32[]{:S(2)}, u32[]{:S(2)}) %collective-permute-start.19) | collective-permute-done | bytes 258080 | tf_op jit(solution)/shard_map/ppermute | solution.py:21
  50.5 3.0 %collective-permute-done.20 = bf16[1,72,1792]{2,1,0:T(8,128)(2,1)} collective-permute-done((bf16[1,72,1792]{2,1,0:T(8,128)(2,1)S(1)}, bf16[1,72,1792]{2,1,0:T(8,128)(2,1)}, u32[]{:S(2)}, u32[]{:S(2)}) %collective-permute-start.20) | collective-permute-done | bytes 258080 | tf_op jit(solution)/shard_map/ppermute | solution.py:21
  55.4 7.6 %collective-permute-done.6 = bf16[288,1792]{1,0:T(8,128)(2,1)} collective-permute-done((bf16[288,1792]{1,0:T(8,128)(2,1)S(1)}, bf16[288,1792]{1,0:T(8,128)(2,1)}, u32[]{:S(2)}, u32[]{:S(2)}) %collective-permute-start.6) | collective-permute-done | bytes 1032224 | tf_op jit(solution)/shard_map/ppermute | solution.py:79
  66.9 7.6 %convolution_convert_fusion.1 = bf16[288,3584]{1,0:T(8,128)(2,1)} fusion(bf16[1,512,3584]{2,1,0:T(8,128)(2,1)} %param.12, f32[288,512]{1,0:T(8,128)S(1)} %fusion.4, bf16[1,3584,512]{2,1,0:T(8,128)(2,1)} %param.10, bf16[288,1792]{1,0:T(8,128)(2,1)} %copy-done.6, bf16[288,1792]{1,0:T(8,128)(2,1)} %copy-done.5), kind=kOutput, calls=%fused_computation.1 | convolution fusion | flops 2119974912 | bytes 12058624 | tf_op jit(solution)/shard_map/dot_general | solution.py:89
  74.4 2.2 %constant_dynamic-slice_fusion.1 = bf16[288,1792]{1,0:T(8,128)(2,1)} fusion(bf16[288,3584]{1,0:T(8,128)(2,1)} %convolution_convert_fusion.1, s32[]{:T(128)S(6)} %select_n.124), kind=kLoop, calls=%fused_computation.132 | loop fusion | bytes 2064388 | tf_op jit(solution)/shard_map/dynamic_slice | solution.py:92
  78.2 6.9 %collective-permute-done.21 = bf16[288,1792]{1,0:T(8,128)(2,1)} collective-permute-done((bf16[288,1792]{1,0:T(8,128)(2,1)S(1)}, bf16[288,1792]{1,0:T(8,128)(2,1)}, u32[]{:S(2)}, u32[]{:S(2)}) %collective-permute-start.21) | collective-permute-done | bytes 1032224 | tf_op jit(solution)/shard_map/ppermute | solution.py:79
  87.8 2.1 %fusion.2 = f32[288,512]{1,0:T(8,128)} fusion(bf16[1,3584,512]{2,1,0:T(8,128)(2,1)S(1)} %copy-done.11, bf16[288,1792]{1,0:T(8,128)(2,1)S(1)} %get-tuple-element.6, bf16[288,1792]{1,0:T(8,128)(2,1)S(1)} %get-tuple-element.5), kind=kOutput, calls=%fused_computation.4 | convolution fusion | flops 1061093376 | bytes 6324224 | tf_op jit(solution)/shard_map/dot_general | solution.py:87
  89.8 6.4 %convolution_convert_fusion = bf16[288,3584]{1,0:T(8,128)(2,1)S(1)} fusion(bf16[1,512,3584]{2,1,0:T(8,128)(2,1)} %param.12, f32[288,512]{1,0:T(8,128)} %fusion.2, bf16[1,3584,512]{2,1,0:T(8,128)(2,1)} %param.10, bf16[288,1792]{1,0:T(8,128)(2,1)} %copy-done.4, bf16[288,1792]{1,0:T(8,128)(2,1)} %copy-done.3), kind=kOutput, calls=%fused_computation | convolution fusion | flops 2119974912 | bytes 12058624 | tf_op jit(solution)/shard_map/dot_general | solution.py:89
  96.3 1.6 collective-permute-start.22
  98.8 2.6 %collective-permute-start.1 = (f32[128,16]{0,1:T(8,128)S(1)}, f32[128,16]{0,1:T(8,128)S(1)}, u32[]{:S(2)}, u32[]{:S(2)}) collective-permute-start(f32[128,16]{0,1:T(8,128)S(1)} %multiply_divide_fusion), channel_id=1, source_target_pairs={{0,1},{1,0},{2,3},{3,2},{4,5},{5,4},{6,7},{7,6},{8,9},{9,8},{10,11... | collective-permute-start | bytes 24584 | tf_op jit(solution)/shard_map/ppermute | solution.py:21
  103.1 4.1 %collective-permute-done.7 = bf16[288,1792]{1,0:T(8,128)(2,1)} collective-permute-done((bf16[288,1792]{1,0:T(8,128)(2,1)}, bf16[288,1792]{1,0:T(8,128)(2,1)}, u32[]{:S(2)}, u32[]{:S(2)}) %collective-permute-start.7) | collective-permute-done | bytes 1032224 | tf_op jit(solution)/shard_map/ppermute | solution.py:93
  108.7 18.5 %collective-permute-done.22 = bf16[288,1792]{1,0:T(8,128)(2,1)S(1)} collective-permute-done((bf16[288,1792]{1,0:T(8,128)(2,1)S(1)}, bf16[288,1792]{1,0:T(8,128)(2,1)S(1)}, u32[]{:S(2)}, u32[]{:S(2)}) %collective-permute-start.22) | collective-permute-done | bytes 1032224 | tf_op jit(solution)/shard_map/ppermute | solution.py:93
  129.1 2.0 %collective-permute-start.25 = (bf16[1,72,1792]{2,1,0:T(8,128)(2,1)S(1)}, bf16[1,72,1792]{2,1,0:T(8,128)(2,1)S(1)}, u32[]{:S(2)}, u32[]{:S(2)}) collective-permute-start(bf16[1,72,1792]{2,1,0:T(8,128)(2,1)S(1)} %get-tuple-element.10), channel_id=1, source_target_pairs={{0,6},{1,7},{2,4},{3,5},{4,2},{5,3},{6,0},{7,1},{8,14},{9,15},{10,... | collective-permute-start | bytes 774152 | tf_op jit(solution)/shard_map/ppermute | solution.py:21
  132.1 11.1 %collective-permute-done.23 = bf16[1,72,1792]{2,1,0:T(8,128)(2,1)S(1)} collective-permute-done((bf16[1,72,1792]{2,1,0:T(8,128)(2,1)S(1)}, bf16[1,72,1792]{2,1,0:T(8,128)(2,1)S(1)}, u32[]{:S(2)}, u32[]{:S(2)}) %collective-permute-start.23) | collective-permute-done | bytes 258080 | tf_op jit(solution)/shard_map/ppermute | solution.py:21
  145.8 3.1 %collective-permute-done.10 = bf16[1,72,1792]{2,1,0:T(8,128)(2,1)S(1)} collective-permute-done((bf16[1,72,1792]{2,1,0:T(8,128)(2,1)S(1)}, bf16[1,72,1792]{2,1,0:T(8,128)(2,1)S(1)}, u32[]{:S(2)}, u32[]{:S(2)}) %collective-permute-start.10) | collective-permute-done | bytes 258080 | tf_op jit(solution)/shard_map/ppermute | solution.py:21
  148.8 2.0 %collective-permute-done.8 = bf16[1,72,1792]{2,1,0:T(8,128)(2,1)S(1)} collective-permute-done((bf16[1,72,1792]{2,1,0:T(8,128)(2,1)S(1)}, bf16[1,72,1792]{2,1,0:T(8,128)(2,1)S(1)}, u32[]{:S(2)}, u32[]{:S(2)}) %collective-permute-start.8) | collective-permute-done | bytes 258080 | tf_op jit(solution)/shard_map/ppermute | solution.py:21
  154.2 21.7 %collective-permute-done.27 = bf16[128,1792]{1,0:T(8,128)(2,1)S(1)} collective-permute-done((bf16[128,1792]{1,0:T(8,128)(2,1)S(1)}, bf16[128,1792]{1,0:T(8,128)(2,1)S(1)}, u32[]{:S(2)}, u32[]{:S(2)}) %collective-permute-start.27) | collective-permute-done | bytes 458784 | tf_op jit(solution)/shard_map/ppermute | solution.py:21
  (107 shorter events, 38.0 us)
Async XLA Ops:
  0.0 11.2 %collective-permute-start = (s32[128,3]{0,1:T(4,128)}, s32[128,3]{0,1:T(4,128)S(1)}, u32[]{:S(2)}, u32[]{:S(2)}) collective-permute-start(s32[128,3]{0,1:T(4,128)} %param.13), channel_id=1, source_target_pairs={{0,1},{1,0},{2,3},{3,2},{4,5},{5,4},{6,7},{7,6},{8,9},{9,8},{10,11... | collective-permute-start | bytes 4616 | tf_op jit(solution)/shard_map/ppermute | solution.py:21
  0.5 10.9 %collective-permute-start.13 = (s32[128,3]{0,1:T(4,128)}, s32[128,3]{0,1:T(4,128)S(1)}, u32[]{:S(2)}, u32[]{:S(2)}) collective-permute-start(s32[128,3]{0,1:T(4,128)} %param.13), channel_id=1, source_target_pairs={{0,9},{1,8},{2,11},{3,10},{4,13},{5,12},{6,15},{7,14},{8,1},{9,0},... | collective-permute-start | bytes 4616 | tf_op jit(solution)/shard_map/ppermute | solution.py:21
  4.2 7.4 %collective-permute-start.12 = (s32[128,3]{0,1:T(4,128)}, s32[128,3]{0,1:T(4,128)S(1)}, u32[]{:S(2)}, u32[]{:S(2)}) collective-permute-start(s32[128,3]{0,1:T(4,128)} %param.13), channel_id=1, source_target_pairs={{0,8},{1,9},{2,10},{3,11},{4,12},{5,13},{6,14},{7,15},{8,0},{9,1},... | collective-permute-start | bytes 4616 | tf_op jit(solution)/shard_map/ppermute | solution.py:21
  7.9 23.4 %collective-permute-start.16 = (bf16[128,1792]{1,0:T(8,128)(2,1)S(1)}, bf16[128,1792]{1,0:T(8,128)(2,1)S(1)}, u32[]{:S(2)}, u32[]{:S(2)}) collective-permute-start(bf16[128,1792]{1,0:T(8,128)(2,1)S(1)} %constant_dynamic-slice_fusion.2), channel_id=1, source_target_pairs={{0,8},{1,9},{2,10},{3,11},{4,12},{5,13},{6,14},{7,15},{8,0},{9,1},... | collective-permute-start | bytes 1376264 | tf_op jit(solution)/shard_map/ppermute | solution.py:21
  13.1 18.2 %collective-permute-start.3 = (bf16[1,72,1792]{2,1,0:T(8,128)(2,1)S(1)}, bf16[1,72,1792]{2,1,0:T(8,128)(2,1)S(1)}, u32[]{:S(2)}, u32[]{:S(2)}) collective-permute-start(bf16[1,72,1792]{2,1,0:T(8,128)(2,1)S(1)} %get-tuple-element.24), channel_id=1, source_target_pairs={{0,2},{1,3},{2,0},{3,1},{4,6},{5,7},{6,4},{7,5},{8,10},{9,11},{10,... | collective-permute-start | bytes 774152 | tf_op jit(solution)/shard_map/ppermute | solution.py:21
  14.7 17.8 %collective-permute-start.4 = (bf16[1,72,1792]{2,1,0:T(8,128)(2,1)S(1)}, bf16[1,72,1792]{2,1,0:T(8,128)(2,1)S(1)}, u32[]{:S(2)}, u32[]{:S(2)}) collective-permute-start(bf16[1,72,1792]{2,1,0:T(8,128)(2,1)S(1)} %get-tuple-element.23), channel_id=1, source_target_pairs={{0,4},{1,5},{2,6},{3,7},{4,0},{5,1},{6,2},{7,3},{8,12},{9,13},{10,... | collective-permute-start | bytes 774152 | tf_op jit(solution)/shard_map/ppermute | solution.py:21
  16.3 20.6 %collective-permute-start.5 = (bf16[1,72,1792]{2,1,0:T(8,128)(2,1)S(1)}, bf16[1,72,1792]{2,1,0:T(8,128)(2,1)S(1)}, u32[]{:S(2)}, u32[]{:S(2)}) collective-permute-start(bf16[1,72,1792]{2,1,0:T(8,128)(2,1)S(1)} %get-tuple-element.22), channel_id=1, source_target_pairs={{0,6},{1,7},{2,4},{3,5},{4,2},{5,3},{6,0},{7,1},{8,14},{9,15},{10,... | collective-permute-start | bytes 774152 | tf_op jit(solution)/shard_map/ppermute | solution.py:21
  31.3 7.3 %collective-permute-start.17 = (bf16[128,1792]{1,0:T(8,128)(2,1)S(1)}, bf16[128,1792]{1,0:T(8,128)(2,1)S(1)}, u32[]{:S(2)}, u32[]{:S(2)}) collective-permute-start(bf16[128,1792]{1,0:T(8,128)(2,1)S(1)} %collective-permute-done.16), channel_id=1, source_target_pairs={{0,1},{1,0},{2,3},{3,2},{4,5},{5,4},{6,7},{7,6},{8,9},{9,8},{10,11... | collective-permute-start | bytes 1376264 | tf_op jit(solution)/shard_map/ppermute | solution.py:21
  37.0 25.9 %collective-permute-start.6 = (bf16[288,1792]{1,0:T(8,128)(2,1)S(1)}, bf16[288,1792]{1,0:T(8,128)(2,1)}, u32[]{:S(2)}, u32[]{:S(2)}) collective-permute-start(bf16[288,1792]{1,0:T(8,128)(2,1)S(1)} %bitcast.75), channel_id=1, source_target_pairs={{0,16},{16,0},{1,17},{17,1},{2,18},{18,2},{3,19},{19,3},{4,20},{20... | collective-permute-start | bytes 3096584 | tf_op jit(solution)/shard_map/ppermute | solution.py:79
  39.8 8.7 %collective-permute-start.18 = (bf16[1,72,1792]{2,1,0:T(8,128)(2,1)}, bf16[1,72,1792]{2,1,0:T(8,128)(2,1)S(1)}, u32[]{:S(2)}, u32[]{:S(2)}) collective-permute-start(bf16[1,72,1792]{2,1,0:T(8,128)(2,1)} %get-tuple-element.16), channel_id=1, source_target_pairs={{0,2},{1,3},{2,0},{3,1},{4,6},{5,7},{6,4},{7,5},{8,10},{9,11},{10,... | collective-permute-start | bytes 774152 | tf_op jit(solution)/shard_map/ppermute | solution.py:21
  41.3 9.2 %collective-permute-start.19 = (bf16[1,72,1792]{2,1,0:T(8,128)(2,1)S(1)}, bf16[1,72,1792]{2,1,0:T(8,128)(2,1)S(1)}, u32[]{:S(2)}, u32[]{:S(2)}) collective-permute-start(bf16[1,72,1792]{2,1,0:T(8,128)(2,1)S(1)} %get-tuple-element.15), channel_id=1, source_target_pairs={{0,4},{1,5},{2,6},{3,7},{4,0},{5,1},{6,2},{7,3},{8,12},{9,13},{10,... | collective-permute-start | bytes 774152 | tf_op jit(solution)/shard_map/ppermute | solution.py:21
  41.3 12.1 %collective-permute-start.20 = (bf16[1,72,1792]{2,1,0:T(8,128)(2,1)S(1)}, bf16[1,72,1792]{2,1,0:T(8,128)(2,1)}, u32[]{:S(2)}, u32[]{:S(2)}) collective-permute-start(bf16[1,72,1792]{2,1,0:T(8,128)(2,1)S(1)} %get-tuple-element.14), channel_id=1, source_target_pairs={{0,6},{1,7},{2,4},{3,5},{4,2},{5,3},{6,0},{7,1},{8,14},{9,15},{10,... | collective-permute-start | bytes 774152 | tf_op jit(solution)/shard_map/ppermute | solution.py:21
  54.8 30.2 %collective-permute-start.21 = (bf16[288,1792]{1,0:T(8,128)(2,1)S(1)}, bf16[288,1792]{1,0:T(8,128)(2,1)}, u32[]{:S(2)}, u32[]{:S(2)}) collective-permute-start(bf16[288,1792]{1,0:T(8,128)(2,1)S(1)} %bitcast.76), channel_id=1, source_target_pairs={{0,16},{16,0},{1,17},{17,1},{2,18},{18,2},{3,19},{19,3},{4,20},{20... | collective-permute-start | bytes 3096584 | tf_op jit(solution)/shard_map/ppermute | solution.py:79
  76.7 30.5 %collective-permute-start.7 = (bf16[288,1792]{1,0:T(8,128)(2,1)}, bf16[288,1792]{1,0:T(8,128)(2,1)}, u32[]{:S(2)}, u32[]{:S(2)}) collective-permute-start(bf16[288,1792]{1,0:T(8,128)(2,1)} %constant_dynamic-slice_fusion.1), channel_id=1, source_target_pairs={{0,16},{16,0},{1,17},{17,1},{2,18},{18,2},{3,19},{19,3},{4,20},{20... | collective-permute-start | bytes 3096584 | tf_op jit(solution)/shard_map/ppermute | solution.py:93
  96.3 30.9 %collective-permute-start.22 = (bf16[288,1792]{1,0:T(8,128)(2,1)S(1)}, bf16[288,1792]{1,0:T(8,128)(2,1)S(1)}, u32[]{:S(2)}, u32[]{:S(2)}) collective-permute-start(bf16[288,1792]{1,0:T(8,128)(2,1)S(1)} %constant_dynamic-slice_fusion), channel_id=1, source_target_pairs={{0,16},{16,0},{1,17},{17,1},{2,18},{18,2},{3,19},{19,3},{4,20},{20... | collective-permute-start | bytes 3096584 | tf_op jit(solution)/shard_map/ppermute | solution.py:93
  98.8 46.8 %collective-permute-start.1 = (f32[128,16]{0,1:T(8,128)S(1)}, f32[128,16]{0,1:T(8,128)S(1)}, u32[]{:S(2)}, u32[]{:S(2)}) collective-permute-start(f32[128,16]{0,1:T(8,128)S(1)} %multiply_divide_fusion), channel_id=1, source_target_pairs={{0,1},{1,0},{2,3},{3,2},{4,5},{5,4},{6,7},{7,6},{8,9},{9,8},{10,11... | collective-permute-start | bytes 24584 | tf_op jit(solution)/shard_map/ppermute | solution.py:21
  127.5 15.7 %collective-permute-start.23 = (bf16[1,72,1792]{2,1,0:T(8,128)(2,1)S(1)}, bf16[1,72,1792]{2,1,0:T(8,128)(2,1)S(1)}, u32[]{:S(2)}, u32[]{:S(2)}) collective-permute-start(bf16[1,72,1792]{2,1,0:T(8,128)(2,1)S(1)} %get-tuple-element.12), channel_id=1, source_target_pairs={{0,2},{1,3},{2,0},{3,1},{4,6},{5,7},{6,4},{7,5},{8,10},{9,11},{10,... | collective-permute-start | bytes 774152 | tf_op jit(solution)/shard_map/ppermute | solution.py:21
  129.1 15.7 %collective-permute-start.24 = (bf16[1,72,1792]{2,1,0:T(8,128)(2,1)S(1)}, bf16[1,72,1792]{2,1,0:T(8,128)(2,1)S(1)}, u32[]{:S(2)}, u32[]{:S(2)}) collective-permute-start(bf16[1,72,1792]{2,1,0:T(8,128)(2,1)S(1)} %get-tuple-element.11), channel_id=1, source_target_pairs={{0,4},{1,5},{2,6},{3,7},{4,0},{5,1},{6,2},{7,3},{8,12},{9,13},{10,... | collective-permute-start | bytes 774152 | tf_op jit(solution)/shard_map/ppermute | solution.py:21
  129.1 15.7 %collective-permute-start.25 = (bf16[1,72,1792]{2,1,0:T(8,128)(2,1)S(1)}, bf16[1,72,1792]{2,1,0:T(8,128)(2,1)S(1)}, u32[]{:S(2)}, u32[]{:S(2)}) collective-permute-start(bf16[1,72,1792]{2,1,0:T(8,128)(2,1)S(1)} %get-tuple-element.10), channel_id=1, source_target_pairs={{0,6},{1,7},{2,4},{3,5},{4,2},{5,3},{6,0},{7,1},{8,14},{9,15},{10,... | collective-permute-start | bytes 774152 | tf_op jit(solution)/shard_map/ppermute | solution.py:21
  131.1 17.7 %collective-permute-start.10 = (bf16[1,72,1792]{2,1,0:T(8,128)(2,1)S(1)}, bf16[1,72,1792]{2,1,0:T(8,128)(2,1)S(1)}, u32[]{:S(2)}, u32[]{:S(2)}) collective-permute-start(bf16[1,72,1792]{2,1,0:T(8,128)(2,1)S(1)} %get-tuple-element.18), channel_id=1, source_target_pairs={{0,6},{1,7},{2,4},{3,5},{4,2},{5,3},{6,0},{7,1},{8,14},{9,15},{10,... | collective-permute-start | bytes 774152 | tf_op jit(solution)/shard_map/ppermute | solution.py:21
  143.2 7.6 %collective-permute-start.8 = (bf16[1,72,1792]{2,1,0:T(8,128)(2,1)S(1)}, bf16[1,72,1792]{2,1,0:T(8,128)(2,1)S(1)}, u32[]{:S(2)}, u32[]{:S(2)}) collective-permute-start(bf16[1,72,1792]{2,1,0:T(8,128)(2,1)S(1)} %get-tuple-element.20), channel_id=1, source_target_pairs={{0,2},{1,3},{2,0},{3,1},{4,6},{5,7},{6,4},{7,5},{8,10},{9,11},{10,... | collective-permute-start | bytes 774152 | tf_op jit(solution)/shard_map/ppermute | solution.py:21
  144.7 6.8 %collective-permute-start.9 = (bf16[1,72,1792]{2,1,0:T(8,128)(2,1)S(1)}, bf16[1,72,1792]{2,1,0:T(8,128)(2,1)S(1)}, u32[]{:S(2)}, u32[]{:S(2)}) collective-permute-start(bf16[1,72,1792]{2,1,0:T(8,128)(2,1)S(1)} %get-tuple-element.19), channel_id=1, source_target_pairs={{0,4},{1,5},{2,6},{3,7},{4,0},{5,1},{6,2},{7,3},{8,12},{9,13},{10,... | collective-permute-start | bytes 774152 | tf_op jit(solution)/shard_map/ppermute | solution.py:21
  145.5 6.9 %collective-permute-start.26 = (bf16[128,1792]{1,0:T(8,128)(2,1)S(1)}, bf16[128,1792]{1,0:T(8,128)(2,1)S(1)}, u32[]{:S(2)}, u32[]{:S(2)}) collective-permute-start(bf16[128,1792]{1,0:T(8,128)(2,1)S(1)} %slice.194), channel_id=1, source_target_pairs={{0,1},{1,0},{2,3},{3,2},{4,5},{5,4},{6,7},{7,6},{8,9},{9,8},{10,11... | collective-permute-start | bytes 1376264 | tf_op jit(solution)/shard_map/ppermute | solution.py:21
  152.5 23.4 %collective-permute-start.27 = (bf16[128,1792]{1,0:T(8,128)(2,1)S(1)}, bf16[128,1792]{1,0:T(8,128)(2,1)S(1)}, u32[]{:S(2)}, u32[]{:S(2)}) collective-permute-start(bf16[128,1792]{1,0:T(8,128)(2,1)S(1)} %fusion.31), channel_id=1, source_target_pairs={{0,8},{1,9},{2,10},{3,11},{4,12},{5,13},{6,14},{7,15},{8,0},{9,1},... | collective-permute-start | bytes 1376264 | tf_op jit(solution)/shard_map/ppermute | solution.py:21
  (16 other events, 190.2 us)

commit v2 on v1

--- a/solution.py
+++ b/solution.py
@@ -1,13 +1,17 @@
+import functools
+
 import jax
 import jax.numpy as jnp
 from jax import lax
+from jax.experimental import pallas as pl
+from jax.experimental.pallas import tpu as pltpu
 from jax.sharding import PartitionSpec as P
 
 EPSILON = 1e-06
 F32, BF16 = jnp.float32, jnp.bfloat16
 
 
-def per_device(sections, experts, tokens, norm_gain, router, w_gate, w_up, w_down, expert_ids):
+def any_sections(sections, experts, tokens, norm_gain, router, w_gate, w_up, w_down, expert_ids):
     tok_count, model_width = tokens.shape
     top_count = expert_ids.shape[1]
     cap = tok_count * top_count * 3 // (2 * experts)
@@ -122,6 +126,382 @@
     return (residual.astype(F32) + sum_near + sum_far.astype(F32)).astype(BF16)
 
 
+def prepare_body(experts, place, *refs):
+    out, first, second = refs[4:7]
+    tokens, gain, router, ids, sems = refs[7:]
+    copies = [
+        pltpu.make_async_copy(source, target, sems.at[i])
+        for i, (source, target) in enumerate(zip(refs[:4], refs[7:11]))
+    ]
+    for copy in copies:
+        copy.start()
+    for copy in copies:
+        copy.wait()
+    tok_count, model_width = tokens.shape
+    width = model_width // 2
+    tokens_f = tokens[...].astype(F32)
+    mean_sq = jnp.mean(tokens_f * tokens_f, axis=-1, keepdims=True)
+    gain_f = gain[...].reshape(1, model_width).astype(F32)
+    normed = (tokens_f * lax.rsqrt(mean_sq + EPSILON) * gain_f).astype(BF16)
+    by_feature = (((1,), (1,)), ((), ()))
+    logits = lax.dot_general(router[...], normed, by_feature, preferred_element_type=F32)
+    expert = lax.broadcasted_iota(jnp.int32, (experts, tok_count), 0)
+    named = ids[0:1, :] == expert
+    for k in range(1, ids.shape[0]):
+        named = named | (ids[k : k + 1, :] == expert)
+    rows = lax.broadcasted_iota(jnp.int32, (tok_count, tok_count), 0)
+    cols = lax.broadcasted_iota(jnp.int32, (tok_count, tok_count), 1)
+    before = jnp.dot(
+        named.astype(F32).astype(BF16),
+        (rows < cols).astype(F32).astype(BF16),
+        preferred_element_type=F32,
+    )
+    slot = jnp.where(named, before, -1.0)
+    scores = jnp.where(named, 1.0 / (1.0 + jnp.exp(-logits)), 0.0)
+    weight = 2.5 * scores / jnp.sum(scores, axis=0, keepdims=True)
+    meta = jnp.concatenate(
+        [slot, weight, jnp.zeros((128 - 2 * experts, tok_count), F32)], axis=0
+    ).astype(BF16)
+    meta = lax.dot_general(
+        (rows == cols).astype(F32).astype(BF16), meta, by_feature, preferred_element_type=F32
+    )
+    meta = meta.astype(BF16)
+    swapped = place[0] == 1
+    low, high = normed[:, :width], normed[:, width:]
+    mine = jnp.where(swapped, high, low)
+    out[:, :width] = mine
+    out[:, width:model_width] = jnp.where(swapped, low, high)
+    out[:, model_width:] = meta
+    first[:, : width // 2] = mine[:, : width // 2]
+    first[:, width // 2 :] = meta
+    second[...] = mine[:, width // 2 :]
+
+
+def prepare(experts, place, tokens, norm_gain, router, expert_ids):
+    tok_count, model_width = tokens.shape
+    arrays = (tokens, norm_gain, router.T, expert_ids.T)
+    return pl.pallas_call(
+        functools.partial(prepare_body, experts),
+        out_shape=[
+            jax.ShapeDtypeStruct((tok_count, columns), BF16)
+            for columns in (model_width + 128, model_width // 4 + 128, model_width // 4)
+        ],
+        in_specs=[pl.BlockSpec(memory_space=pltpu.SMEM)] + [pl.BlockSpec(memory_space=pl.ANY)] * 4,
+        out_specs=[pl.BlockSpec(memory_space=pltpu.VMEM)] * 3,
+        scratch_shapes=[pltpu.VMEM(a.shape, a.dtype) for a in arrays]
+        + [pltpu.SemaphoreType.DMA((4,))],
+        compiler_params=pltpu.CompilerParams(vmem_limit_bytes=60 * 1024 * 1024),
+        name="prepare",
+    )(place, *arrays)
+
+
+def mlp_body(plan, steps, carried, outs, cap, place, *refs):
+    count = 1 + max(piece for _, where in plan for piece, _ in where.values())
+    pieces, (w_gate, w_up, w_down) = refs[:count], refs[count : count + 3]
+    refs = refs[count + 3 :]
+    before = refs[:2] if carried else ()
+    refs = refs[2:] if carried else refs
+    results, (gate_w, up_w, down_w, in_sems, down_sems) = refs[:-5], refs[-5:]
+    model_width, hidden_width = w_gate.shape[1], w_gate.shape[2]
+    step = gate_w.shape[1]
+    total = model_width // step
+
+    def start_of(number):
+        side, index = number // (total // 2), number % (total // 2)
+        return pl.multiple_of(jnp.where(place[0] == side, 0, model_width // 2) + index * step, step)
+
+    def load(at, number):
+        rows = pl.ds(start_of(number), step)
+        return (
+            pltpu.make_async_copy(w_gate.at[0, rows, :], gate_w.at[at], in_sems.at[0, at]),
+            pltpu.make_async_copy(w_up.at[0, rows, :], up_w.at[at], in_sems.at[1, at]),
+        )
+
+    def load_down(number):
+        return pltpu.make_async_copy(
+            w_down.at[0, :, pl.ds(start_of(number), step)], down_w.at[number], down_sems.at[number]
+        )
+
+    order = (2, 0, 1, 3)
+    for at, number in enumerate(steps):
+        for copy in load(at, number):
+            copy.start()
+    for number in order if outs else ():
+        load_down(number).start()
+    gates, ups = [], []
+    first = 0
+    for rows, _ in plan:
+        for sums, ref in zip((gates, ups), before or (None, None)):
+            zero = jnp.zeros((rows, hidden_width), F32)
+            sums.append(zero if ref is None else ref[first : first + rows, :])
+        first += rows
+    for at, number in enumerate(steps):
+        for copy in load(at, number):
+            copy.wait()
+        for b, (_, where) in enumerate(plan):
+            piece, column = where[number]
+            x = pieces[piece][:, column : column + step]
+            gates[b] += jnp.dot(x, gate_w[at], preferred_element_type=F32)
+            ups[b] += jnp.dot(x, up_w[at], preferred_element_type=F32)
+    if not outs:
+        first = 0
+        for gate, up in zip(gates, ups):
+            for ref, value in zip(results, (gate, up)):
+                ref[first : first + value.shape[0], :] = value
+            first += gate.shape[0]
+        return
+    hidden = [(g / (1.0 + jnp.exp(-g)) * u).astype(BF16) for g, u in zip(gates, ups)]
+    if cap:
+        rows = plan[0][0]
+        to = lax.broadcasted_iota(jnp.int32, (rows, rows), 0)
+        of = lax.broadcasted_iota(jnp.int32, (rows, rows), 1)
+        spot = to % (rows // 2)
+        moved = spot // cap * 2 * cap + to // (rows // 2) * cap + spot % cap == of
+        hidden = [
+            jnp.dot(
+                moved.astype(F32).astype(BF16), hidden[0], preferred_element_type=F32
+            ).astype(BF16)
+        ]
+    for number in order:
+        load_down(number).wait()
+        first = 0
+        for h in hidden:
+            y = jnp.dot(h, down_w[number], preferred_element_type=F32).astype(BF16)
+            for (start, rows, covers), ref in zip(outs, results):
+                low, high = max(start, first), min(start + rows, first + h.shape[0])
+                if number in covers and low < high:
+                    at = covers.index(number) * step
+                    ref[low - start : high - start, at : at + step] = y[low - first : high - first]
+            first += h.shape[0]
+
+
+def mlp(place, blocks, steps, before, w_gate, w_up, w_down, outs, cap=0):
+    _, model_width, hidden_width = w_gate.shape
+    total = 4
+    step = model_width // total
+    plan, pieces = [], []
+    for block in blocks:
+        where = {}
+        for piece, covers in block:
+            for at, number in enumerate(covers):
+                where[number] = (len(pieces), at * step)
+            pieces.append(piece)
+        plan.append((block[0][0].shape[0], where))
+    rows = sum(r for r, _ in plan)
+    vmem = pl.BlockSpec(memory_space=pltpu.VMEM)
+    if outs:
+        shapes = [jax.ShapeDtypeStruct((r, len(c) * step), BF16) for _, r, c in outs]
+    else:
+        shapes = [jax.ShapeDtypeStruct((rows, hidden_width), F32)] * 2
+    return pl.pallas_call(
+        functools.partial(mlp_body, plan, steps, bool(before), outs, cap),
+        out_shape=shapes,
+        in_specs=[pl.BlockSpec(memory_space=pltpu.SMEM)]
+        + [vmem] * len(pieces)
+        + [pl.BlockSpec(memory_space=pl.ANY)] * 3
+        + [vmem] * len(before),
+        out_specs=[vmem] * len(shapes),
+        scratch_shapes=[
+            pltpu.VMEM((len(steps), step, hidden_width), BF16),
+            pltpu.VMEM((len(steps), step, hidden_width), BF16),
+            pltpu.VMEM((total if outs else 1, hidden_width, step), BF16),
+            pltpu.SemaphoreType.DMA((2, len(steps))),
+            pltpu.SemaphoreType.DMA((total,)),
+        ],
+        compiler_params=pltpu.CompilerParams(vmem_limit_bytes=40 * 1024 * 1024),
+        cost_estimate=pl.CostEstimate(
+            flops=4 * rows * step * len(steps) * hidden_width
+            + (2 * rows * model_width * hidden_width if outs else 0),
+            bytes_accessed=4 * step * len(steps) * hidden_width
+            + (2 * model_width * hidden_width if outs else 0),
+            transcendentals=rows * hidden_width if outs else 0,
+        ),
+        name="mlp",
+    )(place, *pieces, w_gate, w_up, w_down, *before)
+
+
+def join_body(cap, column, keep, crossed, beside, slanted, *outs):
+    rows, width = keep.shape
+    first = (keep[...].astype(F32) + crossed[...].astype(F32)).astype(BF16)
+    second = beside[:, column : column + width].astype(F32) + slanted[...].astype(F32)
+    second = second.astype(BF16)
+    to = lax.broadcasted_iota(jnp.int32, (2 * cap, rows), 0)
+    of = lax.broadcasted_iota(jnp.int32, (2 * cap, rows), 1)
+    for q, out in enumerate(outs):
+        here = (q * cap + to % cap == of).astype(F32)
+        out[...] = (
+            jnp.dot(jnp.where(to < cap, here, 0.0).astype(BF16), first, preferred_element_type=F32)
+            + jnp.dot(jnp.where(to < cap, 0.0, here).astype(BF16), second, preferred_element_type=F32)
+        ).astype(BF16)
+
+
+def join(cap, chips, column, keep, crossed, beside, slanted):
+    vmem = pl.BlockSpec(memory_space=pltpu.VMEM)
+    return pl.pallas_call(
+        functools.partial(join_body, cap, column),
+        out_shape=[jax.ShapeDtypeStruct((2 * cap, keep.shape[1]), BF16)] * chips,
+        in_specs=[vmem] * 4,
+        out_specs=[vmem] * chips,
+        compiler_params=pltpu.CompilerParams(vmem_limit_bytes=32 * 1024 * 1024),
+        name="join",
+    )(keep, crossed, beside, slanted)
+
+
+def two_sections(experts, tokens, norm_gain, router, w_gate, w_up, w_down, expert_ids):
+    tok_count, model_width = tokens.shape
+    top_count = expert_ids.shape[1]
+    cap = tok_count * top_count * 3 // (2 * experts)
+    width = model_width // 2
+    half = experts // 2
+    chips = experts // 4
+    me = lax.axis_index("expert")
+    section = lax.axis_index("section")
+    place = jnp.reshape(section, (1,)).astype(jnp.int32)
+    group = 2 * cap
+
+    def swap(value, mask):
+        return lax.ppermute(value, "expert", [(i, i ^ mask) for i in range(experts)])
+
+    def cross(value):
+        return lax.ppermute(value, "section", [(0, 1), (1, 0)])
+
+    def slant(value):
+        pairs = [(s * experts + i, (1 - s) * experts + (i ^ 1)) for s in (0, 1) for i in range(experts)]
+        return lax.ppermute(value, ("section", "expert"), pairs)
+
+    packed, mine_0, mine_1 = prepare(experts, place, tokens, norm_gain, router, expert_ids)
+    beside = swap(packed, 1)
+
+    near = (((me // 2) ^ jnp.arange(chips, dtype=jnp.int32)) * 2 + me % 2)[:, None]
+    lanes = jnp.arange(128, dtype=jnp.int32)[None, :]
+    near = jnp.concatenate([near == lanes, near + experts == lanes], axis=0).astype(BF16)
+    row = lax.broadcasted_iota(jnp.int32, (1, group, 2 * tok_count), 1)
+    col = lax.broadcasted_iota(jnp.int32, (1, group, 2 * tok_count), 2)
+    wanted = jnp.where(row // cap == col // tok_count, row % cap, -2).astype(F32)
+
+    def tables(first, second):
+        found = jnp.concatenate(
+            [
+                lax.dot_general(near, m, (((1,), (1,)), ((), ())), preferred_element_type=F32)
+                for m in (first, second)
+            ],
+            axis=1,
+        )
+        chosen = found[:chips, None, :] == wanted
+        factors = jnp.where(chosen, found[chips:, None, :], 0.0).astype(BF16)
+        return chosen.astype(BF16), factors.reshape(chips * group, 2 * tok_count)
+
+    def pick(chosen, first, second):
+        flat = chosen.reshape(-1, 2 * tok_count)
+        return (
+            jnp.dot(flat[:, :tok_count], first, preferred_element_type=F32)
+            + jnp.dot(flat[:, tok_count:], second, preferred_element_type=F32)
+        ).astype(BF16)
+
+    def pieces_of(rows, number):
+        return [rows[q * group : (q + 1) * group] for q in range(number)]
+
+    def spread(pieces):
+        return [swap(piece, 2 * q) if q else piece for q, piece in enumerate(pieces)]
+
+    def mix(factors, rows):
+        return lax.dot_general(
+            factors, rows, (((0,), (0,)), ((), ())), preferred_element_type=F32
+        )
+
+    def stage(*values):
+        return lax.optimization_barrier(values)
+
+    def core_sum(mixed):
+        got = swap(mixed[tok_count:].astype(BF16), 1)
+        return mixed[:tok_count], got
+
+    def both_factors(block):
+        number = jnp.arange(2 * chips, dtype=jnp.int32)
+        number = (((me // 2) ^ (number // 2)) * 2 + (me % 2 ^ number % 2))[:, None]
+        at = jnp.concatenate([number == lanes, number + experts == lanes], axis=0).astype(BF16)
+        found = lax.dot_general(at, block, (((1,), (1,)), ((), ())), preferred_element_type=F32)
+        found = found.reshape(2, chips, 2, 1, tok_count)
+        line = lax.broadcasted_iota(jnp.int32, (1, group, tok_count), 1)
+        slot, weight = jnp.where(line < cap, found[:, :, 0], found[:, :, 1])
+        chosen = slot == (line % cap).astype(F32)
+        return jnp.where(chosen, weight, 0.0).astype(BF16).reshape(chips * group, tok_count)
+
+    weights = (w_gate, w_up, w_down)
+    part = width // 2
+    meta = packed[:, model_width:]
+    far_0 = swap(mine_0, half)
+
+    chosen, factors = tables(meta, beside[:, model_width:])
+    some = pieces_of(pick(chosen[2:], packed[:, :width], beside[:, :width]), chips - 2)
+    whole = pick(chosen[:2], packed[:, :model_width], beside[:, :model_width])
+    some = [swap(piece, 2 * q) for q, piece in enumerate(some, 2)]
+    whole_near = swap(whole[group:], 2)
+    some, whole_0, whole_near, far_0, mine_1 = stage(some, whole[:group], whole_near, far_0, mine_1)
+
+    some = jnp.concatenate(some, axis=0)
+    some_other = cross(some)
+    far_1 = swap(mine_1, half)
+    beside_0 = swap(far_0, 1)
+    far_chosen, _ = tables(far_0[:, part:], beside_0[:, part:])
+    rows_0 = spread(pieces_of(pick(far_chosen, far_0[:, :part], beside_0[:, :part]), chips))
+    some, rows_0, far_1 = stage(some, rows_0, far_1)
+
+    rows_0 = jnp.concatenate(rows_0, axis=0)
+    other_0 = cross(rows_0)
+    rows_1 = spread(pieces_of(pick(far_chosen, far_1, swap(far_1, 1)), chips))
+    whole = jnp.concatenate([whole_0, whole_near], axis=0)
+    all_rows = chips * group
+    (near,) = mlp(
+        place, [[(whole, (0, 1, 2, 3))], [(some, (0, 1)), (some_other, (2, 3))]],
+        (0, 1, 2, 3), (), *weights, [(0, all_rows, (0, 1, 2, 3))],
+    )
+    rows_0, rows_1, near = stage(rows_0, rows_1, near)
+
+    rows_1 = jnp.concatenate(rows_1, axis=0)
+    other_1 = cross(rows_1)
+    near = pieces_of(near, chips)
+    near_back = near[:1] + [swap(near[q], 2 * q) for q in range(1, chips - 1)]
+    sums = mlp(
+        place, [[(rows_0, (0,)), (rows_1, (1,)), (other_0, (2,))]], (0, 1, 2), (), *weights, ()
+    )
+    other_1, near_back, near_last, sums = stage(other_1, near_back, near[-1], sums)
+
+    side = all_rows // 2
+    outs = mlp(
+        place, [[(other_1, (3,))]], (3,), sums, *weights,
+        [(first, side, (k,)) for k in (2, 0, 1, 3) for first in (0, side)], cap,
+    )
+    (give_0, slant_0, keep_0, core_0, keep_1, core_1, give_1, slant_1), near_last = stage(outs, near_last)
+    got_0 = cross(give_0)
+    slant_0 = slant(slant_0)
+    core_0 = swap(core_0, 1)
+    near_last = swap(near_last, 2 * (chips - 1))
+    got_1 = cross(give_1)
+    slant_1 = slant(slant_1)
+    got_0, slant_0, core_0, near_last, core_1, near_back = stage(
+        got_0, slant_0, core_0, near_last, core_1, near_back
+    )
+
+    core_1 = swap(core_1, 1)
+    back_0 = spread(join(cap, chips, 0, keep_0, got_0, core_0, slant_0))
+    near_sum = mix(factors, jnp.concatenate(near_back + [near_last], axis=0))
+    got_1, slant_1, core_1, back_0, near_sum = stage(got_1, slant_1, core_1, back_0, near_sum)
+
+    far_factors = both_factors(far_0[:, part:])
+    far_0 = swap(mix(far_factors, jnp.concatenate(back_0, axis=0)).astype(BF16), half)
+    back_1 = spread(join(cap, chips, 0, keep_1, got_1, core_1, slant_1))
+    near_sum, near_core = core_sum(near_sum)
+    near_sum, near_core, far_0, back_1 = stage(near_sum, near_core, far_0, back_1)
+
+    far_1 = swap(mix(far_factors, jnp.concatenate(back_1, axis=0)).astype(BF16), half)
+    near_sum = near_sum + near_core.astype(F32)
+    near_got = cross(near_sum[:, width:].astype(BF16))
+    far_sum = jnp.concatenate([far_0, far_1], axis=1).astype(F32)
+    residual = lax.dynamic_slice_in_dim(tokens, section * width, width, 1)
+    return (residual.astype(F32) + near_sum[:, :width] + near_got.astype(F32) + far_sum).astype(BF16)
+
+
 def solution(mesh):
     placed = (
         P("expert", None),
@@ -134,7 +514,10 @@
     )
 
     def body(*args):
-        return per_device(mesh.shape["section"], mesh.shape["expert"], *args)
+        sections, experts = mesh.shape["section"], mesh.shape["expert"]
+        if sections == 2 and experts <= 64:
+            return two_sections(experts, *args)
+        return any_sections(sections, experts, *args)
 
     return jax.shard_map(
         body, mesh=mesh, in_specs=placed, out_specs=P("expert", "section"), check_vma=False

time: 177 us -> 143 us (0.81)
  waiting for transfers between devices: 108 us -> 73 us
  Pallas kernels: 0 us -> 18.6 us
  matrix products: 21.1 us -> 7.45 us
  starting transfers between devices: 30 us -> 39.1 us
  other arithmetic: 11 us -> 3.01 us
  local copies, waits for them, and re-layouts: 6.1 us -> 0.84 us
    pallas_call x0 -> x6, Pallas kernels: none -> 18.6 us  [the longest x3 14.3 us: mlp(): pl.pallas_call(functools.partial(mlp_body, plan, steps, bool(before), out...]
    ppermute x24 -> x28, waiting for transfers between devices: 71.4 us -> 53.3 us  [swap(): lax.ppermute(value, 'expert', [(i, i ^ mask) for i in range(experts)])]
    ppermute x4 -> x8, waiting for transfers between devices: 37 us -> 19.7 us  [the longest x6 17.3 us: cross(): return lax.ppermute(value, 'section', [(0, 1), (1, 0)])]
    dot_general x17 -> x16, matrix products: 21.1 us -> 7.45 us  [the longest x3 2.46 us: mix(): lax.dot_general(factors, rows, (((0,), (0,)), ((), ())), preferred_elemen...]
    ppermute x24 -> x28, starting transfers between devices: 24.7 us -> 31.4 us  [swap(): lax.ppermute(value, 'expert', [(i, i ^ mask) for i in range(experts)])]
    convert_element_type x7 -> x5, other arithmetic: 5.14 us -> 2.37 us  [the longest x1 2.04 us: two_sections(): (residual.astype(F32) + near_sum[:, :width] + near_got.astype(F32) + far_...]
    select_n x2 -> x1, other arithmetic: 2.71 us -> 0.09 us  [both_factors(): slot, weight = jnp.where(line < cap, found[:, :, 0], found[:, :, 1])]
    unnamed x24 -> x19, local copies, waits for them, and re-layouts: 2.67 us -> 0.15 us
  transfers between devices with their start and end apart: 28 -> 36, of which waited for: 18 -> 21; matrix products, arithmetic and copies ran while one was open for 20% -> 6% of each run, Pallas kernels for 0% -> 8%
where the time goes in v2:
time: 143 us; the launch traced here: 142 us
  waiting for transfers between devices  73 us (51%)
  starting transfers between devices  39.1 us (27%)
  Pallas kernels  18.6 us (13%)
  matrix products  7.45 us (5%)
  other arithmetic  3.01 us (2%)
    ppermute x28, waiting for transfers between devices, swap(): lax.ppermute(value, 'expert', [(i, i ^ mask) for i in range(experts)])  53.3 us
    ppermute x28, starting transfers between devices, swap(): lax.ppermute(value, 'expert', [(i, i ^ mask) for i in range(experts)])  31.4 us
    ppermute x6, waiting for transfers between devices, cross(): return lax.ppermute(value, 'section', [(0, 1), (1, 0)])  17.3 us
    pallas_call x3, Pallas kernels, mlp(): pl.pallas_call(functools.partial(mlp_body, plan, steps, bool(before), out...  14.3 us
    ppermute x6, starting transfers between devices, cross(): return lax.ppermute(value, 'section', [(0, 1), (1, 0)])  7.62 us
    pallas_call x1, Pallas kernels, prepare(): pl.pallas_call(functools.partial(prepare_body, experts), out_shape=[jax.S...  3.15 us
  transfers between devices with their start and end apart: 36, of which 21 were waited for; matrix products, arithmetic and copies ran while one was open for 6% of the time, Pallas kernels for 8%

profile of v2, /device:TPU:0, one launch (start us, length us, event | category | flops | bytes accessed | tf_op | source)
XLA Modules:
  0.0 142.4 jit_solution(6192272979718046783)
XLA Ops:
  0.0 3.2 %prepare.1 = (bf16[128,3712]{1,0:T(8,128)(2,1)}, bf16[128,1024]{1,0:T(8,128)(2,1)}, bf16[128,896]{1,0:T(8,128)(2,1)}) custom-call(s32[1]{0:T(128)} %bitcast.place, bf16[128,3584]{1,0:T(8,128)(2,1)} %refs_0_.1, bf16[3584]{0:T(1024)(128)(2,1)} %refs_1_.2, bf16[16,3584]{1,0:T(8,128)(2,1)} %bitcast.36, s32[3,128]{1,0:T(4,128)} %bitcast.40), custom_call_target="tpu_custom_call" | custom-call | tf_op jit(solution)/shard_map/prepare/pallas_call | solution.py:183
  3.2 4.1 %collective-permute-start.4 = (bf16[128,1024]{1,0:T(8,128)(2,1)}, bf16[128,1024]{1,0:T(8,128)(2,1)S(1)}, u32[]{:S(2)}, u32[]{:S(2)}) collective-permute-start(bf16[128,1024]{1,0:T(8,128)(2,1)} %get-tuple-element.84), channel_id=1, source_target_pairs={{0,8},{1,9},{2,10},{3,11},{4,12},{5,13},{6,14},{7,15},{8,0},{9,1},... | collective-permute-start | bytes 786440 | tf_op jit(solution)/shard_map/ppermute | solution.py:363
  16.5 3.0 %collective-permute-done.4 = bf16[128,1024]{1,0:T(8,128)(2,1)S(1)} collective-permute-done((bf16[128,1024]{1,0:T(8,128)(2,1)}, bf16[128,1024]{1,0:T(8,128)(2,1)S(1)}, u32[]{:S(2)}, u32[]{:S(2)}) %collective-permute-start.4) | collective-permute-done | bytes 262176 | tf_op jit(solution)/shard_map/ppermute | solution.py:363
  19.5 6.5 %collective-permute-done.2 = bf16[72,1792]{1,0:T(8,128)(2,1)S(1)} collective-permute-done((bf16[72,1792]{1,0:T(8,128)(2,1)S(1)}, bf16[72,1792]{1,0:T(8,128)(2,1)S(1)}, u32[]{:S(2)}, u32[]{:S(2)}) %collective-permute-start.2) | collective-permute-done | bytes 258080 | tf_op jit(solution)/shard_map/ppermute | solution.py:363
  26.1 4.5 %collective-permute-done.1 = bf16[72,1792]{1,0:T(8,128)(2,1)S(1)} collective-permute-done((bf16[72,1792]{1,0:T(8,128)(2,1)S(1)}, bf16[72,1792]{1,0:T(8,128)(2,1)S(1)}, u32[]{:S(2)}, u32[]{:S(2)}) %collective-permute-start.1) | collective-permute-done | bytes 258080 | tf_op jit(solution)/shard_map/ppermute | solution.py:363
  34.9 3.4 %collective-permute-start.8 = (bf16[72,896]{1,0:T(8,128)(2,1)S(1)}, bf16[72,896]{1,0:T(8,128)(2,1)S(1)}, u32[]{:S(2)}, u32[]{:S(2)}) collective-permute-start(bf16[72,896]{1,0:T(8,128)(2,1)S(1)} %get-tuple-element.177), channel_id=1, source_target_pairs={{0,6},{1,7},{2,4},{3,5},{4,2},{5,3},{6,0},{7,1},{8,14},{9,15},{10,... | collective-permute-start | bytes 387080 | tf_op jit(solution)/shard_map/ppermute | solution.py:363
  39.1 5.5 %collective-permute-done.9 = bf16[128,896]{1,0:T(8,128)(2,1)S(1)} collective-permute-done((bf16[128,896]{1,0:T(8,128)(2,1)S(1)}, bf16[128,896]{1,0:T(8,128)(2,1)S(1)}, u32[]{:S(2)}, u32[]{:S(2)}) %collective-permute-start.9) | collective-permute-done | bytes 229408 | tf_op jit(solution)/shard_map/ppermute | solution.py:363
  44.6 1.8 %collective-permute-done.8 = bf16[72,896]{1,0:T(8,128)(2,1)S(1)} collective-permute-done((bf16[72,896]{1,0:T(8,128)(2,1)S(1)}, bf16[72,896]{1,0:T(8,128)(2,1)S(1)}, u32[]{:S(2)}, u32[]{:S(2)}) %collective-permute-start.8) | collective-permute-done | bytes 129056 | tf_op jit(solution)/shard_map/ppermute | solution.py:363
  46.4 1.7 %collective-permute-done.7 = bf16[72,896]{1,0:T(8,128)(2,1)S(1)} collective-permute-done((bf16[72,896]{1,0:T(8,128)(2,1)S(1)}, bf16[72,896]{1,0:T(8,128)(2,1)S(1)}, u32[]{:S(2)}, u32[]{:S(2)}) %collective-permute-start.7) | collective-permute-done | bytes 129056 | tf_op jit(solution)/shard_map/ppermute | solution.py:363
  50.5 2.5 %collective-permute-start.12 = (bf16[72,896]{1,0:T(8,128)(2,1)S(1)}, bf16[72,896]{1,0:T(8,128)(2,1)S(1)}, u32[]{:S(2)}, u32[]{:S(2)}) collective-permute-start(bf16[72,896]{1,0:T(8,128)(2,1)S(1)} %get-tuple-element.174), channel_id=1, source_target_pairs={{0,4},{1,5},{2,6},{3,7},{4,0},{5,1},{6,2},{7,3},{8,12},{9,13},{10,... | collective-permute-start | bytes 387080 | tf_op jit(solution)/shard_map/ppermute | solution.py:363
  53.8 6.8 %mlp.3 = bf16[288,3584]{1,0:T(8,128)(2,1)S(1)} custom-call(s32[1]{0:T(128)} %bitcast.place, bf16[144,3584]{1,0:T(8,128)(2,1)S(1)} %pad_maximum_fusion.refs_0_, bf16[144,1792]{1,0:T(8,128)(2,1)S(1)} %constant_dynamic-update-slice_fusion.refs_1_, bf16[144,1792]{1,0:T(8,128)(2,1)S(1)} %collective-permute-done.14.refs_2_, bf16[1,3584,512]{2,1,0:T(8,128)(2,1)S(1)} %copy-done, ...), custom_call_target="tpu_custom_call" | custom-call | flops 3170893824 | bytes 11010048 | tf_op jit(solution)/shard_map/mlp/pallas_call | solution.py:296
  63.6 3.7 %mlp.4 = (f32[288,512]{1,0:T(8,128)S(1)}, f32[288,512]{1,0:T(8,128)S(1)}) custom-call(s32[1]{0:T(128)} %bitcast.place, bf16[288,896]{1,0:T(8,128)(2,1)S(1)} %constant_dynamic-update-slice_fusion.2.refs_0_, bf16[288,896]{1,0:T(8,128)(2,1)S(1)} %constant_dynamic-update-slice_fusion.6.refs_1_, bf16[288,896]{1,0:T(8,128)(2,1)S(1)} %collective-permute-done.18.refs_2_, ...), custom_call_target="tpu_custom_call" | custom-call | flops 1585446912 | bytes 5505024 | tf_op jit(solution)/shard_map/mlp/pallas_call | solution.py:296
  67.3 6.5 %collective-permute-done.15.refs_0_ = bf16[288,896]{1,0:T(8,128)(2,1)S(1)} collective-permute-done((bf16[288,896]{1,0:T(8,128)(2,1)S(1)}, bf16[288,896]{1,0:T(8,128)(2,1)S(1)}, u32[]{:S(2)}, u32[]{:S(2)}) %collective-permute-start.15) | collective-permute-done | bytes 516128 | tf_op jit(solution)/shard_map/ppermute | solution.py:366
  75.0 3.8 %mlp.5 = (bf16[144,896]{1,0:T(8,128)(2,1)S(1)}, bf16[144,896]{1,0:T(8,128)(2,1)S(1)}, bf16[144,896]{1,0:T(8,128)(2,1)S(1)}, bf16[144,896]{1,0:T(8,128)(2,1)S(1)}...) custom-call(s32[1]{0:T(128)} %bitcast.place, ...), custom_call_target="tpu_custom_call" | custom-call | flops 1585446912 | bytes 5505024 | tf_op jit(solution)/shard_map/mlp/pallas_call | solution.py:296
  78.8 2.4 %collective-permute-start.24 = (bf16[72,3584]{1,0:T(8,128)(2,1)S(1)}, bf16[72,3584]{1,0:T(8,128)(2,1)S(1)}, u32[]{:S(2)}, u32[]{:S(2)}) collective-permute-start(bf16[72,3584]{1,0:T(8,128)(2,1)S(1)} %get-tuple-element.123), channel_id=1, source_target_pairs={{0,6},{1,7},{2,4},{3,5},{4,2},{5,3},{6,0},{7,1},{8,14},{9,15},{10,... | collective-permute-start | bytes 1548296 | tf_op jit(solution)/shard_map/ppermute | solution.py:363
  84.4 10.8 %collective-permute-done.21.crossed = bf16[144,896]{1,0:T(8,128)(2,1)S(1)} collective-permute-done((bf16[144,896]{1,0:T(8,128)(2,1)S(1)}, bf16[144,896]{1,0:T(8,128)(2,1)S(1)}, u32[]{:S(2)}, u32[]{:S(2)}) %collective-permute-start.21) | collective-permute-done | bytes 258080 | tf_op jit(solution)/shard_map/ppermute | solution.py:366
  98.5 2.0 %collective-permute-start.28 = (bf16[72,896]{1,0:T(8,128)(2,1)S(1)}, bf16[72,896]{1,0:T(8,128)(2,1)S(1)}, u32[]{:S(2)}, u32[]{:S(2)}) collective-permute-start(bf16[72,896]{1,0:T(8,128)(2,1)S(1)} %get-tuple-element.136), channel_id=1, source_target_pairs={{0,6},{1,7},{2,4},{3,5},{4,2},{5,3},{6,0},{7,1},{8,14},{9,15},{10,... | collective-permute-start | bytes 387080 | tf_op jit(solution)/shard_map/ppermute | solution.py:363
  103.9 3.4 %collective-permute-done.28 = bf16[72,896]{1,0:T(8,128)(2,1)S(1)} collective-permute-done((bf16[72,896]{1,0:T(8,128)(2,1)S(1)}, bf16[72,896]{1,0:T(8,128)(2,1)S(1)}, u32[]{:S(2)}, u32[]{:S(2)}) %collective-permute-start.28) | collective-permute-done | bytes 129056 | tf_op jit(solution)/shard_map/ppermute | solution.py:363
  108.1 3.2 %collective-permute-start.30 = (bf16[128,896]{1,0:T(8,128)(2,1)S(1)}, bf16[128,896]{1,0:T(8,128)(2,1)S(1)}, u32[]{:S(2)}, u32[]{:S(2)}) collective-permute-start(bf16[128,896]{1,0:T(8,128)(2,1)S(1)} %convolution_convert_fusion.1), channel_id=1, source_target_pairs={{0,8},{1,9},{2,10},{3,11},{4,12},{5,13},{6,14},{7,15},{8,0},{9,1},... | collective-permute-start | bytes 688136 | tf_op jit(solution)/shard_map/ppermute | solution.py:363
  115.6 1.8 %collective-permute-done.31 = bf16[72,896]{1,0:T(8,128)(2,1)S(1)} collective-permute-done((bf16[72,896]{1,0:T(8,128)(2,1)S(1)}, bf16[72,896]{1,0:T(8,128)(2,1)S(1)}, u32[]{:S(2)}, u32[]{:S(2)}) %collective-permute-start.31) | collective-permute-done | bytes 129056 | tf_op jit(solution)/shard_map/ppermute | solution.py:363
  117.4 6.1 %collective-permute-done.32 = bf16[72,896]{1,0:T(8,128)(2,1)S(1)} collective-permute-done((bf16[72,896]{1,0:T(8,128)(2,1)S(1)}, bf16[72,896]{1,0:T(8,128)(2,1)S(1)}, u32[]{:S(2)}, u32[]{:S(2)}) %collective-permute-start.32) | collective-permute-done | bytes 129056 | tf_op jit(solution)/shard_map/ppermute | solution.py:363
  123.5 1.9 %collective-permute-done.33 = bf16[72,896]{1,0:T(8,128)(2,1)S(1)} collective-permute-done((bf16[72,896]{1,0:T(8,128)(2,1)S(1)}, bf16[72,896]{1,0:T(8,128)(2,1)S(1)}, u32[]{:S(2)}, u32[]{:S(2)}) %collective-permute-start.33) | collective-permute-done | bytes 129056 | tf_op jit(solution)/shard_map/ppermute | solution.py:363
  128.0 12.4 %collective-permute-done.35 = bf16[128,896]{1,0:T(8,128)(2,1)} collective-permute-done((bf16[128,896]{1,0:T(8,128)(2,1)}, bf16[128,896]{1,0:T(8,128)(2,1)}, u32[]{:S(2)}, u32[]{:S(2)}) %collective-permute-start.35) | collective-permute-done | bytes 229408 | tf_op jit(solution)/shard_map/ppermute | solution.py:363
  140.4 2.0 %fusion.14 = bf16[128,1792]{1,0:T(8,128)(2,1)} fusion(f32[128,3584]{1,0:T(8,128)S(1)} %convert_add_fusion, bf16[128,1792]{1,0:T(8,128)(2,1)} %collective-permute-done.34, bf16[128,896]{1,0:T(8,128)(2,1)} %collective-permute-done.35, bf16[128,896]{1,0:T(8,128)(2,1)S(1)} %collective-permute-done.30, bf16[128,3584]{1,0:T(8,128)(2,1)S(1)} %copy-done.4, ...), kind=kLoop, calls=%fused_computation.25 | loop fusion | flops 2293760 | bytes 2752516 | tf_op jit(solution)/shard_map/convert_element_type | solution.py:502
  (126 shorter events, 38.9 us)
Async XLA Ops:
  3.2 16.3 %collective-permute-start.4 = (bf16[128,1024]{1,0:T(8,128)(2,1)}, bf16[128,1024]{1,0:T(8,128)(2,1)S(1)}, u32[]{:S(2)}, u32[]{:S(2)}) collective-permute-start(bf16[128,1024]{1,0:T(8,128)(2,1)} %get-tuple-element.84), channel_id=1, source_target_pairs={{0,8},{1,9},{2,10},{3,11},{4,12},{5,13},{6,14},{7,15},{8,0},{9,1},... | collective-permute-start | bytes 786440 | tf_op jit(solution)/shard_map/ppermute | solution.py:363
  12.5 19.4 %collective-permute-start.3 = (bf16[72,3584]{1,0:T(8,128)(2,1)S(1)}, bf16[72,3584]{1,0:T(8,128)(2,1)S(1)}, u32[]{:S(2)}, u32[]{:S(2)}) collective-permute-start(bf16[72,3584]{1,0:T(8,128)(2,1)S(1)} %get-tuple-element.171), channel_id=1, source_target_pairs={{0,2},{1,3},{2,0},{3,1},{4,6},{5,7},{6,4},{7,5},{8,10},{9,11},{10,... | collective-permute-start | bytes 1548296 | tf_op jit(solution)/shard_map/ppermute | solution.py:363
  14.4 11.7 %collective-permute-start.2 = (bf16[72,1792]{1,0:T(8,128)(2,1)S(1)}, bf16[72,1792]{1,0:T(8,128)(2,1)S(1)}, u32[]{:S(2)}, u32[]{:S(2)}) collective-permute-start(bf16[72,1792]{1,0:T(8,128)(2,1)S(1)} %get-tuple-element.181), channel_id=1, source_target_pairs={{0,6},{1,7},{2,4},{3,5},{4,2},{5,3},{6,0},{7,1},{8,14},{9,15},{10,... | collective-permute-start | bytes 774152 | tf_op jit(solution)/shard_map/ppermute | solution.py:363
  16.0 14.5 %collective-permute-start.1 = (bf16[72,1792]{1,0:T(8,128)(2,1)S(1)}, bf16[72,1792]{1,0:T(8,128)(2,1)S(1)}, u32[]{:S(2)}, u32[]{:S(2)}) collective-permute-start(bf16[72,1792]{1,0:T(8,128)(2,1)S(1)} %get-tuple-element.182), channel_id=1, source_target_pairs={{0,4},{1,5},{2,6},{3,7},{4,0},{5,1},{6,2},{7,3},{8,12},{9,13},{10,... | collective-permute-start | bytes 774152 | tf_op jit(solution)/shard_map/ppermute | solution.py:363
  31.9 12.7 %collective-permute-start.9 = (bf16[128,896]{1,0:T(8,128)(2,1)S(1)}, bf16[128,896]{1,0:T(8,128)(2,1)S(1)}, u32[]{:S(2)}, u32[]{:S(2)}) collective-permute-start(bf16[128,896]{1,0:T(8,128)(2,1)S(1)} %copy-done.5), channel_id=1, source_target_pairs={{0,8},{1,9},{2,10},{3,11},{4,12},{5,13},{6,14},{7,15},{8,0},{9,1},... | collective-permute-start | bytes 688136 | tf_op jit(solution)/shard_map/ppermute | solution.py:363
  32.3 21.5 %collective-permute-start.14 = (bf16[144,1792]{1,0:T(8,128)(2,1)S(1)}, bf16[144,1792]{1,0:T(8,128)(2,1)S(1)}, u32[]{:S(2)}, u32[]{:S(2)}) collective-permute-start(bf16[144,1792]{1,0:T(8,128)(2,1)S(1)} %constant_dynamic-update-slice_fusion.refs_1_), channel_id=1, source_target_pairs={{0,16},{16,0},{1,17},{17,1},{2,18},{18,2},{3,19},{19,3},{4,20},{20... | collective-permute-start | bytes 1548296 | tf_op jit(solution)/shard_map/ppermute | solution.py:366
  34.9 11.4 %collective-permute-start.8 = (bf16[72,896]{1,0:T(8,128)(2,1)S(1)}, bf16[72,896]{1,0:T(8,128)(2,1)S(1)}, u32[]{:S(2)}, u32[]{:S(2)}) collective-permute-start(bf16[72,896]{1,0:T(8,128)(2,1)S(1)} %get-tuple-element.177), channel_id=1, source_target_pairs={{0,6},{1,7},{2,4},{3,5},{4,2},{5,3},{6,0},{7,1},{8,14},{9,15},{10,... | collective-permute-start | bytes 387080 | tf_op jit(solution)/shard_map/ppermute | solution.py:363
  48.2 15.4 %collective-permute-start.18 = (bf16[288,896]{1,0:T(8,128)(2,1)S(1)}, bf16[288,896]{1,0:T(8,128)(2,1)S(1)}, u32[]{:S(2)}, u32[]{:S(2)}) collective-permute-start(bf16[288,896]{1,0:T(8,128)(2,1)S(1)} %constant_dynamic-update-slice_fusion.2.refs_0_), channel_id=1, source_target_pairs={{0,16},{16,0},{1,17},{17,1},{2,18},{18,2},{3,19},{19,3},{4,20},{20... | collective-permute-start | bytes 1548296 | tf_op jit(solution)/shard_map/ppermute | solution.py:366
  50.2 10.4 %collective-permute-start.13 = (bf16[72,896]{1,0:T(8,128)(2,1)S(1)}, bf16[72,896]{1,0:T(8,128)(2,1)S(1)}, u32[]{:S(2)}, u32[]{:S(2)}) collective-permute-start(bf16[72,896]{1,0:T(8,128)(2,1)S(1)} %get-tuple-element.173), channel_id=1, source_target_pairs={{0,6},{1,7},{2,4},{3,5},{4,2},{5,3},{6,0},{7,1},{8,14},{9,15},{10,... | collective-permute-start | bytes 387080 | tf_op jit(solution)/shard_map/ppermute | solution.py:363
  50.5 10.1 %collective-permute-start.12 = (bf16[72,896]{1,0:T(8,128)(2,1)S(1)}, bf16[72,896]{1,0:T(8,128)(2,1)S(1)}, u32[]{:S(2)}, u32[]{:S(2)}) collective-permute-start(bf16[72,896]{1,0:T(8,128)(2,1)S(1)} %get-tuple-element.174), channel_id=1, source_target_pairs={{0,4},{1,5},{2,6},{3,7},{4,0},{5,1},{6,2},{7,3},{8,12},{9,13},{10,... | collective-permute-start | bytes 387080 | tf_op jit(solution)/shard_map/ppermute | solution.py:363
  60.7 13.0 %collective-permute-start.15 = (bf16[288,896]{1,0:T(8,128)(2,1)S(1)}, bf16[288,896]{1,0:T(8,128)(2,1)S(1)}, u32[]{:S(2)}, u32[]{:S(2)}) collective-permute-start(bf16[288,896]{1,0:T(8,128)(2,1)S(1)} %constant_dynamic-update-slice_fusion.6.refs_1_), channel_id=1, source_target_pairs={{0,16},{16,0},{1,17},{17,1},{2,18},{18,2},{3,19},{19,3},{4,20},{20... | collective-permute-start | bytes 1548296 | tf_op jit(solution)/shard_map/ppermute | solution.py:366
  62.1 12.8 %collective-permute-start.17 = (bf16[72,3584]{1,0:T(8,128)(2,1)S(1)}, bf16[72,3584]{1,0:T(8,128)(2,1)S(1)}, u32[]{:S(2)}, u32[]{:S(2)}) collective-permute-start(bf16[72,3584]{1,0:T(8,128)(2,1)S(1)} %get-tuple-element.168), channel_id=1, source_target_pairs={{0,4},{1,5},{2,6},{3,7},{4,0},{5,1},{6,2},{7,3},{8,12},{9,13},{10,... | collective-permute-start | bytes 1548296 | tf_op jit(solution)/shard_map/ppermute | solution.py:363
  62.2 12.8 %collective-permute-start.16 = (bf16[72,3584]{1,0:T(8,128)(2,1)S(1)}, bf16[72,3584]{1,0:T(8,128)(2,1)S(1)}, u32[]{:S(2)}, u32[]{:S(2)}) collective-permute-start(bf16[72,3584]{1,0:T(8,128)(2,1)S(1)} %get-tuple-element.169), channel_id=1, source_target_pairs={{0,2},{1,3},{2,0},{3,1},{4,6},{5,7},{6,4},{7,5},{8,10},{9,11},{10,... | collective-permute-start | bytes 1548296 | tf_op jit(solution)/shard_map/ppermute | solution.py:363
  78.8 17.5 %collective-permute-start.24 = (bf16[72,3584]{1,0:T(8,128)(2,1)S(1)}, bf16[72,3584]{1,0:T(8,128)(2,1)S(1)}, u32[]{:S(2)}, u32[]{:S(2)}) collective-permute-start(bf16[72,3584]{1,0:T(8,128)(2,1)S(1)} %get-tuple-element.123), channel_id=1, source_target_pairs={{0,6},{1,7},{2,4},{3,5},{4,2},{5,3},{6,0},{7,1},{8,14},{9,15},{10,... | collective-permute-start | bytes 1548296 | tf_op jit(solution)/shard_map/ppermute | solution.py:363
  81.3 19.2 %collective-permute-start.19 = (bf16[144,896]{1,0:T(8,128)(2,1)S(1)}, bf16[144,896]{1,0:T(8,128)(2,1)S(1)}, u32[]{:S(2)}, u32[]{:S(2)}) collective-permute-start(bf16[144,896]{1,0:T(8,128)(2,1)S(1)} %get-tuple-element.118), channel_id=1, source_target_pairs={{0,16},{16,0},{1,17},{17,1},{2,18},{18,2},{3,19},{19,3},{4,20},{20... | collective-permute-start | bytes 774152 | tf_op jit(solution)/shard_map/ppermute | solution.py:366
  82.1 13.1 %collective-permute-start.21 = (bf16[144,896]{1,0:T(8,128)(2,1)S(1)}, bf16[144,896]{1,0:T(8,128)(2,1)S(1)}, u32[]{:S(2)}, u32[]{:S(2)}) collective-permute-start(bf16[144,896]{1,0:T(8,128)(2,1)S(1)} %get-tuple-element.120), channel_id=1, source_target_pairs={{0,16},{16,0},{1,17},{17,1},{2,18},{18,2},{3,19},{19,3},{4,20},{20... | collective-permute-start | bytes 774152 | tf_op jit(solution)/shard_map/ppermute | solution.py:366
  83.3 13.0 %collective-permute-start.22 = (bf16[144,896]{1,0:T(8,128)(2,1)S(1)}, bf16[144,896]{1,0:T(8,128)(2,1)S(1)}, u32[]{:S(2)}, u32[]{:S(2)}) collective-permute-start(bf16[144,896]{1,0:T(8,128)(2,1)S(1)} %get-tuple-element.121), channel_id=1, source_target_pairs={{0,17},{1,16},{2,19},{3,18},{4,21},{5,20},{6,23},{7,22},{8,25},{9,... | collective-permute-start | bytes 774152 | tf_op jit(solution)/shard_map/ppermute | solution.py:370
  83.3 13.0 %collective-permute-start.23 = (bf16[144,896]{1,0:T(8,128)(2,1)S(1)}, bf16[144,896]{1,0:T(8,128)(2,1)S(1)}, u32[]{:S(2)}, u32[]{:S(2)}) collective-permute-start(bf16[144,896]{1,0:T(8,128)(2,1)S(1)} %get-tuple-element.122), channel_id=1, source_target_pairs={{0,1},{1,0},{2,3},{3,2},{4,5},{5,4},{6,7},{7,6},{8,9},{9,8},{10,11... | collective-permute-start | bytes 774152 | tf_op jit(solution)/shard_map/ppermute | solution.py:363
  107.4 18.0 %collective-permute-start.29 = (bf16[128,3584]{1,0:T(8,128)(2,1)S(1)}, bf16[128,3584]{1,0:T(8,128)(2,1)S(1)}, u32[]{:S(2)}, u32[]{:S(2)}) collective-permute-start(bf16[128,3584]{1,0:T(8,128)(2,1)S(1)} %slice.262), channel_id=1, source_target_pairs={{0,1},{1,0},{2,3},{3,2},{4,5},{5,4},{6,7},{7,6},{8,9},{9,8},{10,11... | collective-permute-start | bytes 2752520 | tf_op jit(solution)/shard_map/ppermute | solution.py:363
  108.1 17.3 %collective-permute-start.30 = (bf16[128,896]{1,0:T(8,128)(2,1)S(1)}, bf16[128,896]{1,0:T(8,128)(2,1)S(1)}, u32[]{:S(2)}, u32[]{:S(2)}) collective-permute-start(bf16[128,896]{1,0:T(8,128)(2,1)S(1)} %convolution_convert_fusion.1), channel_id=1, source_target_pairs={{0,8},{1,9},{2,10},{3,11},{4,12},{5,13},{6,14},{7,15},{8,0},{9,1},... | collective-permute-start | bytes 688136 | tf_op jit(solution)/shard_map/ppermute | solution.py:363
  113.1 10.4 %collective-permute-start.32 = (bf16[72,896]{1,0:T(8,128)(2,1)S(1)}, bf16[72,896]{1,0:T(8,128)(2,1)S(1)}, u32[]{:S(2)}, u32[]{:S(2)}) collective-permute-start(bf16[72,896]{1,0:T(8,128)(2,1)S(1)} %get-tuple-element.152), channel_id=1, source_target_pairs={{0,4},{1,5},{2,6},{3,7},{4,0},{5,1},{6,2},{7,3},{8,12},{9,13},{10,... | collective-permute-start | bytes 387080 | tf_op jit(solution)/shard_map/ppermute | solution.py:363
  114.5 10.9 %collective-permute-start.33 = (bf16[72,896]{1,0:T(8,128)(2,1)S(1)}, bf16[72,896]{1,0:T(8,128)(2,1)S(1)}, u32[]{:S(2)}, u32[]{:S(2)}) collective-permute-start(bf16[72,896]{1,0:T(8,128)(2,1)S(1)} %get-tuple-element.153), channel_id=1, source_target_pairs={{0,6},{1,7},{2,4},{3,5},{4,2},{5,3},{6,0},{7,1},{8,14},{9,15},{10,... | collective-permute-start | bytes 387080 | tf_op jit(solution)/shard_map/ppermute | solution.py:363
  125.7 14.7 %collective-permute-start.34 = (bf16[128,1792]{1,0:T(8,128)(2,1)S(1)}, bf16[128,1792]{1,0:T(8,128)(2,1)}, u32[]{:S(2)}, u32[]{:S(2)}) collective-permute-start(bf16[128,1792]{1,0:T(8,128)(2,1)S(1)} %slice.263), channel_id=1, source_target_pairs={{0,16},{16,0},{1,17},{17,1},{2,18},{18,2},{3,19},{19,3},{4,20},{20... | collective-permute-start | bytes 1376264 | tf_op jit(solution)/shard_map/ppermute | solution.py:366
  128.0 12.4 %collective-permute-start.35 = (bf16[128,896]{1,0:T(8,128)(2,1)}, bf16[128,896]{1,0:T(8,128)(2,1)}, u32[]{:S(2)}, u32[]{:S(2)}) collective-permute-start(bf16[128,896]{1,0:T(8,128)(2,1)} %convolution_convert_fusion), channel_id=1, source_target_pairs={{0,8},{1,9},{2,10},{3,11},{4,12},{5,13},{6,14},{7,15},{8,0},{9,1},... | collective-permute-start | bytes 688136 | tf_op jit(solution)/shard_map/ppermute | solution.py:363
  (18 other events, 145.4 us)

commit v3 on v2

--- a/solution.py
+++ b/solution.py
@@ -8,6 +8,7 @@
 from jax.sharding import PartitionSpec as P
 
 EPSILON = 1e-06
+LEAD = 9
 F32, BF16 = jnp.float32, jnp.bfloat16
 
 
@@ -195,7 +196,7 @@
     )(place, *arrays)
 
 
-def mlp_body(plan, steps, carried, outs, cap, place, *refs):
+def mlp_body(plan, steps, carried, outs, columns, cap, place, *refs):
     count = 1 + max(piece for _, where in plan for piece, _ in where.values())
     pieces, (w_gate, w_up, w_down) = refs[:count], refs[count : count + 3]
     refs = refs[count + 3 :]
@@ -206,27 +207,29 @@
     step = gate_w.shape[1]
     total = model_width // step
 
-    def start_of(number):
-        side, index = number // (total // 2), number % (total // 2)
-        return pl.multiple_of(jnp.where(place[0] == side, 0, model_width // 2) + index * step, step)
+    def start_of(first):
+        moved = jnp.where(place[0] == first // (model_width // 2), 0, model_width // 2)
+        return pl.multiple_of(moved + first % (model_width // 2), 128)
 
     def load(at, number):
-        rows = pl.ds(start_of(number), step)
+        rows = pl.ds(start_of(number * step), step)
         return (
             pltpu.make_async_copy(w_gate.at[0, rows, :], gate_w.at[at], in_sems.at[0, at]),
             pltpu.make_async_copy(w_up.at[0, rows, :], up_w.at[at], in_sems.at[1, at]),
         )
 
     def load_down(number):
+        first, size = columns[number]
         return pltpu.make_async_copy(
-            w_down.at[0, :, pl.ds(start_of(number), step)], down_w.at[number], down_sems.at[number]
-        )
-
-    order = (2, 0, 1, 3)
+            w_down.at[0, :, pl.ds(start_of(first), size)],
+            down_w.at[:, pl.ds(first, size)],
+            down_sems.at[number],
+        )
+
     for at, number in enumerate(steps):
         for copy in load(at, number):
             copy.start()
-    for number in order if outs else ():
+    for number in range(len(columns)):
         load_down(number).start()
     gates, ups = [], []
     first = 0
@@ -262,20 +265,20 @@
                 moved.astype(F32).astype(BF16), hidden[0], preferred_element_type=F32
             ).astype(BF16)
         ]
-    for number in order:
+    for number, (left, size) in enumerate(columns):
         load_down(number).wait()
         first = 0
         for h in hidden:
-            y = jnp.dot(h, down_w[number], preferred_element_type=F32).astype(BF16)
-            for (start, rows, covers), ref in zip(outs, results):
+            y = jnp.dot(h, down_w[:, left : left + size], preferred_element_type=F32).astype(BF16)
+            for (start, rows, out_left, out_size), ref in zip(outs, results):
                 low, high = max(start, first), min(start + rows, first + h.shape[0])
-                if number in covers and low < high:
-                    at = covers.index(number) * step
-                    ref[low - start : high - start, at : at + step] = y[low - first : high - first]
+                if out_left <= left < out_left + out_size and low < high:
+                    at = left - out_left
+                    ref[low - start : high - start, at : at + size] = y[low - first : high - first]
             first += h.shape[0]
 
 
-def mlp(place, blocks, steps, before, w_gate, w_up, w_down, outs, cap=0):
+def mlp(place, blocks, steps, before, w_gate, w_up, w_down, outs, columns, cap=0):
     _, model_width, hidden_width = w_gate.shape
     total = 4
     step = model_width // total
@@ -290,11 +293,11 @@
     rows = sum(r for r, _ in plan)
     vmem = pl.BlockSpec(memory_space=pltpu.VMEM)
     if outs:
-        shapes = [jax.ShapeDtypeStruct((r, len(c) * step), BF16) for _, r, c in outs]
+        shapes = [jax.ShapeDtypeStruct((r, c), BF16) for _, r, _, c in outs]
     else:
         shapes = [jax.ShapeDtypeStruct((rows, hidden_width), F32)] * 2
     return pl.pallas_call(
-        functools.partial(mlp_body, plan, steps, bool(before), outs, cap),
+        functools.partial(mlp_body, plan, steps, bool(before), outs, columns, cap),
         out_shape=shapes,
         in_specs=[pl.BlockSpec(memory_space=pltpu.SMEM)]
         + [vmem] * len(pieces)
@@ -304,9 +307,9 @@
         scratch_shapes=[
             pltpu.VMEM((len(steps), step, hidden_width), BF16),
             pltpu.VMEM((len(steps), step, hidden_width), BF16),
-            pltpu.VMEM((total if outs else 1, hidden_width, step), BF16),
+            pltpu.VMEM((hidden_width, model_width if outs else 128), BF16),
             pltpu.SemaphoreType.DMA((2, len(steps))),
-            pltpu.SemaphoreType.DMA((total,)),
+            pltpu.SemaphoreType.DMA((max(1, len(columns)),)),
         ],
         compiler_params=pltpu.CompilerParams(vmem_limit_bytes=40 * 1024 * 1024),
         cost_estimate=pl.CostEstimate(
@@ -365,10 +368,6 @@
     def cross(value):
         return lax.ppermute(value, "section", [(0, 1), (1, 0)])
 
-    def slant(value):
-        pairs = [(s * experts + i, (1 - s) * experts + (i ^ 1)) for s in (0, 1) for i in range(experts)]
-        return lax.ppermute(value, ("section", "expert"), pairs)
-
     packed, mine_0, mine_1 = prepare(experts, place, tokens, norm_gain, router, expert_ids)
     beside = swap(packed, 1)
 
@@ -416,17 +415,6 @@
         got = swap(mixed[tok_count:].astype(BF16), 1)
         return mixed[:tok_count], got
 
-    def both_factors(block):
-        number = jnp.arange(2 * chips, dtype=jnp.int32)
-        number = (((me // 2) ^ (number // 2)) * 2 + (me % 2 ^ number % 2))[:, None]
-        at = jnp.concatenate([number == lanes, number + experts == lanes], axis=0).astype(BF16)
-        found = lax.dot_general(at, block, (((1,), (1,)), ((), ())), preferred_element_type=F32)
-        found = found.reshape(2, chips, 2, 1, tok_count)
-        line = lax.broadcasted_iota(jnp.int32, (1, group, tok_count), 1)
-        slot, weight = jnp.where(line < cap, found[:, :, 0], found[:, :, 1])
-        chosen = slot == (line % cap).astype(F32)
-        return jnp.where(chosen, weight, 0.0).astype(BF16).reshape(chips * group, tok_count)
-
     weights = (w_gate, w_up, w_down)
     part = width // 2
     meta = packed[:, model_width:]
@@ -435,17 +423,17 @@
     chosen, factors = tables(meta, beside[:, model_width:])
     some = pieces_of(pick(chosen[2:], packed[:, :width], beside[:, :width]), chips - 2)
     whole = pick(chosen[:2], packed[:, :model_width], beside[:, :model_width])
+    far_1 = swap(stage(mine_1, some)[0], half)
     some = [swap(piece, 2 * q) for q, piece in enumerate(some, 2)]
     whole_near = swap(whole[group:], 2)
-    some, whole_0, whole_near, far_0, mine_1 = stage(some, whole[:group], whole_near, far_0, mine_1)
+    some, whole_0, whole_near, far_0, far_1 = stage(some, whole[:group], whole_near, far_0, far_1)
 
     some = jnp.concatenate(some, axis=0)
     some_other = cross(some)
-    far_1 = swap(mine_1, half)
     beside_0 = swap(far_0, 1)
-    far_chosen, _ = tables(far_0[:, part:], beside_0[:, part:])
+    far_chosen, far_factors = tables(far_0[:, part:], beside_0[:, part:])
     rows_0 = spread(pieces_of(pick(far_chosen, far_0[:, :part], beside_0[:, :part]), chips))
-    some, rows_0, far_1 = stage(some, rows_0, far_1)
+    some, rows_0 = stage(some, rows_0)
 
     rows_0 = jnp.concatenate(rows_0, axis=0)
     other_0 = cross(rows_0)
@@ -454,7 +442,8 @@
     all_rows = chips * group
     (near,) = mlp(
         place, [[(whole, (0, 1, 2, 3))], [(some, (0, 1)), (some_other, (2, 3))]],
-        (0, 1, 2, 3), (), *weights, [(0, all_rows, (0, 1, 2, 3))],
+        (0, 1, 2, 3), (), *weights, [(0, all_rows, 0, model_width)],
+        [(k * part, part) for k in range(4)],
     )
     rows_0, rows_1, near = stage(rows_0, rows_1, near)
 
@@ -462,44 +451,42 @@
     other_1 = cross(rows_1)
     near = pieces_of(near, chips)
     near_back = near[:1] + [swap(near[q], 2 * q) for q in range(1, chips - 1)]
+    near_last = swap(near[-1], 2 * (chips - 1))
     sums = mlp(
-        place, [[(rows_0, (0,)), (rows_1, (1,)), (other_0, (2,))]], (0, 1, 2), (), *weights, ()
-    )
-    other_1, near_back, near_last, sums = stage(other_1, near_back, near[-1], sums)
-
-    side = all_rows // 2
+        place, [[(rows_0, (0,)), (rows_1, (1,)), (other_0, (2,))]], (0, 1, 2), (), *weights, (), ()
+    )
+    other_1, near_back, sums = stage(other_1, near_back, sums)
+
+    lead = min(width - 128, (LEAD * width // 14 + 127) // 128 * 128)
+    columns = [(width, lead), (width + lead, width - lead), (0, lead), (lead, width - lead)]
     outs = mlp(
-        place, [[(other_1, (3,))]], (3,), sums, *weights,
-        [(first, side, (k,)) for k in (2, 0, 1, 3) for first in (0, side)], cap,
-    )
-    (give_0, slant_0, keep_0, core_0, keep_1, core_1, give_1, slant_1), near_last = stage(outs, near_last)
+        place, [[(other_1, (3,))]], (3,), sums, *weights, [(0, all_rows, *c) for c in columns], columns
+    )
+    (give_0, give_1, keep_0, keep_1), near_back = stage(outs, near_back)
     got_0 = cross(give_0)
-    slant_0 = slant(slant_0)
-    core_0 = swap(core_0, 1)
-    near_last = swap(near_last, 2 * (chips - 1))
     got_1 = cross(give_1)
-    slant_1 = slant(slant_1)
-    got_0, slant_0, core_0, near_last, core_1, near_back = stage(
-        got_0, slant_0, core_0, near_last, core_1, near_back
-    )
-
-    core_1 = swap(core_1, 1)
-    back_0 = spread(join(cap, chips, 0, keep_0, got_0, core_0, slant_0))
+    got_0, near_last, near_back = stage(got_0, near_last, near_back)
+
+    back_0 = spread(pieces_of((keep_0.astype(F32) + got_0.astype(F32)).astype(BF16), chips))
     near_sum = mix(factors, jnp.concatenate(near_back + [near_last], axis=0))
-    got_1, slant_1, core_1, back_0, near_sum = stage(got_1, slant_1, core_1, back_0, near_sum)
-
-    far_factors = both_factors(far_0[:, part:])
-    far_0 = swap(mix(far_factors, jnp.concatenate(back_0, axis=0)).astype(BF16), half)
-    back_1 = spread(join(cap, chips, 0, keep_1, got_1, core_1, slant_1))
+    far_0, far_0_core = core_sum(mix(far_factors, jnp.concatenate(back_0, axis=0)))
+    got_1, far_0, far_0_core, near_sum = stage(got_1, far_0, far_0_core, near_sum)
+
+    far_0 = swap((far_0 + far_0_core.astype(F32)).astype(BF16), half)
+    back_1 = spread(pieces_of((keep_1.astype(F32) + got_1.astype(F32)).astype(BF16), chips))
     near_sum, near_core = core_sum(near_sum)
-    near_sum, near_core, far_0, back_1 = stage(near_sum, near_core, far_0, back_1)
-
-    far_1 = swap(mix(far_factors, jnp.concatenate(back_1, axis=0)).astype(BF16), half)
+    far_1, far_1_core = core_sum(mix(far_factors, jnp.concatenate(back_1, axis=0)))
+    near_sum, near_core, far_0, far_1, far_1_core = stage(near_sum, near_core, far_0, far_1, far_1_core)
+
+    far_1 = (far_1 + far_1_core.astype(F32)).astype(BF16)
+    far_1 = swap(far_1, half)
     near_sum = near_sum + near_core.astype(F32)
     near_got = cross(near_sum[:, width:].astype(BF16))
-    far_sum = jnp.concatenate([far_0, far_1], axis=1).astype(F32)
     residual = lax.dynamic_slice_in_dim(tokens, section * width, width, 1)
-    return (residual.astype(F32) + near_sum[:, :width] + near_got.astype(F32) + far_sum).astype(BF16)
+    near_sum = residual.astype(F32) + near_sum[:, :width] + near_got.astype(F32)
+    first = (near_sum[:, :lead] + far_0.astype(F32)).astype(BF16)
+    first, rest = stage(first, near_sum[:, lead:])
+    return jnp.concatenate([first, (rest + far_1.astype(F32)).astype(BF16)], axis=1)
 
 
 def solution(mesh):

time: 143 us -> 138 us (0.965)
  starting transfers between devices: 39.1 us -> 36 us
  waiting for transfers between devices: 73 us -> 70.2 us
  local copies, waits for them, and re-layouts: 0.84 us -> 2.37 us
    ppermute x28, starting transfers between devices: 31.4 us -> 26.8 us  [swap(): lax.ppermute(value, 'expert', [(i, i ^ mask) for i in range(experts)])]
    ppermute x2 -> x0, waiting for transfers between devices: 2.37 us -> none  [slant(): return lax.ppermute(value, ('section', 'expert'), pairs)]
    ppermute x6, starting transfers between devices: 7.62 us -> 9.21 us  [cross(): return lax.ppermute(value, 'section', [(0, 1), (1, 0)])]
  transfers between devices with their start and end apart: 36 -> 34, of which waited for: 21 -> 19; matrix products, arithmetic and copies ran while one was open for 6% -> 8% of each run, Pallas kernels for 8% -> 8%
where the time goes in v3:
time: 138 us
  waiting for transfers between devices  70.2 us (51%)
  starting transfers between devices  36 us (26%)
  Pallas kernels  17.7 us (13%)
  matrix products  6.89 us (5%)
  other arithmetic  4.08 us (3%)
  local copies, waits for them, and re-layouts  2.37 us (2%)
    ppermute x28, waiting for transfers between devices, swap(): lax.ppermute(value, 'expert', [(i, i ^ mask) for i in range(experts)])  52.3 us
    ppermute x28, starting transfers between devices, swap(): lax.ppermute(value, 'expert', [(i, i ^ mask) for i in range(experts)])  26.8 us
    ppermute x6, waiting for transfers between devices, cross(): return lax.ppermute(value, 'section', [(0, 1), (1, 0)])  17.9 us
    pallas_call x3, Pallas kernels, mlp(): pl.pallas_call(functools.partial(mlp_body, plan, steps, bool(before), out...  14.5 us
    ppermute x6, starting transfers between devices, cross(): return lax.ppermute(value, 'section', [(0, 1), (1, 0)])  9.21 us
    pallas_call x1, Pallas kernels, prepare(): pl.pallas_call(functools.partial(prepare_body, experts), out_shape=[jax.S...  3.18 us
  transfers between devices with their start and end apart: 34, of which 19 were waited for; matrix products, arithmetic and copies ran while one was open for 8% of the time, Pallas kernels for 8%

profile of v3, /device:TPU:0, one launch (start us, length us, event | category | flops | bytes accessed | tf_op | source)
XLA Modules:
  0.0 137.8 jit_solution(2093547231931778774)
XLA Ops:
  0.0 3.2 %prepare.1 = (bf16[128,3712]{1,0:T(8,128)(2,1)}, bf16[128,1024]{1,0:T(8,128)(2,1)}, bf16[128,896]{1,0:T(8,128)(2,1)}) custom-call(s32[1]{0:T(128)} %bitcast.place, bf16[128,3584]{1,0:T(8,128)(2,1)} %refs_0_.1, bf16[3584]{0:T(1024)(128)(2,1)} %refs_1_.2, bf16[16,3584]{1,0:T(8,128)(2,1)} %bitcast.26, s32[3,128]{1,0:T(4,128)} %bitcast.27), custom_call_target="tpu_custom_call" | custom-call | tf_op jit(solution)/shard_map/prepare/pallas_call | solution.py:184
  3.2 4.1 %collective-permute-start.4 = (bf16[128,1024]{1,0:T(8,128)(2,1)}, bf16[128,1024]{1,0:T(8,128)(2,1)S(1)}, u32[]{:S(2)}, u32[]{:S(2)}) collective-permute-start(bf16[128,1024]{1,0:T(8,128)(2,1)} %get-tuple-element.62), channel_id=1, source_target_pairs={{0,8},{1,9},{2,10},{3,11},{4,12},{5,13},{6,14},{7,15},{8,0},{9,1},... | collective-permute-start | bytes 786440 | tf_op jit(solution)/shard_map/ppermute | solution.py:366
  16.6 3.1 %collective-permute-done.4 = bf16[128,1024]{1,0:T(8,128)(2,1)S(1)} collective-permute-done((bf16[128,1024]{1,0:T(8,128)(2,1)}, bf16[128,1024]{1,0:T(8,128)(2,1)S(1)}, u32[]{:S(2)}, u32[]{:S(2)}) %collective-permute-start.4) | collective-permute-done | bytes 262176 | tf_op jit(solution)/shard_map/ppermute | solution.py:366
  19.7 12.4 %collective-permute-done.5 = bf16[128,896]{1,0:T(8,128)(2,1)S(1)} collective-permute-done((bf16[128,896]{1,0:T(8,128)(2,1)S(1)}, bf16[128,896]{1,0:T(8,128)(2,1)S(1)}, u32[]{:S(2)}, u32[]{:S(2)}) %collective-permute-start.5) | collective-permute-done | bytes 229408 | tf_op jit(solution)/shard_map/ppermute | solution.py:366
  32.0 3.4 %collective-permute-done.1 = bf16[72,1792]{1,0:T(8,128)(2,1)S(1)} collective-permute-done((bf16[72,1792]{1,0:T(8,128)(2,1)S(1)}, bf16[72,1792]{1,0:T(8,128)(2,1)S(1)}, u32[]{:S(2)}, u32[]{:S(2)}) %collective-permute-start.1) | collective-permute-done | bytes 258080 | tf_op jit(solution)/shard_map/ppermute | solution.py:366
  39.3 2.5 %collective-permute-start.8 = (bf16[72,896]{1,0:T(8,128)(2,1)S(1)}, bf16[72,896]{1,0:T(8,128)(2,1)S(1)}, u32[]{:S(2)}, u32[]{:S(2)}) collective-permute-start(bf16[72,896]{1,0:T(8,128)(2,1)S(1)} %get-tuple-element.136), channel_id=1, source_target_pairs={{0,4},{1,5},{2,6},{3,7},{4,0},{5,1},{6,2},{7,3},{8,12},{9,13},{10,... | collective-permute-start | bytes 387080 | tf_op jit(solution)/shard_map/ppermute | solution.py:366
  44.0 2.1 %collective-permute-done.9 = bf16[72,896]{1,0:T(8,128)(2,1)S(1)} collective-permute-done((bf16[72,896]{1,0:T(8,128)(2,1)S(1)}, bf16[72,896]{1,0:T(8,128)(2,1)S(1)}, u32[]{:S(2)}, u32[]{:S(2)}) %collective-permute-start.9) | collective-permute-done | bytes 129056 | tf_op jit(solution)/shard_map/ppermute | solution.py:366
  46.1 2.8 %collective-permute-done.8 = bf16[72,896]{1,0:T(8,128)(2,1)S(1)} collective-permute-done((bf16[72,896]{1,0:T(8,128)(2,1)S(1)}, bf16[72,896]{1,0:T(8,128)(2,1)S(1)}, u32[]{:S(2)}, u32[]{:S(2)}) %collective-permute-start.8) | collective-permute-done | bytes 129056 | tf_op jit(solution)/shard_map/ppermute | solution.py:366
  50.5 7.0 %mlp.3 = bf16[288,3584]{1,0:T(8,128)(2,1)S(1)} custom-call(s32[1]{0:T(128)} %bitcast.place, bf16[144,3584]{1,0:T(8,128)(2,1)S(1)} %pad_maximum_fusion.refs_0_, bf16[144,1792]{1,0:T(8,128)(2,1)S(1)} %constant_dynamic-update-slice_fusion.refs_1_, bf16[144,1792]{1,0:T(8,128)(2,1)S(1)} %collective-permute-done.14.refs_2_, bf16[1,3584,512]{2,1,0:T(8,128)(2,1)S(1)} %copy-done, ...), custom_call_target="tpu_custom_call" | custom-call | flops 3170893824 | bytes 11010048 | tf_op jit(solution)/shard_map/mlp/pallas_call | solution.py:299
  60.9 2.7 %collective-permute-done.18.refs_2_ = bf16[288,896]{1,0:T(8,128)(2,1)S(1)} collective-permute-done((bf16[288,896]{1,0:T(8,128)(2,1)S(1)}, bf16[288,896]{1,0:T(8,128)(2,1)S(1)}, u32[]{:S(2)}, u32[]{:S(2)}) %collective-permute-start.18) | collective-permute-done | bytes 516128 | tf_op jit(solution)/shard_map/ppermute | solution.py:369
  63.6 3.6 %mlp.4 = (f32[288,512]{1,0:T(8,128)S(1)}, f32[288,512]{1,0:T(8,128)S(1)}) custom-call(s32[1]{0:T(128)} %bitcast.place, bf16[288,896]{1,0:T(8,128)(2,1)S(1)} %constant_dynamic-update-slice_fusion.2.refs_0_, bf16[288,896]{1,0:T(8,128)(2,1)S(1)} %constant_dynamic-update-slice_fusion.6.refs_1_, bf16[288,896]{1,0:T(8,128)(2,1)S(1)} %collective-permute-done.18.refs_2_, ...), custom_call_target="tpu_custom_call" | custom-call | flops 1585446912 | bytes 5505024 | tf_op jit(solution)/shard_map/mlp/pallas_call | solution.py:299
  67.3 5.1 %collective-permute-done.15.refs_0_ = bf16[288,896]{1,0:T(8,128)(2,1)S(1)} collective-permute-done((bf16[288,896]{1,0:T(8,128)(2,1)S(1)}, bf16[288,896]{1,0:T(8,128)(2,1)S(1)}, u32[]{:S(2)}, u32[]{:S(2)}) %collective-permute-start.15) | collective-permute-done | bytes 516128 | tf_op jit(solution)/shard_map/ppermute | solution.py:369
  72.4 3.9 %mlp.5 = (bf16[288,1152]{1,0:T(8,128)(2,1)S(1)}, bf16[288,640]{1,0:T(8,128)(2,1)S(1)}, bf16[288,1152]{1,0:T(8,128)(2,1)S(1)}, bf16[288,640]{1,0:T(8,128)(2,1)S(1)}) custom-call(s32[1]{0:T(128)} %bitcast.place, bf16[288,896]{1,0:T(8,128)(2,1)S(1)} %collective-permute-done.15.refs_0_, bf16[1,3584,512]{2,1,0:T(8,128)(2,1)S(1)} %copy-done, ...), custom_call_target="tpu_custom_call" | custom-call | flops 1585446912 | bytes 5505024 | tf_op jit(solution)/shard_map/mlp/pallas_call | solution.py:299
  76.3 1.8 %collective-permute-start.20 = (bf16[288,1152]{1,0:T(8,128)(2,1)S(1)}, bf16[288,1152]{1,0:T(8,128)(2,1)S(1)}, u32[]{:S(2)}, u32[]{:S(2)}) collective-permute-start(bf16[288,1152]{1,0:T(8,128)(2,1)S(1)} %get-tuple-element.96), channel_id=1, source_target_pairs={{0,16},{16,0},{1,17},{17,1},{2,18},{18,2},{3,19},{19,3},{4,20},{20... | collective-permute-start | bytes 1990664 | tf_op jit(solution)/shard_map/ppermute | solution.py:369
  79.1 11.3 %collective-permute-done.21 = bf16[72,3584]{1,0:T(8,128)(2,1)S(1)} collective-permute-done((bf16[72,3584]{1,0:T(8,128)(2,1)S(1)}, bf16[72,3584]{1,0:T(8,128)(2,1)S(1)}, u32[]{:S(2)}, u32[]{:S(2)}) %collective-permute-start.21) | collective-permute-done | bytes 516128 | tf_op jit(solution)/shard_map/ppermute | solution.py:366
  92.5 2.8 %collective-permute-start.23 = (bf16[72,1152]{1,0:T(8,128)(2,1)S(1)}, bf16[72,1152]{1,0:T(8,128)(2,1)S(1)}, u32[]{:S(2)}, u32[]{:S(2)}) collective-permute-start(bf16[72,1152]{1,0:T(8,128)(2,1)S(1)} %get-tuple-element.129), channel_id=1, source_target_pairs={{0,4},{1,5},{2,6},{3,7},{4,0},{5,1},{6,2},{7,3},{8,12},{9,13},{10,... | collective-permute-start | bytes 497672 | tf_op jit(solution)/shard_map/ppermute | solution.py:366
  95.4 1.8 %collective-permute-start.19 = (bf16[288,640]{1,0:T(8,128)(2,1)S(1)}, bf16[288,640]{1,0:T(8,128)(2,1)S(1)}, u32[]{:S(2)}, u32[]{:S(2)}) collective-permute-start(bf16[288,640]{1,0:T(8,128)(2,1)S(1)} %get-tuple-element.94), channel_id=1, source_target_pairs={{0,16},{16,0},{1,17},{17,1},{2,18},{18,2},{3,19},{19,3},{4,20},{20... | collective-permute-start | bytes 1105928 | tf_op jit(solution)/shard_map/ppermute | solution.py:369
  97.8 2.6 %collective-permute-done.23 = bf16[72,1152]{1,0:T(8,128)(2,1)S(1)} collective-permute-done((bf16[72,1152]{1,0:T(8,128)(2,1)S(1)}, bf16[72,1152]{1,0:T(8,128)(2,1)S(1)}, u32[]{:S(2)}, u32[]{:S(2)}) %collective-permute-start.23) | collective-permute-done | bytes 165920 | tf_op jit(solution)/shard_map/ppermute | solution.py:366
  104.8 2.0 %collective-permute-start.29 = (bf16[72,640]{1,0:T(8,128)(2,1)S(1)}, bf16[72,640]{1,0:T(8,128)(2,1)S(1)}, u32[]{:S(2)}, u32[]{:S(2)}) collective-permute-start(bf16[72,640]{1,0:T(8,128)(2,1)S(1)} %get-tuple-element.143), channel_id=1, source_target_pairs={{0,4},{1,5},{2,6},{3,7},{4,0},{5,1},{6,2},{7,3},{8,12},{9,13},{10,... | collective-permute-start | bytes 276488 | tf_op jit(solution)/shard_map/ppermute | solution.py:366
  106.9 2.6 %collective-permute-start.27 = (bf16[128,1152]{1,0:T(8,128)(2,1)S(1)}, bf16[128,1152]{1,0:T(8,128)(2,1)S(1)}, u32[]{:S(2)}, u32[]{:S(2)}) collective-permute-start(bf16[128,1152]{1,0:T(8,128)(2,1)S(1)} %add_convert_fusion.2), channel_id=1, source_target_pairs={{0,8},{1,9},{2,10},{3,11},{4,12},{5,13},{6,14},{7,15},{8,0},{9,1},... | collective-permute-start | bytes 884744 | tf_op jit(solution)/shard_map/ppermute | solution.py:366
  109.7 5.0 %collective-permute-done.29 = bf16[72,640]{1,0:T(8,128)(2,1)S(1)} collective-permute-done((bf16[72,640]{1,0:T(8,128)(2,1)S(1)}, bf16[72,640]{1,0:T(8,128)(2,1)S(1)}, u32[]{:S(2)}, u32[]{:S(2)}) %collective-permute-start.29) | collective-permute-done | bytes 92192 | tf_op jit(solution)/shard_map/ppermute | solution.py:366
  116.6 6.5 %collective-permute-done.27 = bf16[128,1152]{1,0:T(8,128)(2,1)S(1)} collective-permute-done((bf16[128,1152]{1,0:T(8,128)(2,1)S(1)}, bf16[128,1152]{1,0:T(8,128)(2,1)S(1)}, u32[]{:S(2)}, u32[]{:S(2)}) %collective-permute-start.27) | collective-permute-done | bytes 294944 | tf_op jit(solution)/shard_map/ppermute | solution.py:366
  124.0 1.8 %collective-permute-start.32 = (bf16[128,1792]{1,0:T(8,128)(2,1)S(1)}, bf16[128,1792]{1,0:T(8,128)(2,1)}, u32[]{:S(2)}, u32[]{:S(2)}) collective-permute-start(bf16[128,1792]{1,0:T(8,128)(2,1)S(1)} %slice.335), channel_id=1, source_target_pairs={{0,16},{16,0},{1,17},{17,1},{2,18},{18,2},{3,19},{19,3},{4,20},{20... | collective-permute-start | bytes 1376264 | tf_op jit(solution)/shard_map/ppermute | solution.py:369
  126.9 8.8 %collective-permute-done.32 = bf16[128,1792]{1,0:T(8,128)(2,1)} collective-permute-done((bf16[128,1792]{1,0:T(8,128)(2,1)S(1)}, bf16[128,1792]{1,0:T(8,128)(2,1)}, u32[]{:S(2)}, u32[]{:S(2)}) %collective-permute-start.32) | collective-permute-done | bytes 458784 | tf_op jit(solution)/shard_map/ppermute | solution.py:369
  (138 shorter events, 34.4 us)
Async XLA Ops:
  3.2 16.5 %collective-permute-start.4 = (bf16[128,1024]{1,0:T(8,128)(2,1)}, bf16[128,1024]{1,0:T(8,128)(2,1)S(1)}, u32[]{:S(2)}, u32[]{:S(2)}) collective-permute-start(bf16[128,1024]{1,0:T(8,128)(2,1)} %get-tuple-element.62), channel_id=1, source_target_pairs={{0,8},{1,9},{2,10},{3,11},{4,12},{5,13},{6,14},{7,15},{8,0},{9,1},... | collective-permute-start | bytes 786440 | tf_op jit(solution)/shard_map/ppermute | solution.py:366
  12.5 22.9 %collective-permute-start.3 = (bf16[72,3584]{1,0:T(8,128)(2,1)S(1)}, bf16[72,3584]{1,0:T(8,128)(2,1)S(1)}, u32[]{:S(2)}, u32[]{:S(2)}) collective-permute-start(bf16[72,3584]{1,0:T(8,128)(2,1)S(1)} %get-tuple-element.125), channel_id=1, source_target_pairs={{0,2},{1,3},{2,0},{3,1},{4,6},{5,7},{6,4},{7,5},{8,10},{9,11},{10,... | collective-permute-start | bytes 1548296 | tf_op jit(solution)/shard_map/ppermute | solution.py:366
  14.4 17.6 %collective-permute-start.2 = (bf16[72,1792]{1,0:T(8,128)(2,1)S(1)}, bf16[72,1792]{1,0:T(8,128)(2,1)S(1)}, u32[]{:S(2)}, u32[]{:S(2)}) collective-permute-start(bf16[72,1792]{1,0:T(8,128)(2,1)S(1)} %get-tuple-element.139), channel_id=1, source_target_pairs={{0,6},{1,7},{2,4},{3,5},{4,2},{5,3},{6,0},{7,1},{8,14},{9,15},{10,... | collective-permute-start | bytes 774152 | tf_op jit(solution)/shard_map/ppermute | solution.py:366
  16.0 19.4 %collective-permute-start.1 = (bf16[72,1792]{1,0:T(8,128)(2,1)S(1)}, bf16[72,1792]{1,0:T(8,128)(2,1)S(1)}, u32[]{:S(2)}, u32[]{:S(2)}) collective-permute-start(bf16[72,1792]{1,0:T(8,128)(2,1)S(1)} %get-tuple-element.140), channel_id=1, source_target_pairs={{0,4},{1,5},{2,6},{3,7},{4,0},{5,1},{6,2},{7,3},{8,12},{9,13},{10,... | collective-permute-start | bytes 774152 | tf_op jit(solution)/shard_map/ppermute | solution.py:366
  16.5 15.5 %collective-permute-start.5 = (bf16[128,896]{1,0:T(8,128)(2,1)S(1)}, bf16[128,896]{1,0:T(8,128)(2,1)S(1)}, u32[]{:S(2)}, u32[]{:S(2)}) collective-permute-start(bf16[128,896]{1,0:T(8,128)(2,1)S(1)} %copy-done.10), channel_id=1, source_target_pairs={{0,8},{1,9},{2,10},{3,11},{4,12},{5,13},{6,14},{7,15},{8,0},{9,1},... | collective-permute-start | bytes 688136 | tf_op jit(solution)/shard_map/ppermute | solution.py:366
  36.1 14.4 %collective-permute-start.14 = (bf16[144,1792]{1,0:T(8,128)(2,1)S(1)}, bf16[144,1792]{1,0:T(8,128)(2,1)S(1)}, u32[]{:S(2)}, u32[]{:S(2)}) collective-permute-start(bf16[144,1792]{1,0:T(8,128)(2,1)S(1)} %constant_dynamic-update-slice_fusion.refs_1_), channel_id=1, source_target_pairs={{0,16},{16,0},{1,17},{17,1},{2,18},{18,2},{3,19},{19,3},{4,20},{20... | collective-permute-start | bytes 1548296 | tf_op jit(solution)/shard_map/ppermute | solution.py:369
  39.3 9.6 %collective-permute-start.8 = (bf16[72,896]{1,0:T(8,128)(2,1)S(1)}, bf16[72,896]{1,0:T(8,128)(2,1)S(1)}, u32[]{:S(2)}, u32[]{:S(2)}) collective-permute-start(bf16[72,896]{1,0:T(8,128)(2,1)S(1)} %get-tuple-element.136), channel_id=1, source_target_pairs={{0,4},{1,5},{2,6},{3,7},{4,0},{5,1},{6,2},{7,3},{8,12},{9,13},{10,... | collective-permute-start | bytes 387080 | tf_op jit(solution)/shard_map/ppermute | solution.py:366
  41.8 7.6 %collective-permute-start.7 = (bf16[72,896]{1,0:T(8,128)(2,1)S(1)}, bf16[72,896]{1,0:T(8,128)(2,1)S(1)}, u32[]{:S(2)}, u32[]{:S(2)}) collective-permute-start(bf16[72,896]{1,0:T(8,128)(2,1)S(1)} %get-tuple-element.137), channel_id=1, source_target_pairs={{0,2},{1,3},{2,0},{3,1},{4,6},{5,7},{6,4},{7,5},{8,10},{9,11},{10,... | collective-permute-start | bytes 387080 | tf_op jit(solution)/shard_map/ppermute | solution.py:366
  43.0 14.5 %collective-permute-start.13 = (bf16[72,896]{1,0:T(8,128)(2,1)S(1)}, bf16[72,896]{1,0:T(8,128)(2,1)S(1)}, u32[]{:S(2)}, u32[]{:S(2)}) collective-permute-start(bf16[72,896]{1,0:T(8,128)(2,1)S(1)} %get-tuple-element.131), channel_id=1, source_target_pairs={{0,6},{1,7},{2,4},{3,5},{4,2},{5,3},{6,0},{7,1},{8,14},{9,15},{10,... | collective-permute-start | bytes 387080 | tf_op jit(solution)/shard_map/ppermute | solution.py:366
  46.1 11.4 %collective-permute-start.12 = (bf16[72,896]{1,0:T(8,128)(2,1)S(1)}, bf16[72,896]{1,0:T(8,128)(2,1)S(1)}, u32[]{:S(2)}, u32[]{:S(2)}) collective-permute-start(bf16[72,896]{1,0:T(8,128)(2,1)S(1)} %get-tuple-element.132), channel_id=1, source_target_pairs={{0,4},{1,5},{2,6},{3,7},{4,0},{5,1},{6,2},{7,3},{8,12},{9,13},{10,... | collective-permute-start | bytes 387080 | tf_op jit(solution)/shard_map/ppermute | solution.py:366
  48.9 8.6 %collective-permute-start.11 = (bf16[72,896]{1,0:T(8,128)(2,1)S(1)}, bf16[72,896]{1,0:T(8,128)(2,1)S(1)}, u32[]{:S(2)}, u32[]{:S(2)}) collective-permute-start(bf16[72,896]{1,0:T(8,128)(2,1)S(1)} %get-tuple-element.133), channel_id=1, source_target_pairs={{0,2},{1,3},{2,0},{3,1},{4,6},{5,7},{6,4},{7,5},{8,10},{9,11},{10,... | collective-permute-start | bytes 387080 | tf_op jit(solution)/shard_map/ppermute | solution.py:366
  49.5 14.1 %collective-permute-start.18 = (bf16[288,896]{1,0:T(8,128)(2,1)S(1)}, bf16[288,896]{1,0:T(8,128)(2,1)S(1)}, u32[]{:S(2)}, u32[]{:S(2)}) collective-permute-start(bf16[288,896]{1,0:T(8,128)(2,1)S(1)} %constant_dynamic-update-slice_fusion.2.refs_0_), channel_id=1, source_target_pairs={{0,16},{16,0},{1,17},{17,1},{2,18},{18,2},{3,19},{19,3},{4,20},{20... | collective-permute-start | bytes 1548296 | tf_op jit(solution)/shard_map/ppermute | solution.py:369
  57.6 14.7 %collective-permute-start.15 = (bf16[288,896]{1,0:T(8,128)(2,1)S(1)}, bf16[288,896]{1,0:T(8,128)(2,1)S(1)}, u32[]{:S(2)}, u32[]{:S(2)}) collective-permute-start(bf16[288,896]{1,0:T(8,128)(2,1)S(1)} %constant_dynamic-update-slice_fusion.6.refs_1_), channel_id=1, source_target_pairs={{0,16},{16,0},{1,17},{17,1},{2,18},{18,2},{3,19},{19,3},{4,20},{20... | collective-permute-start | bytes 1548296 | tf_op jit(solution)/shard_map/ppermute | solution.py:369
  59.0 13.4 %collective-permute-start.17 = (bf16[72,3584]{1,0:T(8,128)(2,1)S(1)}, bf16[72,3584]{1,0:T(8,128)(2,1)S(1)}, u32[]{:S(2)}, u32[]{:S(2)}) collective-permute-start(bf16[72,3584]{1,0:T(8,128)(2,1)S(1)} %get-tuple-element.122), channel_id=1, source_target_pairs={{0,4},{1,5},{2,6},{3,7},{4,0},{5,1},{6,2},{7,3},{8,12},{9,13},{10,... | collective-permute-start | bytes 1548296 | tf_op jit(solution)/shard_map/ppermute | solution.py:366
  59.2 13.1 %collective-permute-start.16 = (bf16[72,3584]{1,0:T(8,128)(2,1)S(1)}, bf16[72,3584]{1,0:T(8,128)(2,1)S(1)}, u32[]{:S(2)}, u32[]{:S(2)}) collective-permute-start(bf16[72,3584]{1,0:T(8,128)(2,1)S(1)} %get-tuple-element.123), channel_id=1, source_target_pairs={{0,2},{1,3},{2,0},{3,1},{4,6},{5,7},{6,4},{7,5},{8,10},{9,11},{10,... | collective-permute-start | bytes 1548296 | tf_op jit(solution)/shard_map/ppermute | solution.py:366
  76.3 14.9 %collective-permute-start.20 = (bf16[288,1152]{1,0:T(8,128)(2,1)S(1)}, bf16[288,1152]{1,0:T(8,128)(2,1)S(1)}, u32[]{:S(2)}, u32[]{:S(2)}) collective-permute-start(bf16[288,1152]{1,0:T(8,128)(2,1)S(1)} %get-tuple-element.96), channel_id=1, source_target_pairs={{0,16},{16,0},{1,17},{17,1},{2,18},{18,2},{3,19},{19,3},{4,20},{20... | collective-permute-start | bytes 1990664 | tf_op jit(solution)/shard_map/ppermute | solution.py:369
  78.1 12.2 %collective-permute-start.21 = (bf16[72,3584]{1,0:T(8,128)(2,1)S(1)}, bf16[72,3584]{1,0:T(8,128)(2,1)S(1)}, u32[]{:S(2)}, u32[]{:S(2)}) collective-permute-start(bf16[72,3584]{1,0:T(8,128)(2,1)S(1)} %get-tuple-element.121), channel_id=1, source_target_pairs={{0,6},{1,7},{2,4},{3,5},{4,2},{5,3},{6,0},{7,1},{8,14},{9,15},{10,... | collective-permute-start | bytes 1548296 | tf_op jit(solution)/shard_map/ppermute | solution.py:366
  92.5 7.9 %collective-permute-start.23 = (bf16[72,1152]{1,0:T(8,128)(2,1)S(1)}, bf16[72,1152]{1,0:T(8,128)(2,1)S(1)}, u32[]{:S(2)}, u32[]{:S(2)}) collective-permute-start(bf16[72,1152]{1,0:T(8,128)(2,1)S(1)} %get-tuple-element.129), channel_id=1, source_target_pairs={{0,4},{1,5},{2,6},{3,7},{4,0},{5,1},{6,2},{7,3},{8,12},{9,13},{10,... | collective-permute-start | bytes 497672 | tf_op jit(solution)/shard_map/ppermute | solution.py:366
  103.0 20.7 %collective-permute-start.26 = (bf16[128,3584]{1,0:T(8,128)(2,1)S(1)}, bf16[128,3584]{1,0:T(8,128)(2,1)S(1)}, u32[]{:S(2)}, u32[]{:S(2)}) collective-permute-start(bf16[128,3584]{1,0:T(8,128)(2,1)S(1)} %slice.334), channel_id=1, source_target_pairs={{0,1},{1,0},{2,3},{3,2},{4,5},{5,4},{6,7},{7,6},{8,9},{9,8},{10,11... | collective-permute-start | bytes 2752520 | tf_op jit(solution)/shard_map/ppermute | solution.py:366
  104.8 9.9 %collective-permute-start.29 = (bf16[72,640]{1,0:T(8,128)(2,1)S(1)}, bf16[72,640]{1,0:T(8,128)(2,1)S(1)}, u32[]{:S(2)}, u32[]{:S(2)}) collective-permute-start(bf16[72,640]{1,0:T(8,128)(2,1)S(1)} %get-tuple-element.143), channel_id=1, source_target_pairs={{0,4},{1,5},{2,6},{3,7},{4,0},{5,1},{6,2},{7,3},{8,12},{9,13},{10,... | collective-permute-start | bytes 276488 | tf_op jit(solution)/shard_map/ppermute | solution.py:366
  106.8 7.9 %collective-permute-start.28 = (bf16[72,640]{1,0:T(8,128)(2,1)S(1)}, bf16[72,640]{1,0:T(8,128)(2,1)S(1)}, u32[]{:S(2)}, u32[]{:S(2)}) collective-permute-start(bf16[72,640]{1,0:T(8,128)(2,1)S(1)} %get-tuple-element.144), channel_id=1, source_target_pairs={{0,2},{1,3},{2,0},{3,1},{4,6},{5,7},{6,4},{7,5},{8,10},{9,11},{10,... | collective-permute-start | bytes 276488 | tf_op jit(solution)/shard_map/ppermute | solution.py:366
  106.9 16.1 %collective-permute-start.27 = (bf16[128,1152]{1,0:T(8,128)(2,1)S(1)}, bf16[128,1152]{1,0:T(8,128)(2,1)S(1)}, u32[]{:S(2)}, u32[]{:S(2)}) collective-permute-start(bf16[128,1152]{1,0:T(8,128)(2,1)S(1)} %add_convert_fusion.2), channel_id=1, source_target_pairs={{0,8},{1,9},{2,10},{3,11},{4,12},{5,13},{6,14},{7,15},{8,0},{9,1},... | collective-permute-start | bytes 884744 | tf_op jit(solution)/shard_map/ppermute | solution.py:366
  124.0 11.7 %collective-permute-start.32 = (bf16[128,1792]{1,0:T(8,128)(2,1)S(1)}, bf16[128,1792]{1,0:T(8,128)(2,1)}, u32[]{:S(2)}, u32[]{:S(2)}) collective-permute-start(bf16[128,1792]{1,0:T(8,128)(2,1)S(1)} %slice.335), channel_id=1, source_target_pairs={{0,16},{16,0},{1,17},{17,1},{2,18},{18,2},{3,19},{19,3},{4,20},{20... | collective-permute-start | bytes 1376264 | tf_op jit(solution)/shard_map/ppermute | solution.py:369
  126.8 10.1 %collective-permute-start.33 = (bf16[128,640]{1,0:T(8,128)(2,1)S(1)}, bf16[128,640]{1,0:T(8,128)(2,1)S(1)}, u32[]{:S(2)}, u32[]{:S(2)}) collective-permute-start(bf16[128,640]{1,0:T(8,128)(2,1)S(1)} %add_convert_fusion.4), channel_id=1, source_target_pairs={{0,8},{1,9},{2,10},{3,11},{4,12},{5,13},{6,14},{7,15},{8,0},{9,1},... | collective-permute-start | bytes 491528 | tf_op jit(solution)/shard_map/ppermute | solution.py:366
  (23 other events, 140.4 us)

commit v4 on v3

--- a/solution.py
+++ b/solution.py
@@ -196,7 +196,7 @@
     )(place, *arrays)
 
 
-def mlp_body(plan, steps, carried, outs, columns, cap, place, *refs):
+def mlp_body(plan, steps, carried, outs, columns, hand, place, *refs):
     count = 1 + max(piece for _, where in plan for piece, _ in where.values())
     pieces, (w_gate, w_up, w_down) = refs[:count], refs[count : count + 3]
     refs = refs[count + 3 :]
@@ -254,17 +254,8 @@
             first += gate.shape[0]
         return
     hidden = [(g / (1.0 + jnp.exp(-g)) * u).astype(BF16) for g, u in zip(gates, ups)]
-    if cap:
-        rows = plan[0][0]
-        to = lax.broadcasted_iota(jnp.int32, (rows, rows), 0)
-        of = lax.broadcasted_iota(jnp.int32, (rows, rows), 1)
-        spot = to % (rows // 2)
-        moved = spot // cap * 2 * cap + to // (rows // 2) * cap + spot % cap == of
-        hidden = [
-            jnp.dot(
-                moved.astype(F32).astype(BF16), hidden[0], preferred_element_type=F32
-            ).astype(BF16)
-        ]
+    if hand:
+        results[-1][...] = hidden[0]
     for number, (left, size) in enumerate(columns):
         load_down(number).wait()
         first = 0
@@ -278,7 +269,7 @@
             first += h.shape[0]
 
 
-def mlp(place, blocks, steps, before, w_gate, w_up, w_down, outs, columns, cap=0):
+def mlp(place, blocks, steps, before, w_gate, w_up, w_down, outs, columns, hand=False):
     _, model_width, hidden_width = w_gate.shape
     total = 4
     step = model_width // total
@@ -294,10 +285,11 @@
     vmem = pl.BlockSpec(memory_space=pltpu.VMEM)
     if outs:
         shapes = [jax.ShapeDtypeStruct((r, c), BF16) for _, r, _, c in outs]
+        shapes += [jax.ShapeDtypeStruct((rows, hidden_width), BF16)] * hand
     else:
         shapes = [jax.ShapeDtypeStruct((rows, hidden_width), F32)] * 2
     return pl.pallas_call(
-        functools.partial(mlp_body, plan, steps, bool(before), outs, columns, cap),
+        functools.partial(mlp_body, plan, steps, bool(before), outs, columns, hand),
         out_shape=shapes,
         in_specs=[pl.BlockSpec(memory_space=pltpu.SMEM)]
         + [vmem] * len(pieces)
@@ -323,31 +315,47 @@
     )(place, *pieces, w_gate, w_up, w_down, *before)
 
 
-def join_body(cap, column, keep, crossed, beside, slanted, *outs):
-    rows, width = keep.shape
-    first = (keep[...].astype(F32) + crossed[...].astype(F32)).astype(BF16)
-    second = beside[:, column : column + width].astype(F32) + slanted[...].astype(F32)
-    second = second.astype(BF16)
-    to = lax.broadcasted_iota(jnp.int32, (2 * cap, rows), 0)
-    of = lax.broadcasted_iota(jnp.int32, (2 * cap, rows), 1)
-    for q, out in enumerate(outs):
-        here = (q * cap + to % cap == of).astype(F32)
-        out[...] = (
-            jnp.dot(jnp.where(to < cap, here, 0.0).astype(BF16), first, preferred_element_type=F32)
-            + jnp.dot(jnp.where(to < cap, 0.0, here).astype(BF16), second, preferred_element_type=F32)
+def down_body(columns, place, hidden, w_down, *refs):
+    outs, (weights, sems) = refs[: len(columns)], refs[len(columns) :]
+    width = w_down.shape[2] // 2
+    copies = []
+    for number, (first, size) in enumerate(columns):
+        moved = jnp.where(place[0] == first // width, 0, width) + first % width
+        copies.append(pltpu.make_async_copy(
+            w_down.at[0, :, pl.ds(pl.multiple_of(moved, 128), size)],
+            weights.at[:, pl.ds(first, size)],
+            sems.at[number],
+        ))
+    for copy in copies:
+        copy.start()
+    for copy, (first, size), out in zip(copies, columns, outs):
+        copy.wait()
+        out[...] = jnp.dot(
+            hidden[...], weights[:, first : first + size], preferred_element_type=F32
         ).astype(BF16)
 
 
-def join(cap, chips, column, keep, crossed, beside, slanted):
+def down(place, hidden, w_down, columns):
+    rows, hidden_width = hidden.shape
     vmem = pl.BlockSpec(memory_space=pltpu.VMEM)
+    count = sum(size for _, size in columns)
     return pl.pallas_call(
-        functools.partial(join_body, cap, column),
-        out_shape=[jax.ShapeDtypeStruct((2 * cap, keep.shape[1]), BF16)] * chips,
-        in_specs=[vmem] * 4,
-        out_specs=[vmem] * chips,
-        compiler_params=pltpu.CompilerParams(vmem_limit_bytes=32 * 1024 * 1024),
-        name="join",
-    )(keep, crossed, beside, slanted)
+        functools.partial(down_body, columns),
+        out_shape=[jax.ShapeDtypeStruct((rows, size), BF16) for _, size in columns],
+        in_specs=[pl.BlockSpec(memory_space=pltpu.SMEM), vmem, pl.BlockSpec(memory_space=pl.ANY)],
+        out_specs=[vmem] * len(columns),
+        scratch_shapes=[
+            pltpu.VMEM((hidden_width, w_down.shape[2]), BF16),
+            pltpu.SemaphoreType.DMA((len(columns),)),
+        ],
+        compiler_params=pltpu.CompilerParams(vmem_limit_bytes=40 * 1024 * 1024),
+        cost_estimate=pl.CostEstimate(
+            flops=2 * rows * count * hidden_width,
+            bytes_accessed=2 * count * hidden_width,
+            transcendentals=0,
+        ),
+        name="down",
+    )(place, hidden, w_down)
 
 
 def two_sections(experts, tokens, norm_gain, router, w_gate, w_up, w_down, expert_ids):
@@ -458,14 +466,16 @@
     other_1, near_back, sums = stage(other_1, near_back, sums)
 
     lead = min(width - 128, (LEAD * width // 14 + 127) // 128 * 128)
-    columns = [(width, lead), (width + lead, width - lead), (0, lead), (lead, width - lead)]
-    outs = mlp(
-        place, [[(other_1, (3,))]], (3,), sums, *weights, [(0, all_rows, *c) for c in columns], columns
-    )
-    (give_0, give_1, keep_0, keep_1), near_back = stage(outs, near_back)
+    columns = [(width + lead, width - lead), (0, lead), (lead, width - lead)]
+    give_0, hidden = mlp(
+        place, [[(other_1, (3,))]], (3,), sums, *weights,
+        [(0, all_rows, width, lead)], [(width, lead)], True,
+    )
+    give_0, hidden, near_back = stage(give_0, hidden, near_back)
     got_0 = cross(give_0)
+    give_1, keep_0, keep_1 = down(place, hidden, w_down, columns)
+    got_0, near_last, near_back, give_1 = stage(got_0, near_last, near_back, give_1)
     got_1 = cross(give_1)
-    got_0, near_last, near_back = stage(got_0, near_last, near_back)
 
     back_0 = spread(pieces_of((keep_0.astype(F32) + got_0.astype(F32)).astype(BF16), chips))
     near_sum = mix(factors, jnp.concatenate(near_back + [near_last], axis=0))

time: 138 us -> 136 us (0.986)
  waiting for transfers between devices: 70.2 us -> 68.3 us
    ppermute x28, waiting for transfers between devices: 52.3 us -> 50.4 us  [swap(): lax.ppermute(value, 'expert', [(i, i ^ mask) for i in range(experts)])]
    pallas_call x0 -> x1, Pallas kernels: none -> 1.98 us  [down(): pl.pallas_call(functools.partial(down_body, columns), out_shape=[jax.Shap...]
    pallas_call x3, Pallas kernels: 14.5 us -> 12.8 us  [mlp(): pl.pallas_call(functools.partial(mlp_body, plan, steps, bool(before), out...]
  transfers between devices with their start and end apart: 34 -> 34, of which waited for: 19 -> 19; matrix products, arithmetic and copies ran while one was open for 8% -> 8% of each run, Pallas kernels for 8% -> 9%
where the time goes in v4:
time: 136 us
  waiting for transfers between devices  68.3 us (50%)
  starting transfers between devices  36 us (26%)
  Pallas kernels  17.9 us (13%)
  matrix products  6.87 us (5%)
  other arithmetic  4.05 us (3%)
  local copies, waits for them, and re-layouts  2.36 us (2%)
    ppermute x28, waiting for transfers between devices, swap(): lax.ppermute(value, 'expert', [(i, i ^ mask) for i in range(experts)])  50.4 us
    ppermute x28, starting transfers between devices, swap(): lax.ppermute(value, 'expert', [(i, i ^ mask) for i in range(experts)])  26.8 us
    ppermute x6, waiting for transfers between devices, cross(): return lax.ppermute(value, 'section', [(0, 1), (1, 0)])  17.9 us
    pallas_call x3, Pallas kernels, mlp(): pl.pallas_call(functools.partial(mlp_body, plan, steps, bool(before), out...  12.8 us
    ppermute x6, starting transfers between devices, cross(): return lax.ppermute(value, 'section', [(0, 1), (1, 0)])  9.21 us
    pallas_call x1, Pallas kernels, prepare(): pl.pallas_call(functools.partial(prepare_body, experts), out_shape=[jax.S...  3.17 us
  transfers between devices with their start and end apart: 34, of which 19 were waited for; matrix products, arithmetic and copies ran while one was open for 8% of the time, Pallas kernels for 9%

profile of v4, /device:TPU:0, one launch (start us, length us, event | category | flops | bytes accessed | tf_op | source)
XLA Modules:
  0.0 136.0 jit_solution(4229794708088906261)
XLA Ops:
  0.0 3.2 %prepare.1 = (bf16[128,3712]{1,0:T(8,128)(2,1)}, bf16[128,1024]{1,0:T(8,128)(2,1)}, bf16[128,896]{1,0:T(8,128)(2,1)}) custom-call(s32[1]{0:T(128)} %bitcast.place, bf16[128,3584]{1,0:T(8,128)(2,1)} %refs_0_.1, bf16[3584]{0:T(1024)(128)(2,1)} %refs_1_.2, bf16[16,3584]{1,0:T(8,128)(2,1)} %bitcast.26, s32[3,128]{1,0:T(4,128)} %bitcast.27), custom_call_target="tpu_custom_call" | custom-call | tf_op jit(solution)/shard_map/prepare/pallas_call | solution.py:184
  3.2 4.1 %collective-permute-start.4 = (bf16[128,1024]{1,0:T(8,128)(2,1)}, bf16[128,1024]{1,0:T(8,128)(2,1)S(1)}, u32[]{:S(2)}, u32[]{:S(2)}) collective-permute-start(bf16[128,1024]{1,0:T(8,128)(2,1)} %get-tuple-element.62), channel_id=1, source_target_pairs={{0,8},{1,9},{2,10},{3,11},{4,12},{5,13},{6,14},{7,15},{8,0},{9,1},... | collective-permute-start | bytes 786440 | tf_op jit(solution)/shard_map/ppermute | solution.py:374
  16.6 3.1 %collective-permute-done.4 = bf16[128,1024]{1,0:T(8,128)(2,1)S(1)} collective-permute-done((bf16[128,1024]{1,0:T(8,128)(2,1)}, bf16[128,1024]{1,0:T(8,128)(2,1)S(1)}, u32[]{:S(2)}, u32[]{:S(2)}) %collective-permute-start.4) | collective-permute-done | bytes 262176 | tf_op jit(solution)/shard_map/ppermute | solution.py:374
  19.6 12.4 %collective-permute-done.5 = bf16[128,896]{1,0:T(8,128)(2,1)S(1)} collective-permute-done((bf16[128,896]{1,0:T(8,128)(2,1)S(1)}, bf16[128,896]{1,0:T(8,128)(2,1)S(1)}, u32[]{:S(2)}, u32[]{:S(2)}) %collective-permute-start.5) | collective-permute-done | bytes 229408 | tf_op jit(solution)/shard_map/ppermute | solution.py:374
  32.0 3.4 %collective-permute-done.1 = bf16[72,1792]{1,0:T(8,128)(2,1)S(1)} collective-permute-done((bf16[72,1792]{1,0:T(8,128)(2,1)S(1)}, bf16[72,1792]{1,0:T(8,128)(2,1)S(1)}, u32[]{:S(2)}, u32[]{:S(2)}) %collective-permute-start.1) | collective-permute-done | bytes 258080 | tf_op jit(solution)/shard_map/ppermute | solution.py:374
  39.3 2.5 %collective-permute-start.8 = (bf16[72,896]{1,0:T(8,128)(2,1)S(1)}, bf16[72,896]{1,0:T(8,128)(2,1)S(1)}, u32[]{:S(2)}, u32[]{:S(2)}) collective-permute-start(bf16[72,896]{1,0:T(8,128)(2,1)S(1)} %get-tuple-element.136), channel_id=1, source_target_pairs={{0,4},{1,5},{2,6},{3,7},{4,0},{5,1},{6,2},{7,3},{8,12},{9,13},{10,... | collective-permute-start | bytes 387080 | tf_op jit(solution)/shard_map/ppermute | solution.py:374
  44.0 2.1 %collective-permute-done.9 = bf16[72,896]{1,0:T(8,128)(2,1)S(1)} collective-permute-done((bf16[72,896]{1,0:T(8,128)(2,1)S(1)}, bf16[72,896]{1,0:T(8,128)(2,1)S(1)}, u32[]{:S(2)}, u32[]{:S(2)}) %collective-permute-start.9) | collective-permute-done | bytes 129056 | tf_op jit(solution)/shard_map/ppermute | solution.py:374
  46.1 2.8 %collective-permute-done.8 = bf16[72,896]{1,0:T(8,128)(2,1)S(1)} collective-permute-done((bf16[72,896]{1,0:T(8,128)(2,1)S(1)}, bf16[72,896]{1,0:T(8,128)(2,1)S(1)}, u32[]{:S(2)}, u32[]{:S(2)}) %collective-permute-start.8) | collective-permute-done | bytes 129056 | tf_op jit(solution)/shard_map/ppermute | solution.py:374
  50.5 7.0 %mlp.3 = bf16[288,3584]{1,0:T(8,128)(2,1)S(1)} custom-call(s32[1]{0:T(128)} %bitcast.place, bf16[144,3584]{1,0:T(8,128)(2,1)S(1)} %pad_maximum_fusion.refs_0_, bf16[144,1792]{1,0:T(8,128)(2,1)S(1)} %constant_dynamic-update-slice_fusion.refs_1_, bf16[144,1792]{1,0:T(8,128)(2,1)S(1)} %collective-permute-done.14.refs_2_, bf16[1,3584,512]{2,1,0:T(8,128)(2,1)S(1)} %copy-done.1, ...), custom_call_target="tpu_custom_call" | custom-call | flops 3170893824 | bytes 11010048 | tf_op jit(solution)/shard_map/mlp/pallas_call | solution.py:291
  60.9 2.7 %collective-permute-done.18.refs_2_ = bf16[288,896]{1,0:T(8,128)(2,1)S(1)} collective-permute-done((bf16[288,896]{1,0:T(8,128)(2,1)S(1)}, bf16[288,896]{1,0:T(8,128)(2,1)S(1)}, u32[]{:S(2)}, u32[]{:S(2)}) %collective-permute-start.18) | collective-permute-done | bytes 516128 | tf_op jit(solution)/shard_map/ppermute | solution.py:377
  63.6 3.6 %mlp.4 = (f32[288,512]{1,0:T(8,128)S(1)}, f32[288,512]{1,0:T(8,128)S(1)}) custom-call(s32[1]{0:T(128)} %bitcast.place, bf16[288,896]{1,0:T(8,128)(2,1)S(1)} %constant_dynamic-update-slice_fusion.2.refs_0_, bf16[288,896]{1,0:T(8,128)(2,1)S(1)} %constant_dynamic-update-slice_fusion.6.refs_1_, bf16[288,896]{1,0:T(8,128)(2,1)S(1)} %collective-permute-done.18.refs_2_, ...), custom_call_target="tpu_custom_call" | custom-call | flops 1585446912 | bytes 5505024 | tf_op jit(solution)/shard_map/mlp/pallas_call | solution.py:291
  67.2 5.1 %collective-permute-done.15.refs_0_ = bf16[288,896]{1,0:T(8,128)(2,1)S(1)} collective-permute-done((bf16[288,896]{1,0:T(8,128)(2,1)S(1)}, bf16[288,896]{1,0:T(8,128)(2,1)S(1)}, u32[]{:S(2)}, u32[]{:S(2)}) %collective-permute-start.15) | collective-permute-done | bytes 516128 | tf_op jit(solution)/shard_map/ppermute | solution.py:377
  72.3 2.2 %mlp.5 = (bf16[288,1152]{1,0:T(8,128)(2,1)S(1)}, bf16[288,512]{1,0:T(8,128)(2,1)S(1)}) custom-call(s32[1]{0:T(128)} %bitcast.place, bf16[288,896]{1,0:T(8,128)(2,1)S(1)} %collective-permute-done.15.refs_0_, bf16[1,3584,512]{2,1,0:T(8,128)(2,1)S(1)} %copy-done.1, bf16[1,3584,512]{2,1,0:T(8,128)(2,1)S(1)} %copy-done.2, bf16[1,512,3584]{2,1,0:T(8,128)(2,1)S(1)} %copy-done, ...), custom_call_target="tpu_custom_call" | custom-call | flops 1585446912 | bytes 5505024 | tf_op jit(solution)/shard_map/mlp/pallas_call | solution.py:291
  74.5 1.8 %collective-permute-start.19 = (bf16[288,1152]{1,0:T(8,128)(2,1)S(1)}, bf16[288,1152]{1,0:T(8,128)(2,1)S(1)}, u32[]{:S(2)}, u32[]{:S(2)}) collective-permute-start(bf16[288,1152]{1,0:T(8,128)(2,1)S(1)} %get-tuple-element.92), channel_id=1, source_target_pairs={{0,16},{16,0},{1,17},{17,1},{2,18},{18,2},{3,19},{19,3},{4,20},{20... | collective-permute-start | bytes 1990664 | tf_op jit(solution)/shard_map/ppermute | solution.py:377
  77.3 2.0 %down.1 = (bf16[288,640]{1,0:T(8,128)(2,1)S(1)}, bf16[288,1152]{1,0:T(8,128)(2,1)S(1)}, bf16[288,640]{1,0:T(8,128)(2,1)S(1)}) custom-call(s32[1]{0:T(128)} %bitcast.place, bf16[288,512]{1,0:T(8,128)(2,1)S(1)} %get-tuple-element.96.hidden, bf16[1,512,3584]{2,1,0:T(8,128)(2,1)S(1)} %copy-done), custom_call_target="tpu_custom_call" | custom-call | flops 717225984 | bytes 2490368 | tf_op jit(solution)/shard_map/down/pallas_call | solution.py:342
  79.3 9.3 %collective-permute-done.20 = bf16[72,3584]{1,0:T(8,128)(2,1)S(1)} collective-permute-done((bf16[72,3584]{1,0:T(8,128)(2,1)S(1)}, bf16[72,3584]{1,0:T(8,128)(2,1)S(1)}, u32[]{:S(2)}, u32[]{:S(2)}) %collective-permute-start.20) | collective-permute-done | bytes 516128 | tf_op jit(solution)/shard_map/ppermute | solution.py:374
  90.7 2.8 %collective-permute-start.23 = (bf16[72,1152]{1,0:T(8,128)(2,1)S(1)}, bf16[72,1152]{1,0:T(8,128)(2,1)S(1)}, u32[]{:S(2)}, u32[]{:S(2)}) collective-permute-start(bf16[72,1152]{1,0:T(8,128)(2,1)S(1)} %get-tuple-element.129), channel_id=1, source_target_pairs={{0,4},{1,5},{2,6},{3,7},{4,0},{5,1},{6,2},{7,3},{8,12},{9,13},{10,... | collective-permute-start | bytes 497672 | tf_op jit(solution)/shard_map/ppermute | solution.py:374
  93.6 1.8 %collective-permute-start.21 = (bf16[288,640]{1,0:T(8,128)(2,1)S(1)}, bf16[288,640]{1,0:T(8,128)(2,1)S(1)}, u32[]{:S(2)}, u32[]{:S(2)}) collective-permute-start(bf16[288,640]{1,0:T(8,128)(2,1)S(1)} %get-tuple-element.98), channel_id=1, source_target_pairs={{0,16},{16,0},{1,17},{17,1},{2,18},{18,2},{3,19},{19,3},{4,20},{20... | collective-permute-start | bytes 1105928 | tf_op jit(solution)/shard_map/ppermute | solution.py:377
  96.0 2.6 %collective-permute-done.23 = bf16[72,1152]{1,0:T(8,128)(2,1)S(1)} collective-permute-done((bf16[72,1152]{1,0:T(8,128)(2,1)S(1)}, bf16[72,1152]{1,0:T(8,128)(2,1)S(1)}, u32[]{:S(2)}, u32[]{:S(2)}) %collective-permute-start.23) | collective-permute-done | bytes 165920 | tf_op jit(solution)/shard_map/ppermute | solution.py:374
  103.0 2.0 %collective-permute-start.29 = (bf16[72,640]{1,0:T(8,128)(2,1)S(1)}, bf16[72,640]{1,0:T(8,128)(2,1)S(1)}, u32[]{:S(2)}, u32[]{:S(2)}) collective-permute-start(bf16[72,640]{1,0:T(8,128)(2,1)S(1)} %get-tuple-element.143), channel_id=1, source_target_pairs={{0,4},{1,5},{2,6},{3,7},{4,0},{5,1},{6,2},{7,3},{8,12},{9,13},{10,... | collective-permute-start | bytes 276488 | tf_op jit(solution)/shard_map/ppermute | solution.py:374
  105.1 2.7 %collective-permute-start.27 = (bf16[128,1152]{1,0:T(8,128)(2,1)S(1)}, bf16[128,1152]{1,0:T(8,128)(2,1)S(1)}, u32[]{:S(2)}, u32[]{:S(2)}) collective-permute-start(bf16[128,1152]{1,0:T(8,128)(2,1)S(1)} %add_convert_fusion.2), channel_id=1, source_target_pairs={{0,8},{1,9},{2,10},{3,11},{4,12},{5,13},{6,14},{7,15},{8,0},{9,1},... | collective-permute-start | bytes 884744 | tf_op jit(solution)/shard_map/ppermute | solution.py:374
  107.9 5.0 %collective-permute-done.29 = bf16[72,640]{1,0:T(8,128)(2,1)S(1)} collective-permute-done((bf16[72,640]{1,0:T(8,128)(2,1)S(1)}, bf16[72,640]{1,0:T(8,128)(2,1)S(1)}, u32[]{:S(2)}, u32[]{:S(2)}) %collective-permute-start.29) | collective-permute-done | bytes 92192 | tf_op jit(solution)/shard_map/ppermute | solution.py:374
  114.8 6.4 %collective-permute-done.27 = bf16[128,1152]{1,0:T(8,128)(2,1)S(1)} collective-permute-done((bf16[128,1152]{1,0:T(8,128)(2,1)S(1)}, bf16[128,1152]{1,0:T(8,128)(2,1)S(1)}, u32[]{:S(2)}, u32[]{:S(2)}) %collective-permute-start.27) | collective-permute-done | bytes 294944 | tf_op jit(solution)/shard_map/ppermute | solution.py:374
  125.1 8.8 %collective-permute-done.32 = bf16[128,1792]{1,0:T(8,128)(2,1)} collective-permute-done((bf16[128,1792]{1,0:T(8,128)(2,1)S(1)}, bf16[128,1792]{1,0:T(8,128)(2,1)}, u32[]{:S(2)}, u32[]{:S(2)}) %collective-permute-start.32) | collective-permute-done | bytes 458784 | tf_op jit(solution)/shard_map/ppermute | solution.py:377
  (139 shorter events, 36.2 us)
Async XLA Ops:
  3.2 16.5 %collective-permute-start.4 = (bf16[128,1024]{1,0:T(8,128)(2,1)}, bf16[128,1024]{1,0:T(8,128)(2,1)S(1)}, u32[]{:S(2)}, u32[]{:S(2)}) collective-permute-start(bf16[128,1024]{1,0:T(8,128)(2,1)} %get-tuple-element.62), channel_id=1, source_target_pairs={{0,8},{1,9},{2,10},{3,11},{4,12},{5,13},{6,14},{7,15},{8,0},{9,1},... | collective-permute-start | bytes 786440 | tf_op jit(solution)/shard_map/ppermute | solution.py:374
  12.5 22.9 %collective-permute-start.3 = (bf16[72,3584]{1,0:T(8,128)(2,1)S(1)}, bf16[72,3584]{1,0:T(8,128)(2,1)S(1)}, u32[]{:S(2)}, u32[]{:S(2)}) collective-permute-start(bf16[72,3584]{1,0:T(8,128)(2,1)S(1)} %get-tuple-element.125), channel_id=1, source_target_pairs={{0,2},{1,3},{2,0},{3,1},{4,6},{5,7},{6,4},{7,5},{8,10},{9,11},{10,... | collective-permute-start | bytes 1548296 | tf_op jit(solution)/shard_map/ppermute | solution.py:374
  14.4 17.6 %collective-permute-start.2 = (bf16[72,1792]{1,0:T(8,128)(2,1)S(1)}, bf16[72,1792]{1,0:T(8,128)(2,1)S(1)}, u32[]{:S(2)}, u32[]{:S(2)}) collective-permute-start(bf16[72,1792]{1,0:T(8,128)(2,1)S(1)} %get-tuple-element.139), channel_id=1, source_target_pairs={{0,6},{1,7},{2,4},{3,5},{4,2},{5,3},{6,0},{7,1},{8,14},{9,15},{10,... | collective-permute-start | bytes 774152 | tf_op jit(solution)/shard_map/ppermute | solution.py:374
  16.0 19.4 %collective-permute-start.1 = (bf16[72,1792]{1,0:T(8,128)(2,1)S(1)}, bf16[72,1792]{1,0:T(8,128)(2,1)S(1)}, u32[]{:S(2)}, u32[]{:S(2)}) collective-permute-start(bf16[72,1792]{1,0:T(8,128)(2,1)S(1)} %get-tuple-element.140), channel_id=1, source_target_pairs={{0,4},{1,5},{2,6},{3,7},{4,0},{5,1},{6,2},{7,3},{8,12},{9,13},{10,... | collective-permute-start | bytes 774152 | tf_op jit(solution)/shard_map/ppermute | solution.py:374
  16.5 15.5 %collective-permute-start.5 = (bf16[128,896]{1,0:T(8,128)(2,1)S(1)}, bf16[128,896]{1,0:T(8,128)(2,1)S(1)}, u32[]{:S(2)}, u32[]{:S(2)}) collective-permute-start(bf16[128,896]{1,0:T(8,128)(2,1)S(1)} %copy-done.10), channel_id=1, source_target_pairs={{0,8},{1,9},{2,10},{3,11},{4,12},{5,13},{6,14},{7,15},{8,0},{9,1},... | collective-permute-start | bytes 688136 | tf_op jit(solution)/shard_map/ppermute | solution.py:374
  36.1 14.4 %collective-permute-start.14 = (bf16[144,1792]{1,0:T(8,128)(2,1)S(1)}, bf16[144,1792]{1,0:T(8,128)(2,1)S(1)}, u32[]{:S(2)}, u32[]{:S(2)}) collective-permute-start(bf16[144,1792]{1,0:T(8,128)(2,1)S(1)} %constant_dynamic-update-slice_fusion.refs_1_), channel_id=1, source_target_pairs={{0,16},{16,0},{1,17},{17,1},{2,18},{18,2},{3,19},{19,3},{4,20},{20... | collective-permute-start | bytes 1548296 | tf_op jit(solution)/shard_map/ppermute | solution.py:377
  39.3 9.6 %collective-permute-start.8 = (bf16[72,896]{1,0:T(8,128)(2,1)S(1)}, bf16[72,896]{1,0:T(8,128)(2,1)S(1)}, u32[]{:S(2)}, u32[]{:S(2)}) collective-permute-start(bf16[72,896]{1,0:T(8,128)(2,1)S(1)} %get-tuple-element.136), channel_id=1, source_target_pairs={{0,4},{1,5},{2,6},{3,7},{4,0},{5,1},{6,2},{7,3},{8,12},{9,13},{10,... | collective-permute-start | bytes 387080 | tf_op jit(solution)/shard_map/ppermute | solution.py:374
  41.8 7.6 %collective-permute-start.7 = (bf16[72,896]{1,0:T(8,128)(2,1)S(1)}, bf16[72,896]{1,0:T(8,128)(2,1)S(1)}, u32[]{:S(2)}, u32[]{:S(2)}) collective-permute-start(bf16[72,896]{1,0:T(8,128)(2,1)S(1)} %get-tuple-element.137), channel_id=1, source_target_pairs={{0,2},{1,3},{2,0},{3,1},{4,6},{5,7},{6,4},{7,5},{8,10},{9,11},{10,... | collective-permute-start | bytes 387080 | tf_op jit(solution)/shard_map/ppermute | solution.py:374
  43.0 14.5 %collective-permute-start.13 = (bf16[72,896]{1,0:T(8,128)(2,1)S(1)}, bf16[72,896]{1,0:T(8,128)(2,1)S(1)}, u32[]{:S(2)}, u32[]{:S(2)}) collective-permute-start(bf16[72,896]{1,0:T(8,128)(2,1)S(1)} %get-tuple-element.131), channel_id=1, source_target_pairs={{0,6},{1,7},{2,4},{3,5},{4,2},{5,3},{6,0},{7,1},{8,14},{9,15},{10,... | collective-permute-start | bytes 387080 | tf_op jit(solution)/shard_map/ppermute | solution.py:374
  46.1 11.4 %collective-permute-start.12 = (bf16[72,896]{1,0:T(8,128)(2,1)S(1)}, bf16[72,896]{1,0:T(8,128)(2,1)S(1)}, u32[]{:S(2)}, u32[]{:S(2)}) collective-permute-start(bf16[72,896]{1,0:T(8,128)(2,1)S(1)} %get-tuple-element.132), channel_id=1, source_target_pairs={{0,4},{1,5},{2,6},{3,7},{4,0},{5,1},{6,2},{7,3},{8,12},{9,13},{10,... | collective-permute-start | bytes 387080 | tf_op jit(solution)/shard_map/ppermute | solution.py:374
  48.9 8.6 %collective-permute-start.11 = (bf16[72,896]{1,0:T(8,128)(2,1)S(1)}, bf16[72,896]{1,0:T(8,128)(2,1)S(1)}, u32[]{:S(2)}, u32[]{:S(2)}) collective-permute-start(bf16[72,896]{1,0:T(8,128)(2,1)S(1)} %get-tuple-element.133), channel_id=1, source_target_pairs={{0,2},{1,3},{2,0},{3,1},{4,6},{5,7},{6,4},{7,5},{8,10},{9,11},{10,... | collective-permute-start | bytes 387080 | tf_op jit(solution)/shard_map/ppermute | solution.py:374
  49.5 14.1 %collective-permute-start.18 = (bf16[288,896]{1,0:T(8,128)(2,1)S(1)}, bf16[288,896]{1,0:T(8,128)(2,1)S(1)}, u32[]{:S(2)}, u32[]{:S(2)}) collective-permute-start(bf16[288,896]{1,0:T(8,128)(2,1)S(1)} %constant_dynamic-update-slice_fusion.2.refs_0_), channel_id=1, source_target_pairs={{0,16},{16,0},{1,17},{17,1},{2,18},{18,2},{3,19},{19,3},{4,20},{20... | collective-permute-start | bytes 1548296 | tf_op jit(solution)/shard_map/ppermute | solution.py:377
  57.6 14.7 %collective-permute-start.15 = (bf16[288,896]{1,0:T(8,128)(2,1)S(1)}, bf16[288,896]{1,0:T(8,128)(2,1)S(1)}, u32[]{:S(2)}, u32[]{:S(2)}) collective-permute-start(bf16[288,896]{1,0:T(8,128)(2,1)S(1)} %constant_dynamic-update-slice_fusion.6.refs_1_), channel_id=1, source_target_pairs={{0,16},{16,0},{1,17},{17,1},{2,18},{18,2},{3,19},{19,3},{4,20},{20... | collective-permute-start | bytes 1548296 | tf_op jit(solution)/shard_map/ppermute | solution.py:377
  59.0 13.4 %collective-permute-start.17 = (bf16[72,3584]{1,0:T(8,128)(2,1)S(1)}, bf16[72,3584]{1,0:T(8,128)(2,1)S(1)}, u32[]{:S(2)}, u32[]{:S(2)}) collective-permute-start(bf16[72,3584]{1,0:T(8,128)(2,1)S(1)} %get-tuple-element.122), channel_id=1, source_target_pairs={{0,4},{1,5},{2,6},{3,7},{4,0},{5,1},{6,2},{7,3},{8,12},{9,13},{10,... | collective-permute-start | bytes 1548296 | tf_op jit(solution)/shard_map/ppermute | solution.py:374
  59.2 13.1 %collective-permute-start.16 = (bf16[72,3584]{1,0:T(8,128)(2,1)S(1)}, bf16[72,3584]{1,0:T(8,128)(2,1)S(1)}, u32[]{:S(2)}, u32[]{:S(2)}) collective-permute-start(bf16[72,3584]{1,0:T(8,128)(2,1)S(1)} %get-tuple-element.123), channel_id=1, source_target_pairs={{0,2},{1,3},{2,0},{3,1},{4,6},{5,7},{6,4},{7,5},{8,10},{9,11},{10,... | collective-permute-start | bytes 1548296 | tf_op jit(solution)/shard_map/ppermute | solution.py:374
  74.5 14.9 %collective-permute-start.19 = (bf16[288,1152]{1,0:T(8,128)(2,1)S(1)}, bf16[288,1152]{1,0:T(8,128)(2,1)S(1)}, u32[]{:S(2)}, u32[]{:S(2)}) collective-permute-start(bf16[288,1152]{1,0:T(8,128)(2,1)S(1)} %get-tuple-element.92), channel_id=1, source_target_pairs={{0,16},{16,0},{1,17},{17,1},{2,18},{18,2},{3,19},{19,3},{4,20},{20... | collective-permute-start | bytes 1990664 | tf_op jit(solution)/shard_map/ppermute | solution.py:377
  76.3 12.2 %collective-permute-start.20 = (bf16[72,3584]{1,0:T(8,128)(2,1)S(1)}, bf16[72,3584]{1,0:T(8,128)(2,1)S(1)}, u32[]{:S(2)}, u32[]{:S(2)}) collective-permute-start(bf16[72,3584]{1,0:T(8,128)(2,1)S(1)} %get-tuple-element.121), channel_id=1, source_target_pairs={{0,6},{1,7},{2,4},{3,5},{4,2},{5,3},{6,0},{7,1},{8,14},{9,15},{10,... | collective-permute-start | bytes 1548296 | tf_op jit(solution)/shard_map/ppermute | solution.py:374
  90.7 7.8 %collective-permute-start.23 = (bf16[72,1152]{1,0:T(8,128)(2,1)S(1)}, bf16[72,1152]{1,0:T(8,128)(2,1)S(1)}, u32[]{:S(2)}, u32[]{:S(2)}) collective-permute-start(bf16[72,1152]{1,0:T(8,128)(2,1)S(1)} %get-tuple-element.129), channel_id=1, source_target_pairs={{0,4},{1,5},{2,6},{3,7},{4,0},{5,1},{6,2},{7,3},{8,12},{9,13},{10,... | collective-permute-start | bytes 497672 | tf_op jit(solution)/shard_map/ppermute | solution.py:374
  101.2 20.7 %collective-permute-start.26 = (bf16[128,3584]{1,0:T(8,128)(2,1)S(1)}, bf16[128,3584]{1,0:T(8,128)(2,1)S(1)}, u32[]{:S(2)}, u32[]{:S(2)}) collective-permute-start(bf16[128,3584]{1,0:T(8,128)(2,1)S(1)} %slice.334), channel_id=1, source_target_pairs={{0,1},{1,0},{2,3},{3,2},{4,5},{5,4},{6,7},{7,6},{8,9},{9,8},{10,11... | collective-permute-start | bytes 2752520 | tf_op jit(solution)/shard_map/ppermute | solution.py:374
  103.0 10.0 %collective-permute-start.29 = (bf16[72,640]{1,0:T(8,128)(2,1)S(1)}, bf16[72,640]{1,0:T(8,128)(2,1)S(1)}, u32[]{:S(2)}, u32[]{:S(2)}) collective-permute-start(bf16[72,640]{1,0:T(8,128)(2,1)S(1)} %get-tuple-element.143), channel_id=1, source_target_pairs={{0,4},{1,5},{2,6},{3,7},{4,0},{5,1},{6,2},{7,3},{8,12},{9,13},{10,... | collective-permute-start | bytes 276488 | tf_op jit(solution)/shard_map/ppermute | solution.py:374
  105.0 7.9 %collective-permute-start.28 = (bf16[72,640]{1,0:T(8,128)(2,1)S(1)}, bf16[72,640]{1,0:T(8,128)(2,1)S(1)}, u32[]{:S(2)}, u32[]{:S(2)}) collective-permute-start(bf16[72,640]{1,0:T(8,128)(2,1)S(1)} %get-tuple-element.144), channel_id=1, source_target_pairs={{0,2},{1,3},{2,0},{3,1},{4,6},{5,7},{6,4},{7,5},{8,10},{9,11},{10,... | collective-permute-start | bytes 276488 | tf_op jit(solution)/shard_map/ppermute | solution.py:374
  105.1 16.1 %collective-permute-start.27 = (bf16[128,1152]{1,0:T(8,128)(2,1)S(1)}, bf16[128,1152]{1,0:T(8,128)(2,1)S(1)}, u32[]{:S(2)}, u32[]{:S(2)}) collective-permute-start(bf16[128,1152]{1,0:T(8,128)(2,1)S(1)} %add_convert_fusion.2), channel_id=1, source_target_pairs={{0,8},{1,9},{2,10},{3,11},{4,12},{5,13},{6,14},{7,15},{8,0},{9,1},... | collective-permute-start | bytes 884744 | tf_op jit(solution)/shard_map/ppermute | solution.py:374
  122.2 11.7 %collective-permute-start.32 = (bf16[128,1792]{1,0:T(8,128)(2,1)S(1)}, bf16[128,1792]{1,0:T(8,128)(2,1)}, u32[]{:S(2)}, u32[]{:S(2)}) collective-permute-start(bf16[128,1792]{1,0:T(8,128)(2,1)S(1)} %slice.335), channel_id=1, source_target_pairs={{0,16},{16,0},{1,17},{17,1},{2,18},{18,2},{3,19},{19,3},{4,20},{20... | collective-permute-start | bytes 1376264 | tf_op jit(solution)/shard_map/ppermute | solution.py:377
  125.0 10.1 %collective-permute-start.33 = (bf16[128,640]{1,0:T(8,128)(2,1)S(1)}, bf16[128,640]{1,0:T(8,128)(2,1)S(1)}, u32[]{:S(2)}, u32[]{:S(2)}) collective-permute-start(bf16[128,640]{1,0:T(8,128)(2,1)S(1)} %add_convert_fusion.4), channel_id=1, source_target_pairs={{0,8},{1,9},{2,10},{3,11},{4,12},{5,13},{6,14},{7,15},{8,0},{9,1},... | collective-permute-start | bytes 491528 | tf_op jit(solution)/shard_map/ppermute | solution.py:374
  (23 other events, 141.2 us)

commit v5 on v4

--- a/solution.py
+++ b/solution.py
@@ -8,7 +8,7 @@
 from jax.sharding import PartitionSpec as P
 
 EPSILON = 1e-06
-LEAD = 9
+LEAD = 8
 F32, BF16 = jnp.float32, jnp.bfloat16
 
 
@@ -434,14 +434,15 @@
     far_1 = swap(stage(mine_1, some)[0], half)
     some = [swap(piece, 2 * q) for q, piece in enumerate(some, 2)]
     whole_near = swap(whole[group:], 2)
-    some, whole_0, whole_near, far_0, far_1 = stage(some, whole[:group], whole_near, far_0, far_1)
+    whole_0 = whole[:group]
+    some, far_0, far_1 = stage(some, far_0, far_1)
 
     some = jnp.concatenate(some, axis=0)
     some_other = cross(some)
     beside_0 = swap(far_0, 1)
     far_chosen, far_factors = tables(far_0[:, part:], beside_0[:, part:])
     rows_0 = spread(pieces_of(pick(far_chosen, far_0[:, :part], beside_0[:, :part]), chips))
-    some, rows_0 = stage(some, rows_0)
+    some, rows_0, whole_near = stage(some, rows_0, whole_near)
 
     rows_0 = jnp.concatenate(rows_0, axis=0)
     other_0 = cross(rows_0)

time: 136 us -> 136 us (level)
  starting transfers between devices: 36 us -> 33.3 us
where the time goes in v5:
time: 136 us; the launch traced here: 135 us
  waiting for transfers between devices  69.5 us (51%)
  starting transfers between devices  33.3 us (24%)
  Pallas kernels  17.3 us (13%)
  matrix products  6.94 us (5%)
  other arithmetic  4.12 us (3%)
  local copies, waits for them, and re-layouts  3.62 us (3%)
    ppermute x28, waiting for transfers between devices, swap(): lax.ppermute(value, 'expert', [(i, i ^ mask) for i in range(experts)])  50.3 us
    ppermute x28, starting transfers between devices, swap(): lax.ppermute(value, 'expert', [(i, i ^ mask) for i in range(experts)])  25.5 us
    ppermute x6, waiting for transfers between devices, cross(): return lax.ppermute(value, 'section', [(0, 1), (1, 0)])  19.2 us
    pallas_call x3, Pallas kernels, mlp(): pl.pallas_call(functools.partial(mlp_body, plan, steps, bool(before), out...  12.5 us
    ppermute x6, starting transfers between devices, cross(): return lax.ppermute(value, 'section', [(0, 1), (1, 0)])  7.86 us
    pallas_call x1, Pallas kernels, prepare(): pl.pallas_call(functools.partial(prepare_body, experts), out_shape=[jax.S...  3.17 us
  transfers between devices with their start and end apart: 34, of which 19 were waited for; matrix products, arithmetic and copies ran while one was open for 8% of the time, Pallas kernels for 9%

profile of v5, /device:TPU:0, one launch (start us, length us, event | category | flops | bytes accessed | tf_op | source)
XLA Modules:
  0.0 135.4 jit_solution(1639768475721328318)
XLA Ops:
  0.0 3.2 %prepare.1 = (bf16[128,3712]{1,0:T(8,128)(2,1)}, bf16[128,1024]{1,0:T(8,128)(2,1)}, bf16[128,896]{1,0:T(8,128)(2,1)}) custom-call(s32[1]{0:T(128)} %bitcast.place, bf16[128,3584]{1,0:T(8,128)(2,1)} %refs_0_.1, bf16[3584]{0:T(1024)(128)(2,1)} %refs_1_.2, bf16[16,3584]{1,0:T(8,128)(2,1)} %bitcast.26, s32[3,128]{1,0:T(4,128)} %bitcast.27), custom_call_target="tpu_custom_call" | custom-call | tf_op jit(solution)/shard_map/prepare/pallas_call | solution.py:184
  3.2 4.1 %collective-permute-start.3 = (bf16[128,1024]{1,0:T(8,128)(2,1)}, bf16[128,1024]{1,0:T(8,128)(2,1)S(1)}, u32[]{:S(2)}, u32[]{:S(2)}) collective-permute-start(bf16[128,1024]{1,0:T(8,128)(2,1)} %get-tuple-element.61), channel_id=1, source_target_pairs={{0,8},{1,9},{2,10},{3,11},{4,12},{5,13},{6,14},{7,15},{8,0},{9,1},... | collective-permute-start | bytes 786440 | tf_op jit(solution)/shard_map/ppermute | solution.py:374
  12.0 2.6 %collective-permute-start.2 = (bf16[72,1792]{1,0:T(8,128)(2,1)S(1)}, bf16[72,1792]{1,0:T(8,128)(2,1)S(1)}, u32[]{:S(2)}, u32[]{:S(2)}) collective-permute-start(bf16[72,1792]{1,0:T(8,128)(2,1)S(1)} %get-tuple-element.137), channel_id=1, source_target_pairs={{0,6},{1,7},{2,4},{3,5},{4,2},{5,3},{6,0},{7,1},{8,14},{9,15},{10,... | collective-permute-start | bytes 774152 | tf_op jit(solution)/shard_map/ppermute | solution.py:374
  16.6 3.7 %collective-permute-done.3 = bf16[128,1024]{1,0:T(8,128)(2,1)S(1)} collective-permute-done((bf16[128,1024]{1,0:T(8,128)(2,1)}, bf16[128,1024]{1,0:T(8,128)(2,1)S(1)}, u32[]{:S(2)}, u32[]{:S(2)}) %collective-permute-start.3) | collective-permute-done | bytes 262176 | tf_op jit(solution)/shard_map/ppermute | solution.py:374
  20.3 10.5 %collective-permute-done.4 = bf16[128,896]{1,0:T(8,128)(2,1)S(1)} collective-permute-done((bf16[128,896]{1,0:T(8,128)(2,1)S(1)}, bf16[128,896]{1,0:T(8,128)(2,1)S(1)}, u32[]{:S(2)}, u32[]{:S(2)}) %collective-permute-start.4) | collective-permute-done | bytes 229408 | tf_op jit(solution)/shard_map/ppermute | solution.py:374
  30.9 4.5 %collective-permute-done.1 = bf16[72,1792]{1,0:T(8,128)(2,1)S(1)} collective-permute-done((bf16[72,1792]{1,0:T(8,128)(2,1)S(1)}, bf16[72,1792]{1,0:T(8,128)(2,1)S(1)}, u32[]{:S(2)}, u32[]{:S(2)}) %collective-permute-start.1) | collective-permute-done | bytes 258080 | tf_op jit(solution)/shard_map/ppermute | solution.py:374
  36.1 1.6 %collective-permute-start.14 = (bf16[144,1792]{1,0:T(8,128)(2,1)S(1)}, bf16[144,1792]{1,0:T(8,128)(2,1)S(1)}, u32[]{:S(2)}, u32[]{:S(2)}) collective-permute-start(bf16[144,1792]{1,0:T(8,128)(2,1)S(1)} %constant_dynamic-update-slice_fusion.refs_1_), channel_id=1, source_target_pairs={{0,16},{16,0},{1,17},{17,1},{2,18},{18,2},{3,19},{19,3},{4,20},{20... | collective-permute-start | bytes 1548296 | tf_op jit(solution)/shard_map/ppermute | solution.py:377
  39.0 2.5 %collective-permute-start.7 = (bf16[72,896]{1,0:T(8,128)(2,1)S(1)}, bf16[72,896]{1,0:T(8,128)(2,1)S(1)}, u32[]{:S(2)}, u32[]{:S(2)}) collective-permute-start(bf16[72,896]{1,0:T(8,128)(2,1)S(1)} %get-tuple-element.134), channel_id=1, source_target_pairs={{0,4},{1,5},{2,6},{3,7},{4,0},{5,1},{6,2},{7,3},{8,12},{9,13},{10,... | collective-permute-start | bytes 387080 | tf_op jit(solution)/shard_map/ppermute | solution.py:374
  43.7 2.3 %collective-permute-done.8 = bf16[72,896]{1,0:T(8,128)(2,1)S(1)} collective-permute-done((bf16[72,896]{1,0:T(8,128)(2,1)S(1)}, bf16[72,896]{1,0:T(8,128)(2,1)S(1)}, u32[]{:S(2)}, u32[]{:S(2)}) %collective-permute-start.8) | collective-permute-done | bytes 129056 | tf_op jit(solution)/shard_map/ppermute | solution.py:374
  46.0 2.6 %collective-permute-done.7 = bf16[72,896]{1,0:T(8,128)(2,1)S(1)} collective-permute-done((bf16[72,896]{1,0:T(8,128)(2,1)S(1)}, bf16[72,896]{1,0:T(8,128)(2,1)S(1)}, u32[]{:S(2)}, u32[]{:S(2)}) %collective-permute-start.7) | collective-permute-done | bytes 129056 | tf_op jit(solution)/shard_map/ppermute | solution.py:374
  50.6 7.0 %mlp.3 = bf16[288,3584]{1,0:T(8,128)(2,1)S(1)} custom-call(s32[1]{0:T(128)} %bitcast.place, bf16[144,3584]{1,0:T(8,128)(2,1)S(1)} %pad_maximum_fusion.refs_0_, bf16[144,1792]{1,0:T(8,128)(2,1)S(1)} %constant_dynamic-update-slice_fusion.refs_1_, bf16[144,1792]{1,0:T(8,128)(2,1)S(1)} %collective-permute-done.14.refs_2_, bf16[1,3584,512]{2,1,0:T(8,128)(2,1)S(1)} %copy-done.1, ...), custom_call_target="tpu_custom_call" | custom-call | flops 3170893824 | bytes 11010048 | tf_op jit(solution)/shard_map/mlp/pallas_call | solution.py:291
  60.5 3.2 %collective-permute-done.18.refs_2_ = bf16[288,896]{1,0:T(8,128)(2,1)S(1)} collective-permute-done((bf16[288,896]{1,0:T(8,128)(2,1)S(1)}, bf16[288,896]{1,0:T(8,128)(2,1)S(1)}, u32[]{:S(2)}, u32[]{:S(2)}) %collective-permute-start.18) | collective-permute-done | bytes 516128 | tf_op jit(solution)/shard_map/ppermute | solution.py:377
  63.7 3.6 %mlp.4 = (f32[288,512]{1,0:T(8,128)S(1)}, f32[288,512]{1,0:T(8,128)S(1)}) custom-call(s32[1]{0:T(128)} %bitcast.place, bf16[288,896]{1,0:T(8,128)(2,1)S(1)} %constant_dynamic-update-slice_fusion.2.refs_0_, bf16[288,896]{1,0:T(8,128)(2,1)S(1)} %constant_dynamic-update-slice_fusion.6.refs_1_, bf16[288,896]{1,0:T(8,128)(2,1)S(1)} %collective-permute-done.18.refs_2_, ...), custom_call_target="tpu_custom_call" | custom-call | flops 1585446912 | bytes 5505024 | tf_op jit(solution)/shard_map/mlp/pallas_call | solution.py:291
  67.3 5.2 %collective-permute-done.15.refs_0_ = bf16[288,896]{1,0:T(8,128)(2,1)S(1)} collective-permute-done((bf16[288,896]{1,0:T(8,128)(2,1)S(1)}, bf16[288,896]{1,0:T(8,128)(2,1)S(1)}, u32[]{:S(2)}, u32[]{:S(2)}) %collective-permute-start.15) | collective-permute-done | bytes 516128 | tf_op jit(solution)/shard_map/ppermute | solution.py:377
  72.5 1.9 %mlp.5 = (bf16[288,1024]{1,0:T(8,128)(2,1)S(1)}, bf16[288,512]{1,0:T(8,128)(2,1)S(1)}) custom-call(s32[1]{0:T(128)} %bitcast.place, bf16[288,896]{1,0:T(8,128)(2,1)S(1)} %collective-permute-done.15.refs_0_, bf16[1,3584,512]{2,1,0:T(8,128)(2,1)S(1)} %copy-done.1, bf16[1,3584,512]{2,1,0:T(8,128)(2,1)S(1)} %copy-done.2, bf16[1,512,3584]{2,1,0:T(8,128)(2,1)S(1)} %copy-done, ...), custom_call_target="tpu_custom_call" | custom-call | flops 1585446912 | bytes 5505024 | tf_op jit(solution)/shard_map/mlp/pallas_call | solution.py:291
  74.4 1.8 %collective-permute-start.19 = (bf16[288,1024]{1,0:T(8,128)(2,1)S(1)}, bf16[288,1024]{1,0:T(8,128)(2,1)S(1)}, u32[]{:S(2)}, u32[]{:S(2)}) collective-permute-start(bf16[288,1024]{1,0:T(8,128)(2,1)S(1)} %get-tuple-element.90), channel_id=1, source_target_pairs={{0,16},{16,0},{1,17},{17,1},{2,18},{18,2},{3,19},{19,3},{4,20},{20... | collective-permute-start | bytes 1769480 | tf_op jit(solution)/shard_map/ppermute | solution.py:377
  78.5 10.1 %collective-permute-done.20 = bf16[72,3584]{1,0:T(8,128)(2,1)S(1)} collective-permute-done((bf16[72,3584]{1,0:T(8,128)(2,1)S(1)}, bf16[72,3584]{1,0:T(8,128)(2,1)S(1)}, u32[]{:S(2)}, u32[]{:S(2)}) %collective-permute-start.20) | collective-permute-done | bytes 516128 | tf_op jit(solution)/shard_map/ppermute | solution.py:374
  89.5 2.8 %collective-permute-start.23 = (bf16[72,1024]{1,0:T(8,128)(2,1)S(1)}, bf16[72,1024]{1,0:T(8,128)(2,1)S(1)}, u32[]{:S(2)}, u32[]{:S(2)}) collective-permute-start(bf16[72,1024]{1,0:T(8,128)(2,1)S(1)} %get-tuple-element.127), channel_id=1, source_target_pairs={{0,4},{1,5},{2,6},{3,7},{4,0},{5,1},{6,2},{7,3},{8,12},{9,13},{10,... | collective-permute-start | bytes 442376 | tf_op jit(solution)/shard_map/ppermute | solution.py:374
  95.0 2.0 %collective-permute-done.23 = bf16[72,1024]{1,0:T(8,128)(2,1)S(1)} collective-permute-done((bf16[72,1024]{1,0:T(8,128)(2,1)S(1)}, bf16[72,1024]{1,0:T(8,128)(2,1)S(1)}, u32[]{:S(2)}, u32[]{:S(2)}) %collective-permute-start.23) | collective-permute-done | bytes 147488 | tf_op jit(solution)/shard_map/ppermute | solution.py:374
  103.0 1.7 %collective-permute-start.29 = (bf16[72,768]{1,0:T(8,128)(2,1)S(1)}, bf16[72,768]{1,0:T(8,128)(2,1)S(1)}, u32[]{:S(2)}, u32[]{:S(2)}) collective-permute-start(bf16[72,768]{1,0:T(8,128)(2,1)S(1)} %get-tuple-element.141), channel_id=1, source_target_pairs={{0,4},{1,5},{2,6},{3,7},{4,0},{5,1},{6,2},{7,3},{8,12},{9,13},{10,... | collective-permute-start | bytes 331784 | tf_op jit(solution)/shard_map/ppermute | solution.py:374
  105.1 2.5 %collective-permute-start.27 = (bf16[128,1024]{1,0:T(8,128)(2,1)S(1)}, bf16[128,1024]{1,0:T(8,128)(2,1)S(1)}, u32[]{:S(2)}, u32[]{:S(2)}) collective-permute-start(bf16[128,1024]{1,0:T(8,128)(2,1)S(1)} %add_convert_fusion.2), channel_id=1, source_target_pairs={{0,8},{1,9},{2,10},{3,11},{4,12},{5,13},{6,14},{7,15},{8,0},{9,1},... | collective-permute-start | bytes 786440 | tf_op jit(solution)/shard_map/ppermute | solution.py:374
  108.3 5.5 %collective-permute-done.29 = bf16[72,768]{1,0:T(8,128)(2,1)S(1)} collective-permute-done((bf16[72,768]{1,0:T(8,128)(2,1)S(1)}, bf16[72,768]{1,0:T(8,128)(2,1)S(1)}, u32[]{:S(2)}, u32[]{:S(2)}) %collective-permute-start.29) | collective-permute-done | bytes 110624 | tf_op jit(solution)/shard_map/ppermute | solution.py:374
  115.1 4.5 %collective-permute-done.27 = bf16[128,1024]{1,0:T(8,128)(2,1)S(1)} collective-permute-done((bf16[128,1024]{1,0:T(8,128)(2,1)S(1)}, bf16[128,1024]{1,0:T(8,128)(2,1)S(1)}, u32[]{:S(2)}, u32[]{:S(2)}) %collective-permute-start.27) | collective-permute-done | bytes 262176 | tf_op jit(solution)/shard_map/ppermute | solution.py:374
  124.1 9.2 %collective-permute-done.32 = bf16[128,1792]{1,0:T(8,128)(2,1)} collective-permute-done((bf16[128,1792]{1,0:T(8,128)(2,1)}, bf16[128,1792]{1,0:T(8,128)(2,1)}, u32[]{:S(2)}, u32[]{:S(2)}) %collective-permute-start.32) | collective-permute-done | bytes 458784 | tf_op jit(solution)/shard_map/ppermute | solution.py:377
  (139 shorter events, 36.3 us)
Async XLA Ops:
  3.2 17.2 %collective-permute-start.3 = (bf16[128,1024]{1,0:T(8,128)(2,1)}, bf16[128,1024]{1,0:T(8,128)(2,1)S(1)}, u32[]{:S(2)}, u32[]{:S(2)}) collective-permute-start(bf16[128,1024]{1,0:T(8,128)(2,1)} %get-tuple-element.61), channel_id=1, source_target_pairs={{0,8},{1,9},{2,10},{3,11},{4,12},{5,13},{6,14},{7,15},{8,0},{9,1},... | collective-permute-start | bytes 786440 | tf_op jit(solution)/shard_map/ppermute | solution.py:374
  12.0 18.9 %collective-permute-start.2 = (bf16[72,1792]{1,0:T(8,128)(2,1)S(1)}, bf16[72,1792]{1,0:T(8,128)(2,1)S(1)}, u32[]{:S(2)}, u32[]{:S(2)}) collective-permute-start(bf16[72,1792]{1,0:T(8,128)(2,1)S(1)} %get-tuple-element.137), channel_id=1, source_target_pairs={{0,6},{1,7},{2,4},{3,5},{4,2},{5,3},{6,0},{7,1},{8,14},{9,15},{10,... | collective-permute-start | bytes 774152 | tf_op jit(solution)/shard_map/ppermute | solution.py:374
  14.6 20.8 %collective-permute-start.1 = (bf16[72,1792]{1,0:T(8,128)(2,1)S(1)}, bf16[72,1792]{1,0:T(8,128)(2,1)S(1)}, u32[]{:S(2)}, u32[]{:S(2)}) collective-permute-start(bf16[72,1792]{1,0:T(8,128)(2,1)S(1)} %get-tuple-element.138), channel_id=1, source_target_pairs={{0,4},{1,5},{2,6},{3,7},{4,0},{5,1},{6,2},{7,3},{8,12},{9,13},{10,... | collective-permute-start | bytes 774152 | tf_op jit(solution)/shard_map/ppermute | solution.py:374
  15.0 15.8 %collective-permute-start.4 = (bf16[128,896]{1,0:T(8,128)(2,1)S(1)}, bf16[128,896]{1,0:T(8,128)(2,1)S(1)}, u32[]{:S(2)}, u32[]{:S(2)}) collective-permute-start(bf16[128,896]{1,0:T(8,128)(2,1)S(1)} %copy-done.10), channel_id=1, source_target_pairs={{0,8},{1,9},{2,10},{3,11},{4,12},{5,13},{6,14},{7,15},{8,0},{9,1},... | collective-permute-start | bytes 688136 | tf_op jit(solution)/shard_map/ppermute | solution.py:374
  16.3 26.6 %collective-permute-start.9 = (bf16[72,3584]{1,0:T(8,128)(2,1)S(1)}, bf16[72,3584]{1,0:T(8,128)(2,1)S(1)}, u32[]{:S(2)}, u32[]{:S(2)}) collective-permute-start(bf16[72,3584]{1,0:T(8,128)(2,1)S(1)} %get-tuple-element.124), channel_id=1, source_target_pairs={{0,2},{1,3},{2,0},{3,1},{4,6},{5,7},{6,4},{7,5},{8,10},{9,11},{10,... | collective-permute-start | bytes 1548296 | tf_op jit(solution)/shard_map/ppermute | solution.py:374
  36.1 14.5 %collective-permute-start.14 = (bf16[144,1792]{1,0:T(8,128)(2,1)S(1)}, bf16[144,1792]{1,0:T(8,128)(2,1)S(1)}, u32[]{:S(2)}, u32[]{:S(2)}) collective-permute-start(bf16[144,1792]{1,0:T(8,128)(2,1)S(1)} %constant_dynamic-update-slice_fusion.refs_1_), channel_id=1, source_target_pairs={{0,16},{16,0},{1,17},{17,1},{2,18},{18,2},{3,19},{19,3},{4,20},{20... | collective-permute-start | bytes 1548296 | tf_op jit(solution)/shard_map/ppermute | solution.py:377
  39.0 9.6 %collective-permute-start.7 = (bf16[72,896]{1,0:T(8,128)(2,1)S(1)}, bf16[72,896]{1,0:T(8,128)(2,1)S(1)}, u32[]{:S(2)}, u32[]{:S(2)}) collective-permute-start(bf16[72,896]{1,0:T(8,128)(2,1)S(1)} %get-tuple-element.134), channel_id=1, source_target_pairs={{0,4},{1,5},{2,6},{3,7},{4,0},{5,1},{6,2},{7,3},{8,12},{9,13},{10,... | collective-permute-start | bytes 387080 | tf_op jit(solution)/shard_map/ppermute | solution.py:374
  41.5 7.8 %collective-permute-start.6 = (bf16[72,896]{1,0:T(8,128)(2,1)S(1)}, bf16[72,896]{1,0:T(8,128)(2,1)S(1)}, u32[]{:S(2)}, u32[]{:S(2)}) collective-permute-start(bf16[72,896]{1,0:T(8,128)(2,1)S(1)} %get-tuple-element.135), channel_id=1, source_target_pairs={{0,2},{1,3},{2,0},{3,1},{4,6},{5,7},{6,4},{7,5},{8,10},{9,11},{10,... | collective-permute-start | bytes 387080 | tf_op jit(solution)/shard_map/ppermute | solution.py:374
  42.9 14.6 %collective-permute-start.13 = (bf16[72,896]{1,0:T(8,128)(2,1)S(1)}, bf16[72,896]{1,0:T(8,128)(2,1)S(1)}, u32[]{:S(2)}, u32[]{:S(2)}) collective-permute-start(bf16[72,896]{1,0:T(8,128)(2,1)S(1)} %get-tuple-element.129), channel_id=1, source_target_pairs={{0,6},{1,7},{2,4},{3,5},{4,2},{5,3},{6,0},{7,1},{8,14},{9,15},{10,... | collective-permute-start | bytes 387080 | tf_op jit(solution)/shard_map/ppermute | solution.py:374
  46.0 11.6 %collective-permute-start.12 = (bf16[72,896]{1,0:T(8,128)(2,1)S(1)}, bf16[72,896]{1,0:T(8,128)(2,1)S(1)}, u32[]{:S(2)}, u32[]{:S(2)}) collective-permute-start(bf16[72,896]{1,0:T(8,128)(2,1)S(1)} %get-tuple-element.130), channel_id=1, source_target_pairs={{0,4},{1,5},{2,6},{3,7},{4,0},{5,1},{6,2},{7,3},{8,12},{9,13},{10,... | collective-permute-start | bytes 387080 | tf_op jit(solution)/shard_map/ppermute | solution.py:374
  48.6 8.9 %collective-permute-start.11 = (bf16[72,896]{1,0:T(8,128)(2,1)S(1)}, bf16[72,896]{1,0:T(8,128)(2,1)S(1)}, u32[]{:S(2)}, u32[]{:S(2)}) collective-permute-start(bf16[72,896]{1,0:T(8,128)(2,1)S(1)} %get-tuple-element.131), channel_id=1, source_target_pairs={{0,2},{1,3},{2,0},{3,1},{4,6},{5,7},{6,4},{7,5},{8,10},{9,11},{10,... | collective-permute-start | bytes 387080 | tf_op jit(solution)/shard_map/ppermute | solution.py:374
  49.4 14.3 %collective-permute-start.18 = (bf16[288,896]{1,0:T(8,128)(2,1)S(1)}, bf16[288,896]{1,0:T(8,128)(2,1)S(1)}, u32[]{:S(2)}, u32[]{:S(2)}) collective-permute-start(bf16[288,896]{1,0:T(8,128)(2,1)S(1)} %constant_dynamic-update-slice_fusion.2.refs_0_), channel_id=1, source_target_pairs={{0,16},{16,0},{1,17},{17,1},{2,18},{18,2},{3,19},{19,3},{4,20},{20... | collective-permute-start | bytes 1548296 | tf_op jit(solution)/shard_map/ppermute | solution.py:377
  57.7 14.8 %collective-permute-start.15 = (bf16[288,896]{1,0:T(8,128)(2,1)S(1)}, bf16[288,896]{1,0:T(8,128)(2,1)S(1)}, u32[]{:S(2)}, u32[]{:S(2)}) collective-permute-start(bf16[288,896]{1,0:T(8,128)(2,1)S(1)} %constant_dynamic-update-slice_fusion.6.refs_1_), channel_id=1, source_target_pairs={{0,16},{16,0},{1,17},{17,1},{2,18},{18,2},{3,19},{19,3},{4,20},{20... | collective-permute-start | bytes 1548296 | tf_op jit(solution)/shard_map/ppermute | solution.py:377
  59.0 13.5 %collective-permute-start.17 = (bf16[72,3584]{1,0:T(8,128)(2,1)S(1)}, bf16[72,3584]{1,0:T(8,128)(2,1)S(1)}, u32[]{:S(2)}, u32[]{:S(2)}) collective-permute-start(bf16[72,3584]{1,0:T(8,128)(2,1)S(1)} %get-tuple-element.120), channel_id=1, source_target_pairs={{0,4},{1,5},{2,6},{3,7},{4,0},{5,1},{6,2},{7,3},{8,12},{9,13},{10,... | collective-permute-start | bytes 1548296 | tf_op jit(solution)/shard_map/ppermute | solution.py:374
  59.1 13.4 %collective-permute-start.16 = (bf16[72,3584]{1,0:T(8,128)(2,1)S(1)}, bf16[72,3584]{1,0:T(8,128)(2,1)S(1)}, u32[]{:S(2)}, u32[]{:S(2)}) collective-permute-start(bf16[72,3584]{1,0:T(8,128)(2,1)S(1)} %get-tuple-element.121), channel_id=1, source_target_pairs={{0,2},{1,3},{2,0},{3,1},{4,6},{5,7},{6,4},{7,5},{8,10},{9,11},{10,... | collective-permute-start | bytes 1548296 | tf_op jit(solution)/shard_map/ppermute | solution.py:374
  74.4 14.2 %collective-permute-start.19 = (bf16[288,1024]{1,0:T(8,128)(2,1)S(1)}, bf16[288,1024]{1,0:T(8,128)(2,1)S(1)}, u32[]{:S(2)}, u32[]{:S(2)}) collective-permute-start(bf16[288,1024]{1,0:T(8,128)(2,1)S(1)} %get-tuple-element.90), channel_id=1, source_target_pairs={{0,16},{16,0},{1,17},{17,1},{2,18},{18,2},{3,19},{19,3},{4,20},{20... | collective-permute-start | bytes 1769480 | tf_op jit(solution)/shard_map/ppermute | solution.py:377
  76.2 12.4 %collective-permute-start.20 = (bf16[72,3584]{1,0:T(8,128)(2,1)S(1)}, bf16[72,3584]{1,0:T(8,128)(2,1)S(1)}, u32[]{:S(2)}, u32[]{:S(2)}) collective-permute-start(bf16[72,3584]{1,0:T(8,128)(2,1)S(1)} %get-tuple-element.119), channel_id=1, source_target_pairs={{0,6},{1,7},{2,4},{3,5},{4,2},{5,3},{6,0},{7,1},{8,14},{9,15},{10,... | collective-permute-start | bytes 1548296 | tf_op jit(solution)/shard_map/ppermute | solution.py:374
  92.5 8.6 %collective-permute-start.21 = (bf16[288,768]{1,0:T(8,128)(2,1)S(1)}, bf16[288,768]{1,0:T(8,128)(2,1)S(1)}, u32[]{:S(2)}, u32[]{:S(2)}) collective-permute-start(bf16[288,768]{1,0:T(8,128)(2,1)S(1)} %get-tuple-element.96), channel_id=1, source_target_pairs={{0,16},{16,0},{1,17},{17,1},{2,18},{18,2},{3,19},{19,3},{4,20},{20... | collective-permute-start | bytes 1327112 | tf_op jit(solution)/shard_map/ppermute | solution.py:377
  101.2 19.0 %collective-permute-start.26 = (bf16[128,3584]{1,0:T(8,128)(2,1)S(1)}, bf16[128,3584]{1,0:T(8,128)(2,1)S(1)}, u32[]{:S(2)}, u32[]{:S(2)}) collective-permute-start(bf16[128,3584]{1,0:T(8,128)(2,1)S(1)} %slice.334), channel_id=1, source_target_pairs={{0,1},{1,0},{2,3},{3,2},{4,5},{5,4},{6,7},{7,6},{8,9},{9,8},{10,11... | collective-permute-start | bytes 2752520 | tf_op jit(solution)/shard_map/ppermute | solution.py:374
  103.0 10.8 %collective-permute-start.29 = (bf16[72,768]{1,0:T(8,128)(2,1)S(1)}, bf16[72,768]{1,0:T(8,128)(2,1)S(1)}, u32[]{:S(2)}, u32[]{:S(2)}) collective-permute-start(bf16[72,768]{1,0:T(8,128)(2,1)S(1)} %get-tuple-element.141), channel_id=1, source_target_pairs={{0,4},{1,5},{2,6},{3,7},{4,0},{5,1},{6,2},{7,3},{8,12},{9,13},{10,... | collective-permute-start | bytes 331784 | tf_op jit(solution)/shard_map/ppermute | solution.py:374
  104.7 9.1 %collective-permute-start.28 = (bf16[72,768]{1,0:T(8,128)(2,1)S(1)}, bf16[72,768]{1,0:T(8,128)(2,1)S(1)}, u32[]{:S(2)}, u32[]{:S(2)}) collective-permute-start(bf16[72,768]{1,0:T(8,128)(2,1)S(1)} %get-tuple-element.142), channel_id=1, source_target_pairs={{0,2},{1,3},{2,0},{3,1},{4,6},{5,7},{6,4},{7,5},{8,10},{9,11},{10,... | collective-permute-start | bytes 331784 | tf_op jit(solution)/shard_map/ppermute | solution.py:374
  105.1 14.5 %collective-permute-start.27 = (bf16[128,1024]{1,0:T(8,128)(2,1)S(1)}, bf16[128,1024]{1,0:T(8,128)(2,1)S(1)}, u32[]{:S(2)}, u32[]{:S(2)}) collective-permute-start(bf16[128,1024]{1,0:T(8,128)(2,1)S(1)} %add_convert_fusion.2), channel_id=1, source_target_pairs={{0,8},{1,9},{2,10},{3,11},{4,12},{5,13},{6,14},{7,15},{8,0},{9,1},... | collective-permute-start | bytes 786440 | tf_op jit(solution)/shard_map/ppermute | solution.py:374
  121.8 11.5 %collective-permute-start.32 = (bf16[128,1792]{1,0:T(8,128)(2,1)}, bf16[128,1792]{1,0:T(8,128)(2,1)}, u32[]{:S(2)}, u32[]{:S(2)}) collective-permute-start(bf16[128,1792]{1,0:T(8,128)(2,1)} %slice.335), channel_id=1, source_target_pairs={{0,16},{16,0},{1,17},{17,1},{2,18},{18,2},{3,19},{19,3},{4,20},{20... | collective-permute-start | bytes 1376264 | tf_op jit(solution)/shard_map/ppermute | solution.py:377
  124.0 10.5 %collective-permute-start.33 = (bf16[128,768]{1,0:T(8,128)(2,1)S(1)}, bf16[128,768]{1,0:T(8,128)(2,1)S(1)}, u32[]{:S(2)}, u32[]{:S(2)}) collective-permute-start(bf16[128,768]{1,0:T(8,128)(2,1)S(1)} %add_convert_fusion.4), channel_id=1, source_target_pairs={{0,8},{1,9},{2,10},{3,11},{4,12},{5,13},{6,14},{7,15},{8,0},{9,1},... | collective-permute-start | bytes 589832 | tf_op jit(solution)/shard_map/ppermute | solution.py:374
  (23 other events, 129.1 us)

commit v6 on v5

--- a/solution.py
+++ b/solution.py
@@ -442,7 +442,7 @@
     beside_0 = swap(far_0, 1)
     far_chosen, far_factors = tables(far_0[:, part:], beside_0[:, part:])
     rows_0 = spread(pieces_of(pick(far_chosen, far_0[:, :part], beside_0[:, :part]), chips))
-    some, rows_0, whole_near = stage(some, rows_0, whole_near)
+    some, rows_0 = stage(some, rows_0)
 
     rows_0 = jnp.concatenate(rows_0, axis=0)
     other_0 = cross(rows_0)

time: 136 us -> 136 us (level)
  no operation moved by 1% of the time
where the time goes in v6:
time: 136 us; the launch traced here: 135 us
  waiting for transfers between devices  69.7 us (51%)
  starting transfers between devices  33.2 us (24%)
  Pallas kernels  17.3 us (13%)
  matrix products  6.92 us (5%)
  other arithmetic  4.13 us (3%)
  local copies, waits for them, and re-layouts  3.62 us (3%)
    ppermute x28, waiting for transfers between devices, swap(): lax.ppermute(value, 'expert', [(i, i ^ mask) for i in range(experts)])  50.5 us
    ppermute x28, starting transfers between devices, swap(): lax.ppermute(value, 'expert', [(i, i ^ mask) for i in range(experts)])  25.4 us
    ppermute x6, waiting for transfers between devices, cross(): return lax.ppermute(value, 'section', [(0, 1), (1, 0)])  19.2 us
    pallas_call x3, Pallas kernels, mlp(): pl.pallas_call(functools.partial(mlp_body, plan, steps, bool(before), out...  12.5 us
    ppermute x6, starting transfers between devices, cross(): return lax.ppermute(value, 'section', [(0, 1), (1, 0)])  7.85 us
    pallas_call x1, Pallas kernels, prepare(): pl.pallas_call(functools.partial(prepare_body, experts), out_shape=[jax.S...  3.17 us
  transfers between devices with their start and end apart: 34, of which 19 were waited for; matrix products, arithmetic and copies ran while one was open for 8% of the time, Pallas kernels for 9%

profile of v6, /device:TPU:0, one launch (start us, length us, event | category | flops | bytes accessed | tf_op | source)
XLA Modules:
  0.0 135.4 jit_solution(14894847969123975364)
XLA Ops:
  0.0 3.2 %prepare.1 = (bf16[128,3712]{1,0:T(8,128)(2,1)}, bf16[128,1024]{1,0:T(8,128)(2,1)}, bf16[128,896]{1,0:T(8,128)(2,1)}) custom-call(s32[1]{0:T(128)} %bitcast.place, bf16[128,3584]{1,0:T(8,128)(2,1)} %refs_0_.1, bf16[3584]{0:T(1024)(128)(2,1)} %refs_1_.2, bf16[16,3584]{1,0:T(8,128)(2,1)} %bitcast.26, s32[3,128]{1,0:T(4,128)} %bitcast.27), custom_call_target="tpu_custom_call" | custom-call | tf_op jit(solution)/shard_map/prepare/pallas_call | solution.py:184
  3.2 4.1 %collective-permute-start.3 = (bf16[128,1024]{1,0:T(8,128)(2,1)}, bf16[128,1024]{1,0:T(8,128)(2,1)S(1)}, u32[]{:S(2)}, u32[]{:S(2)}) collective-permute-start(bf16[128,1024]{1,0:T(8,128)(2,1)} %get-tuple-element.60), channel_id=1, source_target_pairs={{0,8},{1,9},{2,10},{3,11},{4,12},{5,13},{6,14},{7,15},{8,0},{9,1},... | collective-permute-start | bytes 786440 | tf_op jit(solution)/shard_map/ppermute | solution.py:374
  12.0 2.6 %collective-permute-start.2 = (bf16[72,1792]{1,0:T(8,128)(2,1)S(1)}, bf16[72,1792]{1,0:T(8,128)(2,1)S(1)}, u32[]{:S(2)}, u32[]{:S(2)}) collective-permute-start(bf16[72,1792]{1,0:T(8,128)(2,1)S(1)} %get-tuple-element.135), channel_id=1, source_target_pairs={{0,6},{1,7},{2,4},{3,5},{4,2},{5,3},{6,0},{7,1},{8,14},{9,15},{10,... | collective-permute-start | bytes 774152 | tf_op jit(solution)/shard_map/ppermute | solution.py:374
  16.6 3.7 %collective-permute-done.3 = bf16[128,1024]{1,0:T(8,128)(2,1)S(1)} collective-permute-done((bf16[128,1024]{1,0:T(8,128)(2,1)}, bf16[128,1024]{1,0:T(8,128)(2,1)S(1)}, u32[]{:S(2)}, u32[]{:S(2)}) %collective-permute-start.3) | collective-permute-done | bytes 262176 | tf_op jit(solution)/shard_map/ppermute | solution.py:374
  20.3 10.5 %collective-permute-done.4 = bf16[128,896]{1,0:T(8,128)(2,1)S(1)} collective-permute-done((bf16[128,896]{1,0:T(8,128)(2,1)S(1)}, bf16[128,896]{1,0:T(8,128)(2,1)S(1)}, u32[]{:S(2)}, u32[]{:S(2)}) %collective-permute-start.4) | collective-permute-done | bytes 229408 | tf_op jit(solution)/shard_map/ppermute | solution.py:374
  30.9 4.5 %collective-permute-done.1 = bf16[72,1792]{1,0:T(8,128)(2,1)S(1)} collective-permute-done((bf16[72,1792]{1,0:T(8,128)(2,1)S(1)}, bf16[72,1792]{1,0:T(8,128)(2,1)S(1)}, u32[]{:S(2)}, u32[]{:S(2)}) %collective-permute-start.1) | collective-permute-done | bytes 258080 | tf_op jit(solution)/shard_map/ppermute | solution.py:374
  36.0 1.6 %collective-permute-start.14 = (bf16[144,1792]{1,0:T(8,128)(2,1)S(1)}, bf16[144,1792]{1,0:T(8,128)(2,1)S(1)}, u32[]{:S(2)}, u32[]{:S(2)}) collective-permute-start(bf16[144,1792]{1,0:T(8,128)(2,1)S(1)} %constant_dynamic-update-slice_fusion.refs_1_), channel_id=1, source_target_pairs={{0,16},{16,0},{1,17},{17,1},{2,18},{18,2},{3,19},{19,3},{4,20},{20... | collective-permute-start | bytes 1548296 | tf_op jit(solution)/shard_map/ppermute | solution.py:377
  39.1 2.5 %collective-permute-start.7 = (bf16[72,896]{1,0:T(8,128)(2,1)S(1)}, bf16[72,896]{1,0:T(8,128)(2,1)S(1)}, u32[]{:S(2)}, u32[]{:S(2)}) collective-permute-start(bf16[72,896]{1,0:T(8,128)(2,1)S(1)} %get-tuple-element.132), channel_id=1, source_target_pairs={{0,4},{1,5},{2,6},{3,7},{4,0},{5,1},{6,2},{7,3},{8,12},{9,13},{10,... | collective-permute-start | bytes 387080 | tf_op jit(solution)/shard_map/ppermute | solution.py:374
  43.8 2.3 %collective-permute-done.8 = bf16[72,896]{1,0:T(8,128)(2,1)S(1)} collective-permute-done((bf16[72,896]{1,0:T(8,128)(2,1)S(1)}, bf16[72,896]{1,0:T(8,128)(2,1)S(1)}, u32[]{:S(2)}, u32[]{:S(2)}) %collective-permute-start.8) | collective-permute-done | bytes 129056 | tf_op jit(solution)/shard_map/ppermute | solution.py:374
  46.1 2.6 %collective-permute-done.7 = bf16[72,896]{1,0:T(8,128)(2,1)S(1)} collective-permute-done((bf16[72,896]{1,0:T(8,128)(2,1)S(1)}, bf16[72,896]{1,0:T(8,128)(2,1)S(1)}, u32[]{:S(2)}, u32[]{:S(2)}) %collective-permute-start.7) | collective-permute-done | bytes 129056 | tf_op jit(solution)/shard_map/ppermute | solution.py:374
  50.5 7.0 %mlp.3 = bf16[288,3584]{1,0:T(8,128)(2,1)S(1)} custom-call(s32[1]{0:T(128)} %bitcast.place, bf16[144,3584]{1,0:T(8,128)(2,1)S(1)} %pad_maximum_fusion.refs_0_, bf16[144,1792]{1,0:T(8,128)(2,1)S(1)} %constant_dynamic-update-slice_fusion.refs_1_, bf16[144,1792]{1,0:T(8,128)(2,1)S(1)} %collective-permute-done.14.refs_2_, bf16[1,3584,512]{2,1,0:T(8,128)(2,1)S(1)} %copy-done.1, ...), custom_call_target="tpu_custom_call" | custom-call | flops 3170893824 | bytes 11010048 | tf_op jit(solution)/shard_map/mlp/pallas_call | solution.py:291
  60.5 3.3 %collective-permute-done.18.refs_2_ = bf16[288,896]{1,0:T(8,128)(2,1)S(1)} collective-permute-done((bf16[288,896]{1,0:T(8,128)(2,1)S(1)}, bf16[288,896]{1,0:T(8,128)(2,1)S(1)}, u32[]{:S(2)}, u32[]{:S(2)}) %collective-permute-start.18) | collective-permute-done | bytes 516128 | tf_op jit(solution)/shard_map/ppermute | solution.py:377
  63.8 3.6 %mlp.4 = (f32[288,512]{1,0:T(8,128)S(1)}, f32[288,512]{1,0:T(8,128)S(1)}) custom-call(s32[1]{0:T(128)} %bitcast.place, bf16[288,896]{1,0:T(8,128)(2,1)S(1)} %constant_dynamic-update-slice_fusion.2.refs_0_, bf16[288,896]{1,0:T(8,128)(2,1)S(1)} %constant_dynamic-update-slice_fusion.6.refs_1_, bf16[288,896]{1,0:T(8,128)(2,1)S(1)} %collective-permute-done.18.refs_2_, ...), custom_call_target="tpu_custom_call" | custom-call | flops 1585446912 | bytes 5505024 | tf_op jit(solution)/shard_map/mlp/pallas_call | solution.py:291
  67.4 5.1 %collective-permute-done.15.refs_0_ = bf16[288,896]{1,0:T(8,128)(2,1)S(1)} collective-permute-done((bf16[288,896]{1,0:T(8,128)(2,1)S(1)}, bf16[288,896]{1,0:T(8,128)(2,1)S(1)}, u32[]{:S(2)}, u32[]{:S(2)}) %collective-permute-start.15) | collective-permute-done | bytes 516128 | tf_op jit(solution)/shard_map/ppermute | solution.py:377
  72.5 1.9 %mlp.5 = (bf16[288,1024]{1,0:T(8,128)(2,1)S(1)}, bf16[288,512]{1,0:T(8,128)(2,1)S(1)}) custom-call(s32[1]{0:T(128)} %bitcast.place, bf16[288,896]{1,0:T(8,128)(2,1)S(1)} %collective-permute-done.15.refs_0_, bf16[1,3584,512]{2,1,0:T(8,128)(2,1)S(1)} %copy-done.1, bf16[1,3584,512]{2,1,0:T(8,128)(2,1)S(1)} %copy-done.2, bf16[1,512,3584]{2,1,0:T(8,128)(2,1)S(1)} %copy-done, ...), custom_call_target="tpu_custom_call" | custom-call | flops 1585446912 | bytes 5505024 | tf_op jit(solution)/shard_map/mlp/pallas_call | solution.py:291
  74.4 1.8 %collective-permute-start.19 = (bf16[288,1024]{1,0:T(8,128)(2,1)S(1)}, bf16[288,1024]{1,0:T(8,128)(2,1)S(1)}, u32[]{:S(2)}, u32[]{:S(2)}) collective-permute-start(bf16[288,1024]{1,0:T(8,128)(2,1)S(1)} %get-tuple-element.88), channel_id=1, source_target_pairs={{0,16},{16,0},{1,17},{17,1},{2,18},{18,2},{3,19},{19,3},{4,20},{20... | collective-permute-start | bytes 1769480 | tf_op jit(solution)/shard_map/ppermute | solution.py:377
  78.4 10.2 %collective-permute-done.20 = bf16[72,3584]{1,0:T(8,128)(2,1)S(1)} collective-permute-done((bf16[72,3584]{1,0:T(8,128)(2,1)S(1)}, bf16[72,3584]{1,0:T(8,128)(2,1)S(1)}, u32[]{:S(2)}, u32[]{:S(2)}) %collective-permute-start.20) | collective-permute-done | bytes 516128 | tf_op jit(solution)/shard_map/ppermute | solution.py:374
  89.5 2.8 %collective-permute-start.23 = (bf16[72,1024]{1,0:T(8,128)(2,1)S(1)}, bf16[72,1024]{1,0:T(8,128)(2,1)S(1)}, u32[]{:S(2)}, u32[]{:S(2)}) collective-permute-start(bf16[72,1024]{1,0:T(8,128)(2,1)S(1)} %get-tuple-element.125), channel_id=1, source_target_pairs={{0,4},{1,5},{2,6},{3,7},{4,0},{5,1},{6,2},{7,3},{8,12},{9,13},{10,... | collective-permute-start | bytes 442376 | tf_op jit(solution)/shard_map/ppermute | solution.py:374
  95.0 2.0 %collective-permute-done.23 = bf16[72,1024]{1,0:T(8,128)(2,1)S(1)} collective-permute-done((bf16[72,1024]{1,0:T(8,128)(2,1)S(1)}, bf16[72,1024]{1,0:T(8,128)(2,1)S(1)}, u32[]{:S(2)}, u32[]{:S(2)}) %collective-permute-start.23) | collective-permute-done | bytes 147488 | tf_op jit(solution)/shard_map/ppermute | solution.py:374
  103.0 1.7 %collective-permute-start.29 = (bf16[72,768]{1,0:T(8,128)(2,1)S(1)}, bf16[72,768]{1,0:T(8,128)(2,1)S(1)}, u32[]{:S(2)}, u32[]{:S(2)}) collective-permute-start(bf16[72,768]{1,0:T(8,128)(2,1)S(1)} %get-tuple-element.139), channel_id=1, source_target_pairs={{0,4},{1,5},{2,6},{3,7},{4,0},{5,1},{6,2},{7,3},{8,12},{9,13},{10,... | collective-permute-start | bytes 331784 | tf_op jit(solution)/shard_map/ppermute | solution.py:374
  105.1 2.4 %collective-permute-start.27 = (bf16[128,1024]{1,0:T(8,128)(2,1)S(1)}, bf16[128,1024]{1,0:T(8,128)(2,1)S(1)}, u32[]{:S(2)}, u32[]{:S(2)}) collective-permute-start(bf16[128,1024]{1,0:T(8,128)(2,1)S(1)} %add_convert_fusion.2), channel_id=1, source_target_pairs={{0,8},{1,9},{2,10},{3,11},{4,12},{5,13},{6,14},{7,15},{8,0},{9,1},... | collective-permute-start | bytes 786440 | tf_op jit(solution)/shard_map/ppermute | solution.py:374
  108.3 5.5 %collective-permute-done.29 = bf16[72,768]{1,0:T(8,128)(2,1)S(1)} collective-permute-done((bf16[72,768]{1,0:T(8,128)(2,1)S(1)}, bf16[72,768]{1,0:T(8,128)(2,1)S(1)}, u32[]{:S(2)}, u32[]{:S(2)}) %collective-permute-start.29) | collective-permute-done | bytes 110624 | tf_op jit(solution)/shard_map/ppermute | solution.py:374
  115.1 4.5 %collective-permute-done.27 = bf16[128,1024]{1,0:T(8,128)(2,1)S(1)} collective-permute-done((bf16[128,1024]{1,0:T(8,128)(2,1)S(1)}, bf16[128,1024]{1,0:T(8,128)(2,1)S(1)}, u32[]{:S(2)}, u32[]{:S(2)}) %collective-permute-start.27) | collective-permute-done | bytes 262176 | tf_op jit(solution)/shard_map/ppermute | solution.py:374
  124.1 9.2 %collective-permute-done.32 = bf16[128,1792]{1,0:T(8,128)(2,1)} collective-permute-done((bf16[128,1792]{1,0:T(8,128)(2,1)}, bf16[128,1792]{1,0:T(8,128)(2,1)}, u32[]{:S(2)}, u32[]{:S(2)}) %collective-permute-start.32) | collective-permute-done | bytes 458784 | tf_op jit(solution)/shard_map/ppermute | solution.py:377
  (139 shorter events, 36.4 us)
Async XLA Ops:
  3.2 17.2 %collective-permute-start.3 = (bf16[128,1024]{1,0:T(8,128)(2,1)}, bf16[128,1024]{1,0:T(8,128)(2,1)S(1)}, u32[]{:S(2)}, u32[]{:S(2)}) collective-permute-start(bf16[128,1024]{1,0:T(8,128)(2,1)} %get-tuple-element.60), channel_id=1, source_target_pairs={{0,8},{1,9},{2,10},{3,11},{4,12},{5,13},{6,14},{7,15},{8,0},{9,1},... | collective-permute-start | bytes 786440 | tf_op jit(solution)/shard_map/ppermute | solution.py:374
  12.0 18.9 %collective-permute-start.2 = (bf16[72,1792]{1,0:T(8,128)(2,1)S(1)}, bf16[72,1792]{1,0:T(8,128)(2,1)S(1)}, u32[]{:S(2)}, u32[]{:S(2)}) collective-permute-start(bf16[72,1792]{1,0:T(8,128)(2,1)S(1)} %get-tuple-element.135), channel_id=1, source_target_pairs={{0,6},{1,7},{2,4},{3,5},{4,2},{5,3},{6,0},{7,1},{8,14},{9,15},{10,... | collective-permute-start | bytes 774152 | tf_op jit(solution)/shard_map/ppermute | solution.py:374
  14.6 20.8 %collective-permute-start.1 = (bf16[72,1792]{1,0:T(8,128)(2,1)S(1)}, bf16[72,1792]{1,0:T(8,128)(2,1)S(1)}, u32[]{:S(2)}, u32[]{:S(2)}) collective-permute-start(bf16[72,1792]{1,0:T(8,128)(2,1)S(1)} %get-tuple-element.136), channel_id=1, source_target_pairs={{0,4},{1,5},{2,6},{3,7},{4,0},{5,1},{6,2},{7,3},{8,12},{9,13},{10,... | collective-permute-start | bytes 774152 | tf_op jit(solution)/shard_map/ppermute | solution.py:374
  15.0 15.8 %collective-permute-start.4 = (bf16[128,896]{1,0:T(8,128)(2,1)S(1)}, bf16[128,896]{1,0:T(8,128)(2,1)S(1)}, u32[]{:S(2)}, u32[]{:S(2)}) collective-permute-start(bf16[128,896]{1,0:T(8,128)(2,1)S(1)} %copy-done.10), channel_id=1, source_target_pairs={{0,8},{1,9},{2,10},{3,11},{4,12},{5,13},{6,14},{7,15},{8,0},{9,1},... | collective-permute-start | bytes 688136 | tf_op jit(solution)/shard_map/ppermute | solution.py:374
  16.3 21.5 %collective-permute-start.13 = (bf16[72,3584]{1,0:T(8,128)(2,1)S(1)}, bf16[72,3584]{1,0:T(8,128)(2,1)S(1)}, u32[]{:S(2)}, u32[]{:S(2)}) collective-permute-start(bf16[72,3584]{1,0:T(8,128)(2,1)S(1)} %get-tuple-element.122), channel_id=1, source_target_pairs={{0,2},{1,3},{2,0},{3,1},{4,6},{5,7},{6,4},{7,5},{8,10},{9,11},{10,... | collective-permute-start | bytes 1548296 | tf_op jit(solution)/shard_map/ppermute | solution.py:374
  36.0 14.4 %collective-permute-start.14 = (bf16[144,1792]{1,0:T(8,128)(2,1)S(1)}, bf16[144,1792]{1,0:T(8,128)(2,1)S(1)}, u32[]{:S(2)}, u32[]{:S(2)}) collective-permute-start(bf16[144,1792]{1,0:T(8,128)(2,1)S(1)} %constant_dynamic-update-slice_fusion.refs_1_), channel_id=1, source_target_pairs={{0,16},{16,0},{1,17},{17,1},{2,18},{18,2},{3,19},{19,3},{4,20},{20... | collective-permute-start | bytes 1548296 | tf_op jit(solution)/shard_map/ppermute | solution.py:377
  39.1 9.6 %collective-permute-start.7 = (bf16[72,896]{1,0:T(8,128)(2,1)S(1)}, bf16[72,896]{1,0:T(8,128)(2,1)S(1)}, u32[]{:S(2)}, u32[]{:S(2)}) collective-permute-start(bf16[72,896]{1,0:T(8,128)(2,1)S(1)} %get-tuple-element.132), channel_id=1, source_target_pairs={{0,4},{1,5},{2,6},{3,7},{4,0},{5,1},{6,2},{7,3},{8,12},{9,13},{10,... | collective-permute-start | bytes 387080 | tf_op jit(solution)/shard_map/ppermute | solution.py:374
  41.6 7.8 %collective-permute-start.6 = (bf16[72,896]{1,0:T(8,128)(2,1)S(1)}, bf16[72,896]{1,0:T(8,128)(2,1)S(1)}, u32[]{:S(2)}, u32[]{:S(2)}) collective-permute-start(bf16[72,896]{1,0:T(8,128)(2,1)S(1)} %get-tuple-element.133), channel_id=1, source_target_pairs={{0,2},{1,3},{2,0},{3,1},{4,6},{5,7},{6,4},{7,5},{8,10},{9,11},{10,... | collective-permute-start | bytes 387080 | tf_op jit(solution)/shard_map/ppermute | solution.py:374
  43.0 14.5 %collective-permute-start.12 = (bf16[72,896]{1,0:T(8,128)(2,1)S(1)}, bf16[72,896]{1,0:T(8,128)(2,1)S(1)}, u32[]{:S(2)}, u32[]{:S(2)}) collective-permute-start(bf16[72,896]{1,0:T(8,128)(2,1)S(1)} %get-tuple-element.127), channel_id=1, source_target_pairs={{0,6},{1,7},{2,4},{3,5},{4,2},{5,3},{6,0},{7,1},{8,14},{9,15},{10,... | collective-permute-start | bytes 387080 | tf_op jit(solution)/shard_map/ppermute | solution.py:374
  46.1 11.4 %collective-permute-start.11 = (bf16[72,896]{1,0:T(8,128)(2,1)S(1)}, bf16[72,896]{1,0:T(8,128)(2,1)S(1)}, u32[]{:S(2)}, u32[]{:S(2)}) collective-permute-start(bf16[72,896]{1,0:T(8,128)(2,1)S(1)} %get-tuple-element.128), channel_id=1, source_target_pairs={{0,4},{1,5},{2,6},{3,7},{4,0},{5,1},{6,2},{7,3},{8,12},{9,13},{10,... | collective-permute-start | bytes 387080 | tf_op jit(solution)/shard_map/ppermute | solution.py:374
  48.7 8.8 %collective-permute-start.10 = (bf16[72,896]{1,0:T(8,128)(2,1)S(1)}, bf16[72,896]{1,0:T(8,128)(2,1)S(1)}, u32[]{:S(2)}, u32[]{:S(2)}) collective-permute-start(bf16[72,896]{1,0:T(8,128)(2,1)S(1)} %get-tuple-element.129), channel_id=1, source_target_pairs={{0,2},{1,3},{2,0},{3,1},{4,6},{5,7},{6,4},{7,5},{8,10},{9,11},{10,... | collective-permute-start | bytes 387080 | tf_op jit(solution)/shard_map/ppermute | solution.py:374
  49.5 14.3 %collective-permute-start.18 = (bf16[288,896]{1,0:T(8,128)(2,1)S(1)}, bf16[288,896]{1,0:T(8,128)(2,1)S(1)}, u32[]{:S(2)}, u32[]{:S(2)}) collective-permute-start(bf16[288,896]{1,0:T(8,128)(2,1)S(1)} %constant_dynamic-update-slice_fusion.2.refs_0_), channel_id=1, source_target_pairs={{0,16},{16,0},{1,17},{17,1},{2,18},{18,2},{3,19},{19,3},{4,20},{20... | collective-permute-start | bytes 1548296 | tf_op jit(solution)/shard_map/ppermute | solution.py:377
  57.6 14.9 %collective-permute-start.15 = (bf16[288,896]{1,0:T(8,128)(2,1)S(1)}, bf16[288,896]{1,0:T(8,128)(2,1)S(1)}, u32[]{:S(2)}, u32[]{:S(2)}) collective-permute-start(bf16[288,896]{1,0:T(8,128)(2,1)S(1)} %constant_dynamic-update-slice_fusion.6.refs_1_), channel_id=1, source_target_pairs={{0,16},{16,0},{1,17},{17,1},{2,18},{18,2},{3,19},{19,3},{4,20},{20... | collective-permute-start | bytes 1548296 | tf_op jit(solution)/shard_map/ppermute | solution.py:377
  59.0 13.5 %collective-permute-start.17 = (bf16[72,3584]{1,0:T(8,128)(2,1)S(1)}, bf16[72,3584]{1,0:T(8,128)(2,1)S(1)}, u32[]{:S(2)}, u32[]{:S(2)}) collective-permute-start(bf16[72,3584]{1,0:T(8,128)(2,1)S(1)} %get-tuple-element.118), channel_id=1, source_target_pairs={{0,4},{1,5},{2,6},{3,7},{4,0},{5,1},{6,2},{7,3},{8,12},{9,13},{10,... | collective-permute-start | bytes 1548296 | tf_op jit(solution)/shard_map/ppermute | solution.py:374
  59.1 13.5 %collective-permute-start.16 = (bf16[72,3584]{1,0:T(8,128)(2,1)S(1)}, bf16[72,3584]{1,0:T(8,128)(2,1)S(1)}, u32[]{:S(2)}, u32[]{:S(2)}) collective-permute-start(bf16[72,3584]{1,0:T(8,128)(2,1)S(1)} %get-tuple-element.119), channel_id=1, source_target_pairs={{0,2},{1,3},{2,0},{3,1},{4,6},{5,7},{6,4},{7,5},{8,10},{9,11},{10,... | collective-permute-start | bytes 1548296 | tf_op jit(solution)/shard_map/ppermute | solution.py:374
  74.4 14.2 %collective-permute-start.19 = (bf16[288,1024]{1,0:T(8,128)(2,1)S(1)}, bf16[288,1024]{1,0:T(8,128)(2,1)S(1)}, u32[]{:S(2)}, u32[]{:S(2)}) collective-permute-start(bf16[288,1024]{1,0:T(8,128)(2,1)S(1)} %get-tuple-element.88), channel_id=1, source_target_pairs={{0,16},{16,0},{1,17},{17,1},{2,18},{18,2},{3,19},{19,3},{4,20},{20... | collective-permute-start | bytes 1769480 | tf_op jit(solution)/shard_map/ppermute | solution.py:377
  76.2 12.4 %collective-permute-start.20 = (bf16[72,3584]{1,0:T(8,128)(2,1)S(1)}, bf16[72,3584]{1,0:T(8,128)(2,1)S(1)}, u32[]{:S(2)}, u32[]{:S(2)}) collective-permute-start(bf16[72,3584]{1,0:T(8,128)(2,1)S(1)} %get-tuple-element.117), channel_id=1, source_target_pairs={{0,6},{1,7},{2,4},{3,5},{4,2},{5,3},{6,0},{7,1},{8,14},{9,15},{10,... | collective-permute-start | bytes 1548296 | tf_op jit(solution)/shard_map/ppermute | solution.py:374
  92.5 8.6 %collective-permute-start.21 = (bf16[288,768]{1,0:T(8,128)(2,1)S(1)}, bf16[288,768]{1,0:T(8,128)(2,1)S(1)}, u32[]{:S(2)}, u32[]{:S(2)}) collective-permute-start(bf16[288,768]{1,0:T(8,128)(2,1)S(1)} %get-tuple-element.94), channel_id=1, source_target_pairs={{0,16},{16,0},{1,17},{17,1},{2,18},{18,2},{3,19},{19,3},{4,20},{20... | collective-permute-start | bytes 1327112 | tf_op jit(solution)/shard_map/ppermute | solution.py:377
  101.2 19.0 %collective-permute-start.26 = (bf16[128,3584]{1,0:T(8,128)(2,1)S(1)}, bf16[128,3584]{1,0:T(8,128)(2,1)S(1)}, u32[]{:S(2)}, u32[]{:S(2)}) collective-permute-start(bf16[128,3584]{1,0:T(8,128)(2,1)S(1)} %slice.334), channel_id=1, source_target_pairs={{0,1},{1,0},{2,3},{3,2},{4,5},{5,4},{6,7},{7,6},{8,9},{9,8},{10,11... | collective-permute-start | bytes 2752520 | tf_op jit(solution)/shard_map/ppermute | solution.py:374
  103.0 10.8 %collective-permute-start.29 = (bf16[72,768]{1,0:T(8,128)(2,1)S(1)}, bf16[72,768]{1,0:T(8,128)(2,1)S(1)}, u32[]{:S(2)}, u32[]{:S(2)}) collective-permute-start(bf16[72,768]{1,0:T(8,128)(2,1)S(1)} %get-tuple-element.139), channel_id=1, source_target_pairs={{0,4},{1,5},{2,6},{3,7},{4,0},{5,1},{6,2},{7,3},{8,12},{9,13},{10,... | collective-permute-start | bytes 331784 | tf_op jit(solution)/shard_map/ppermute | solution.py:374
  104.7 9.0 %collective-permute-start.28 = (bf16[72,768]{1,0:T(8,128)(2,1)S(1)}, bf16[72,768]{1,0:T(8,128)(2,1)S(1)}, u32[]{:S(2)}, u32[]{:S(2)}) collective-permute-start(bf16[72,768]{1,0:T(8,128)(2,1)S(1)} %get-tuple-element.140), channel_id=1, source_target_pairs={{0,2},{1,3},{2,0},{3,1},{4,6},{5,7},{6,4},{7,5},{8,10},{9,11},{10,... | collective-permute-start | bytes 331784 | tf_op jit(solution)/shard_map/ppermute | solution.py:374
  105.1 14.5 %collective-permute-start.27 = (bf16[128,1024]{1,0:T(8,128)(2,1)S(1)}, bf16[128,1024]{1,0:T(8,128)(2,1)S(1)}, u32[]{:S(2)}, u32[]{:S(2)}) collective-permute-start(bf16[128,1024]{1,0:T(8,128)(2,1)S(1)} %add_convert_fusion.2), channel_id=1, source_target_pairs={{0,8},{1,9},{2,10},{3,11},{4,12},{5,13},{6,14},{7,15},{8,0},{9,1},... | collective-permute-start | bytes 786440 | tf_op jit(solution)/shard_map/ppermute | solution.py:374
  121.8 11.5 %collective-permute-start.32 = (bf16[128,1792]{1,0:T(8,128)(2,1)}, bf16[128,1792]{1,0:T(8,128)(2,1)}, u32[]{:S(2)}, u32[]{:S(2)}) collective-permute-start(bf16[128,1792]{1,0:T(8,128)(2,1)} %slice.335), channel_id=1, source_target_pairs={{0,16},{16,0},{1,17},{17,1},{2,18},{18,2},{3,19},{19,3},{4,20},{20... | collective-permute-start | bytes 1376264 | tf_op jit(solution)/shard_map/ppermute | solution.py:377
  124.0 10.5 %collective-permute-start.33 = (bf16[128,768]{1,0:T(8,128)(2,1)S(1)}, bf16[128,768]{1,0:T(8,128)(2,1)S(1)}, u32[]{:S(2)}, u32[]{:S(2)}) collective-permute-start(bf16[128,768]{1,0:T(8,128)(2,1)S(1)} %add_convert_fusion.4), channel_id=1, source_target_pairs={{0,8},{1,9},{2,10},{3,11},{4,12},{5,13},{6,14},{7,15},{8,0},{9,1},... | collective-permute-start | bytes 589832 | tf_op jit(solution)/shard_map/ppermute | solution.py:374
  (23 other events, 130.5 us)
